TPU v7x, 128 devices: a whole 4x4x4 slice. The times are simulated.
128 devices in a mesh: space: 16 (over z, y), mp: 8 (over x, core).
Axes of the slice: x: 4, y: 4, z: 4, core: 2. Of those that a mesh axis runs over, the one named last changes fastest.
Arguments:
- points: bfloat16 [32768, 512], P('space'), may hold values from -6 to 6
- cotangent: bfloat16 [32768, 512], P('space'), may hold values from -6 to 6
- cell_counts: int32 [2048], P('space'), may hold values from 8 to 16
- norm_gain: float32 [512], replicated, may hold values from 0.1 to 1.9
- w_qkv: bfloat16 [512, 1536], P(None, 'mp'), as said below
- w_proj: bfloat16 [512, 512], P('mp'), may hold values from -0.25 to 0.25
Outputs:
- grad_points: bfloat16 [32768, 512], P('space', 'mp')
- grad_qkv: float32 [512, 1536], P('space', 'mp')
- grad_proj: float32 [512, 512], P('mp', 'space')
Inputs may be any that keep to these rules, and one draw needn't show every extreme that they name: `w_qkv`: columns ordered by head, then query, key, value, then the 16 channels of a head.
All inputs are finite; a program needn't handle non-finite values.
Results may differ from a plain program's by a relative error of at most 0.025.
The roundings to bfloat16 on the way count: a program that leaves them out, or rounds other values in their place, can miss the bound.
Values may be sent and summed in bfloat16 or wider, within the bound.
No kernel may reach another device: no remote copies, remote signals or barrier semaphores. Data moves between devices by JAX's collectives and lax.ppermute only.
A program may use at most 128 MiB of HBM per device.

v0:
```python
import jax
import jax.numpy as jnp
from jax import lax
from jax.sharding import PartitionSpec as P

H = 32
PATCH = 1024


EPS = 1e-05
MASKED = -1e30


def prefix(part, axis, combine, identity):
    place = lax.axis_index(axis)
    gathered = lax.all_gather(part, axis)
    state = jnp.zeros_like(part) + jnp.asarray(identity, part.dtype)

    def one(step, state):
        return combine(state, lax.dynamic_index_in_dim(gathered, step, 0, False))

    return lax.fori_loop(0, place, one, state)


def passed_along(block, axis, distance):
    devices = range(lax.axis_size(axis))
    route = [(i - distance, i) for i in devices if i - distance in devices]
    return lax.ppermute(block, axis, route)


def norm_rows(matrix, gain_vec):
    as_f32 = matrix.astype(jnp.float32)
    center = as_f32 - jnp.mean(as_f32, axis=-1, keepdims=True)
    spread = lax.rsqrt(jnp.mean(center * center, axis=-1, keepdims=True) + EPS)
    normed = center * spread
    return (normed, spread, (normed * gain_vec).astype(jnp.bfloat16))


def add_counts(earlier, later):
    return earlier + later


def join_rows(own_rows, next_rows, live_count, row_limit):
    width = own_rows.shape[1]
    extra = next_rows.shape[0]
    longer_ids = jnp.arange(row_limit + extra, dtype=jnp.int32)
    own_long = jnp.concatenate([own_rows, jnp.zeros((extra, width), own_rows.dtype)], axis=0)
    placed = lax.dynamic_update_slice_in_dim(
        jnp.zeros((row_limit + extra, width), own_rows.dtype), next_rows, live_count, 0
    )
    return jnp.where((longer_ids < live_count)[:, None], own_long, placed)


def attend_block(query_rows, key_rows, value_rows, up_rows, key_bias, attn_scale):
    scores = (
        jnp.einsum("hqe,hke->hqk", query_rows, key_rows, preferred_element_type=jnp.float32)
        * attn_scale
    )
    scores = scores + key_bias[None, None, :]
    row_max = jnp.max(scores, axis=-1, keepdims=True)
    exp_scores = jnp.exp(scores - row_max)
    prob_wide = exp_scores / jnp.sum(exp_scores, axis=-1, keepdims=True)
    probs_low = prob_wide.astype(jnp.bfloat16)
    attended = jnp.einsum(
        "hqk,hke->hqe", probs_low, value_rows, preferred_element_type=jnp.float32
    ).astype(jnp.bfloat16)
    dprob = jnp.einsum("hqe,hke->hqk", up_rows, value_rows, preferred_element_type=jnp.float32)
    row_delta = jnp.sum(prob_wide * dprob, axis=-1, keepdims=True)
    dscore = (prob_wide * (dprob - row_delta) * attn_scale).astype(jnp.bfloat16)
    grad_q = jnp.einsum(
        "hqk,hke->hqe", dscore, key_rows, preferred_element_type=jnp.float32
    ).astype(jnp.bfloat16)
    key_term = jnp.einsum("hqk,hqe->hke", dscore, query_rows, preferred_element_type=jnp.float32)
    value_term = jnp.einsum("hqk,hqe->hke", probs_low, up_rows, preferred_element_type=jnp.float32)
    return (attended, grad_q, key_term, value_term)


def on_device(points, cotangent, cell_counts, norm_gain, w_qkv, w_proj):
    dev_rows, feat_width = points.shape
    head_size = feat_width // H
    heads_here = w_qkv.shape[1] // (3 * head_size)
    n_space = lax.axis_size("space")
    n_model = lax.axis_size("mp")
    sp_index = lax.axis_index("space")
    mp_index = lax.axis_index("mp")
    live_count = jnp.sum(cell_counts, dtype=jnp.int32)
    first_pos = prefix(live_count, "space", add_counts, jnp.int32(0))
    head_len = (PATCH - first_pos % PATCH) % PATCH
    tail_len = jnp.where(
        sp_index == n_space - 1, 0, (PATCH - (first_pos + live_count) % PATCH) % PATCH
    )
    next_x, next_dy = passed_along((points[:PATCH], cotangent[:PATCH]), "space", -1)
    joined_x = join_rows(points, next_x, live_count, dev_rows)
    joined_dy = join_rows(cotangent, next_dy, live_count, dev_rows)
    row_ids = jnp.arange(dev_rows, dtype=jnp.int32)
    filled = live_count - head_len + tail_len
    is_valid = row_ids < filled
    zero_low = jnp.zeros((), jnp.bfloat16)
    buffer_x = jnp.where(
        is_valid[:, None], lax.dynamic_slice_in_dim(joined_x, head_len, dev_rows, 0), zero_low
    )
    buffer_dy = jnp.where(
        is_valid[:, None], lax.dynamic_slice_in_dim(joined_dy, head_len, dev_rows, 0), zero_low
    )
    normed, spread, normed_low = norm_rows(buffer_x, norm_gain)
    proj_qkv = jnp.dot(normed_low, w_qkv, preferred_element_type=jnp.float32).astype(jnp.bfloat16)
    qkv_heads = proj_qkv.reshape(dev_rows, heads_here, 3, head_size)
    upstream = lax.dot_general(
        buffer_dy, w_proj, (((1,), (1,)), ((), ())), preferred_element_type=jnp.float32
    ).astype(jnp.bfloat16)
    up_heads = upstream.reshape(dev_rows, heads_here, head_size)
    key_bias = jnp.where(is_valid, 0.0, MASKED).astype(jnp.float32)
    n_patch = (filled + PATCH - 1) // PATCH
    q_block = min(512, PATCH)
    attn_scale = head_size ** (-0.5)

    def patch_step(patch_idx, state_pair):
        attended_all, grads_all = state_pair
        first_row = patch_idx * PATCH
        qkv_block = lax.dynamic_slice_in_dim(qkv_heads, first_row, PATCH, 0)
        query_rows = jnp.transpose(qkv_block[:, :, 0], (1, 0, 2))
        key_rows = jnp.transpose(qkv_block[:, :, 1], (1, 0, 2))
        value_rows = jnp.transpose(qkv_block[:, :, 2], (1, 0, 2))
        up_rows = jnp.transpose(lax.dynamic_slice_in_dim(up_heads, first_row, PATCH, 0), (1, 0, 2))
        patch_bias = lax.dynamic_slice_in_dim(key_bias, first_row, PATCH, 0)
        key_sum = jnp.zeros((heads_here, PATCH, head_size), jnp.float32)
        value_sum = jnp.zeros((heads_here, PATCH, head_size), jnp.float32)
        attended_parts = []
        query_parts = []
        for block_start in range(0, PATCH, q_block):
            block_end = block_start + q_block
            attended, grad_q, key_term, value_term = attend_block(
                query_rows[:, block_start:block_end],
                key_rows,
                value_rows,
                up_rows[:, block_start:block_end],
                patch_bias,
                attn_scale,
            )
            attended_parts.append(attended)
            query_parts.append(grad_q)
            key_sum = key_sum + key_term
            value_sum = value_sum + value_term
        attended_patch = jnp.transpose(jnp.concatenate(attended_parts, axis=1), (1, 0, 2))
        grad_patch = jnp.stack(
            [
                jnp.concatenate(query_parts, axis=1),
                key_sum.astype(jnp.bfloat16),
                value_sum.astype(jnp.bfloat16),
            ],
            axis=2,
        )
        grad_patch = jnp.transpose(grad_patch, (1, 0, 2, 3))
        attended_all = lax.dynamic_update_slice_in_dim(attended_all, attended_patch, first_row, 0)
        grads_all = lax.dynamic_update_slice_in_dim(grads_all, grad_patch, first_row, 0)
        return (attended_all, grads_all)

    start_pair = (
        jnp.zeros((dev_rows, heads_here, head_size), jnp.bfloat16),
        jnp.zeros((dev_rows, heads_here, 3, head_size), jnp.bfloat16),
    )
    attended_all, grads_all = lax.fori_loop(0, n_patch, patch_step, start_pair)
    attended_rows = attended_all.reshape(dev_rows, heads_here * head_size)
    dqkv = grads_all.reshape(dev_rows, heads_here * 3 * head_size)
    proj_local = lax.dot_general(
        attended_rows, buffer_dy, (((0,), (0,)), ((), ())), preferred_element_type=jnp.float32
    )
    du_part = lax.dot_general(
        dqkv, w_qkv, (((1,), (1,)), ((), ())), preferred_element_type=jnp.float32
    )
    own_cols = feat_width // n_model
    dunit = lax.psum(du_part.astype(jnp.bfloat16), "mp").astype(jnp.float32)
    scaled = dunit * norm_gain
    dnorm_full = spread * (
        scaled
        - jnp.mean(scaled, axis=-1, keepdims=True)
        - normed * jnp.mean(scaled * normed, axis=-1, keepdims=True)
    )
    dnorm = lax.dynamic_slice_in_dim(dnorm_full, mp_index * own_cols, own_cols, 1)
    dy_own = lax.dynamic_slice_in_dim(buffer_dy, mp_index * own_cols, own_cols, 1).astype(
        jnp.float32
    )
    dx_buffer = jnp.where(is_valid[:, None], dy_own + dnorm, 0.0).astype(jnp.bfloat16)
    lead_ids = jnp.arange(PATCH, dtype=jnp.int32)
    pad_rows = jnp.zeros((PATCH, own_cols), jnp.bfloat16)
    after_pad = jnp.concatenate([dx_buffer, pad_rows], axis=0)
    tail_block = jnp.where(
        (lead_ids < tail_len)[:, None],
        lax.dynamic_slice_in_dim(after_pad, live_count - head_len, PATCH, 0),
        zero_low,
    )
    from_left = passed_along(tail_block, "space", 1)
    left_pad = jnp.concatenate(
        [from_left, jnp.zeros((dev_rows - PATCH, own_cols), jnp.bfloat16)], axis=0
    )
    before_pad = jnp.concatenate([pad_rows, dx_buffer], axis=0)
    own_grads = lax.dynamic_slice_in_dim(before_pad, PATCH - head_len, dev_rows, 0)
    grad_points = jnp.where(
        (row_ids < head_len)[:, None],
        left_pad,
        jnp.where((row_ids < live_count)[:, None], own_grads, zero_low),
    )
    weight_rows = feat_width // n_space
    qkv_local = lax.dot_general(
        normed_low, dqkv, (((0,), (0,)), ((), ())), preferred_element_type=jnp.float32
    )
    total_qkv, total_proj = (
        lax.psum(qkv_local.astype(jnp.bfloat16), "space").astype(jnp.float32),
        lax.psum(proj_local.astype(jnp.bfloat16), "space").astype(jnp.float32),
    )
    grad_qkv = lax.dynamic_slice_in_dim(total_qkv, sp_index * weight_rows, weight_rows, 0)
    grad_proj = lax.dynamic_slice_in_dim(total_proj, sp_index * weight_rows, weight_rows, 1)
    return (grad_points, grad_qkv, grad_proj)


def solution(mesh):
    return jax.shard_map(
        on_device,
        mesh=mesh,
        in_specs=(
            P("space", None),
            P("space", None),
            P("space"),
            P(),
            P(None, "mp"),
            P("mp", None),
        ),
        out_specs=(P("space", "mp"), P("space", "mp"), P("mp", "space")),
        check_vma=False,
    )
```

profile of v0, /device:TPU:0, one launch (start us, length us, event | category | flops | bytes accessed | tf_op | source)
XLA Modules:
  0.0 533.1 jit_solution(14900290361788057873)
XLA Ops:
  7.2 1.3 slice.28
  13.7 1.3 dynamic-update-slice
  16.3 55.3 %all-reduce.5 = s32[16]{0:T(128)S(1)} all-reduce(s32[16]{0:T(128)S(1)} %dynamic-update-slice), channel_id=1, replica_groups=mesh['space'=16,'mp'=8] {'space'}, use_global_device_ids=true, to_apply=%add.5 | all-reduce | flops 16 | bytes 128
  75.1 1.9 broadcast.85.clone
  77.0 6.2 %dynamic_update_slice.13 = bf16[3072,512]{1,0:T(8,128)(2,1)} dynamic-update-slice(bf16[3072,512]{1,0:T(8,128)(2,1)} %broadcast.85.clone, bf16[1024,512]{1,0:T(8,128)(2,1)S(1)} %collective-permute-done.1, s32[]{:T(128)S(6)} %select_n.99, s32[]{:T(128)} %constant.85.clone.1) | dynamic-update-slice | bytes 2097156 | tf_op jit(solution)/shard_map/dynamic_update_slice | solution.py:48
  83.2 3.7 convert_reduce_fusion
  88.0 1.9 broadcast.85.clone.1
  89.9 6.5 %dynamic_update_slice.12 = bf16[3072,512]{1,0:T(8,128)(2,1)} dynamic-update-slice(bf16[3072,512]{1,0:T(8,128)(2,1)} %broadcast.85.clone.1, bf16[1024,512]{1,0:T(8,128)(2,1)} %collective-permute-done, s32[]{:T(128)S(6)} %select_n.99, s32[]{:T(128)} %constant.85.clone.1) | dynamic-update-slice | bytes 2097156 | tf_op jit(solution)/shard_map/dynamic_update_slice | solution.py:48
  96.4 4.2 fusion.117
  100.6 1.4 copy-done.1
  101.9 1.5 convolution_convert_fusion.2
  103.4 1.4 convolution_convert_fusion.1
  106.6 243.5 %while.23 = (s32[]{:T(128)}, bf16[2048,4,16]{0,2,1:T(8,128)(2,1)}, bf16[2048,4,3,16]{0,3,2,1:T(8,128)(2,1)}, s32[]{:T(128)}, bf16[2048,4,3,16]{0,3,2,1:T(8,128)(...) while((s32[]{:T(128)}, bf16[2048,4,16]{0,2,1:T(8,128)(2,1)}, ...), condition=%wide.region_12.13_spmd, body=%wide.region_5.12_spmd.sunk | while | flops 898906112 | bytes 216531472 | solution.py:162
  106.6 4.7 fusion.197
  111.4 4.6 fusion.198
  116.0 4.7 fusion.195
  120.7 4.7 fusion.196
  126.2 4.5 fusion.202
  130.7 21.1 %fusion.207 = bf16[4,512,16]{1,2,0:T(8,128)(2,1)S(1)} fusion(f32[4,512,1024]{2,1,0:T(8,128)} %fusion.202, bf16[2048,4,3,16]{0,3,2,1:T(8,128)(2,1)S(1)} %get-tuple-element.259, s32[]{:T(128)S(6)} %select_n.137, s32[]{:T(128)S(6)} %add.212, f32[4,512,1024]{2,1,0:T(8,128)} %get-tuple-element.204, f32[4,512]{1,0:T(4,128)} %copy-done.19), kind=kOutput, calls=%fused_computation.45.clone.1 | convolution fusion | flops 81824768 | bytes 33767432 | tf_op jit(solution)/shard_map/while/body/hqk,hke->hqe/dot_general | solution.py:70
  151.8 4.5 fusion.204
  156.3 21.7 %fusion.206 = bf16[4,512,16]{1,2,0:T(8,128)(2,1)} fusion(f32[4,512,1024]{2,1,0:T(8,128)} %fusion.204, bf16[2048,4,3,16]{0,3,2,1:T(8,128)(2,1)S(1)} %get-tuple-element.259, s32[]{:T(128)S(6)} %select_n.137, s32[]{:T(128)S(6)} %add.212, f32[4,512,1024]{2,1,0:T(8,128)} %get-tuple-element.202, f32[4,512]{1,0:T(4,128)} %copy-done.21), kind=kOutput, calls=%fused_computation.44.clone.1 | convolution fusion | flops 81824768 | bytes 33767432 | tf_op jit(solution)/shard_map/while/body/hqk,hke->hqe/dot_general | solution.py:70
  178.9 22.2 %fusion.203 = f32[4,1024,16]{1,2,0:T(8,128)} fusion(f32[4,512,1024]{2,1,0:T(8,128)} %fusion.202, bf16[4,1024,16]{1,2,0:T(8,128)(2,1)S(1)} %dynamic-slice_bitcast_fusion.47, f32[4,512,1024]{2,1,0:T(8,128)} %get-tuple-element.204, f32[4,512]{1,0:T(4,128)} %copy-done.19), kind=kOutput, calls=%fused_computation.22.clone.1 | convolution fusion | flops 81792000 | bytes 33898496 | tf_op jit(solution)/shard_map/while/body/hqk,hqe->hke/dot_general | solution.py:73
  201.1 17.9 %fusion.205 = bf16[4,1024,1,16]{1,3,0,2:T(8,128)(2,1)} fusion(f32[4,1024,16]{1,2,0:T(8,128)} %fusion.203, f32[4,512,1024]{2,1,0:T(8,128)} %fusion.204, bf16[4,1024,16]{1,2,0:T(8,128)(2,1)S(1)} %dynamic-slice_bitcast_fusion.47, f32[4,512,1024]{2,1,0:T(8,128)} %get-tuple-element.202, f32[4,512]{1,0:T(4,128)S(1)} %copy-done.22), kind=kOutput, calls=%fused_computation.41.clone.1 | convolution fusion | flops 81923072 | bytes 34029568 | tf_op jit(solution)/shard_map/while/body/hqk,hqe->hke/dot_general | solution.py:73
  219.0 4.1 fusion.200
  223.2 4.2 fusion.201
  228.4 4.7 fusion.197
  233.1 4.6 fusion.198
  237.8 4.7 fusion.195
  242.5 4.7 fusion.196
  247.9 4.5 fusion.202
  252.4 21.1 %fusion.207 = bf16[4,512,16]{1,2,0:T(8,128)(2,1)S(1)} fusion(f32[4,512,1024]{2,1,0:T(8,128)} %fusion.202, bf16[2048,4,3,16]{0,3,2,1:T(8,128)(2,1)S(1)} %get-tuple-element.259, s32[]{:T(128)S(6)} %select_n.137, s32[]{:T(128)S(6)} %add.212, f32[4,512,1024]{2,1,0:T(8,128)} %get-tuple-element.204, f32[4,512]{1,0:T(4,128)} %copy-done.19), kind=kOutput, calls=%fused_computation.45.clone.1 | convolution fusion | flops 81824768 | bytes 33767432 | tf_op jit(solution)/shard_map/while/body/hqk,hke->hqe/dot_general | solution.py:70
  273.5 4.5 fusion.204
  278.0 21.7 %fusion.206 = bf16[4,512,16]{1,2,0:T(8,128)(2,1)} fusion(f32[4,512,1024]{2,1,0:T(8,128)} %fusion.204, bf16[2048,4,3,16]{0,3,2,1:T(8,128)(2,1)S(1)} %get-tuple-element.259, s32[]{:T(128)S(6)} %select_n.137, s32[]{:T(128)S(6)} %add.212, f32[4,512,1024]{2,1,0:T(8,128)} %get-tuple-element.202, f32[4,512]{1,0:T(4,128)} %copy-done.21), kind=kOutput, calls=%fused_computation.44.clone.1 | convolution fusion | flops 81824768 | bytes 33767432 | tf_op jit(solution)/shard_map/while/body/hqk,hke->hqe/dot_general | solution.py:70
  300.6 22.2 %fusion.203 = f32[4,1024,16]{1,2,0:T(8,128)} fusion(f32[4,512,1024]{2,1,0:T(8,128)} %fusion.202, bf16[4,1024,16]{1,2,0:T(8,128)(2,1)S(1)} %dynamic-slice_bitcast_fusion.47, f32[4,512,1024]{2,1,0:T(8,128)} %get-tuple-element.204, f32[4,512]{1,0:T(4,128)} %copy-done.19), kind=kOutput, calls=%fused_computation.22.clone.1 | convolution fusion | flops 81792000 | bytes 33898496 | tf_op jit(solution)/shard_map/while/body/hqk,hqe->hke/dot_general | solution.py:73
  322.9 17.9 %fusion.205 = bf16[4,1024,1,16]{1,3,0,2:T(8,128)(2,1)} fusion(f32[4,1024,16]{1,2,0:T(8,128)} %fusion.203, f32[4,512,1024]{2,1,0:T(8,128)} %fusion.204, bf16[4,1024,16]{1,2,0:T(8,128)(2,1)S(1)} %dynamic-slice_bitcast_fusion.47, f32[4,512,1024]{2,1,0:T(8,128)} %get-tuple-element.202, f32[4,512]{1,0:T(4,128)S(1)} %copy-done.22), kind=kOutput, calls=%fused_computation.41.clone.1 | convolution fusion | flops 81923072 | bytes 34029568 | tf_op jit(solution)/shard_map/while/body/hqk,hqe->hke/dot_general | solution.py:73
  340.8 4.1 fusion.200
  344.9 4.2 fusion.201
  350.1 3.2 convolution_convert_fusion
  354.0 2.5 convolution_convert_fusion.4
  356.5 3.9 convolution_convert_fusion.3
  360.5 70.9 %all-reduce.10.cloned.1.call-done = bf16[2048,512]{1,0:T(8,128)(2,1)} async-done(((bf16[2048,512]{1,0:T(8,128)(2,1)}), bf16[2048,512]{1,0:T(8,128)(2,1)}) %all-reduce.10.cloned.1.call-update) | async-done | bytes 2097168 | tf_op jit(solution)/shard_map/psum | solution.py:172
  431.4 3.6 fusion.120
  435.0 2.1 fusion.125
  437.7 3.4 collective-permute-start.2
  441.1 78.3 %all-reduce.12.cloned.1.call-done = (bf16[512,192]{1,0:T(8,128)(2,1)}, bf16[64,512]{0,1:T(8,128)(2,1)}) async-done(((bf16[512,192]{1,0:T(8,128)(2,1)}, bf16[64,512]{0,1:T(8,128)(2,1)}), (bf16[512,192]{1,0:T(8,128)(2,1)}, bf16[64,512]{0,1:T(8,128)(2,1)})) %all-reduce.12.cloned.1.call-update) | async-done | bytes 262160 | tf_op jit(solution)/shard_map/psum | solution.py:208
  519.4 1.3 dynamic-slice_convert_fusion.1
  520.7 1.3 dynamic-slice_convert_fusion
  522.0 3.3 fusion.127
  (104 shorter events, 17.1 us)
Async XLA Ops:
  7.2 96.2 %copy-start = (bf16[512,192]{0,1:T(8,128)(2,1)S(1)}, bf16[512,192]{0,1:T(8,128)(2,1)}, u32[]{:S(2)}) copy-start(bf16[512,192]{0,1:T(8,128)(2,1)} %param.14) | copy-start | bytes 589828
  7.2 424.2 %all-reduce.10.cloned.1.call-start = ((), (), s32[]{:S(2)}) async-start(), calls=%async_computation | async-start | bytes 4194304 | tf_op jit(solution)/shard_map/psum | solution.py:172
  8.6 66.6 %collective-permute-start.1 = (bf16[1024,512]{1,0:T(8,128)(2,1)S(1)}, bf16[1024,512]{1,0:T(8,128)(2,1)S(1)}, u32[]{:S(2)}, u32[]{:S(2)}) collective-permute-start(bf16[1024,512]{1,0:T(8,128)(2,1)S(1)} %slice.28), channel_id=1, source_target_pairs={{8,0},{16,8},{24,16},{32,24},{40,32},{48,40},{56,48},{64,56},{72,6... | collective-permute-start | bytes 3145736 | tf_op jit(solution)/shard_map/ppermute | solution.py:28
  15.0 73.1 %collective-permute-start = (bf16[1024,512]{1,0:T(8,128)(2,1)S(1)}, bf16[1024,512]{1,0:T(8,128)(2,1)}, u32[]{:S(2)}, u32[]{:S(2)}) collective-permute-start(bf16[1024,512]{1,0:T(8,128)(2,1)S(1)} %slice.27), channel_id=1, source_target_pairs={{8,0},{16,8},{24,16},{32,24},{40,32},{48,40},{56,48},{64,56},{72,6... | collective-permute-start | bytes 3145736 | tf_op jit(solution)/shard_map/ppermute | solution.py:28
  73.3 23.1 %copy-start.15 = (pred[2048]{0:T(1024)(128)(4,1)}, pred[2048]{0:T(1024)(128)(4,1)S(1)}, u32[]{:S(2)}) copy-start(pred[2048]{0:T(1024)(128)(4,1)S(1)} %iota_compare_fusion.2) | copy-start | bytes 6148
  86.9 17.9 %copy-start.3 = (bf16[2048,512]{1,0:T(8,128)(2,1)}, bf16[2048,512]{1,0:T(8,128)(2,1)S(1)}, u32[]{:S(2)}) copy-start(bf16[2048,512]{1,0:T(8,128)(2,1)S(1)} %get-tuple-element.115) | copy-start | bytes 6291460
  86.9 15.0 %copy-start.14 = (bf16[64,512]{1,0:T(8,128)(2,1)S(1)}, bf16[64,512]{1,0:T(8,128)(2,1)}, u32[]{:S(2)}) copy-start(bf16[64,512]{1,0:T(8,128)(2,1)} %param.15) | copy-start | bytes 196612
  86.9 16.5 %copy-start.17 = (f32[512]{0:T(512)S(1)}, f32[512]{0:T(512)}, u32[]{:S(2)}) copy-start(f32[512]{0:T(512)} %param.13) | copy-start | bytes 6148
  87.0 17.9 %copy-start.12 = (f32[2048]{0:T(1024)}, f32[2048]{0:T(1024)S(1)}, u32[]{:S(2)}) copy-start(f32[2048]{0:T(1024)S(1)} %broadcast_multiply_fusion.2) | copy-start | bytes 24580
  88.0 16.9 %copy-start.10 = (f32[2048]{0:T(1024)}, f32[2048]{0:T(1024)S(1)}, u32[]{:S(2)}) copy-start(f32[2048]{0:T(1024)S(1)} %add_rsqrt_fusion) | copy-start | bytes 24580
  100.5 1.4 copy-start.1
  106.6 247.4 %copy-start.2 = (bf16[2048,512]{1,0:T(8,128)(2,1)S(1)}, bf16[2048,512]{1,0:T(8,128)(2,1)}, u32[]{:S(2)}) copy-start(bf16[2048,512]{1,0:T(8,128)(2,1)} %copy-done.1) | copy-start | bytes 6291460
  106.6 249.9 %copy-start.11 = (f32[2048]{0:T(1024)S(1)}, f32[2048]{0:T(1024)}, u32[]{:S(2)}) copy-start(f32[2048]{0:T(1024)} %copy-done.10) | copy-start | bytes 24580
  111.4 4.6 copy-start.19
  120.7 4.7 copy-start.21
  120.7 4.7 copy-start.5
  120.7 4.7 copy-start.8
  125.5 0.7 copy-start.9
  178.9 22.3 %copy-start.22 = (f32[4,512]{1,0:T(4,128)S(1)}, f32[4,512]{1,0:T(4,128)}, u32[]{:S(2)}) copy-start(f32[4,512]{1,0:T(4,128)} %copy-done.21) | copy-start | bytes 24580 | tf_op jit(solution)/shard_map/while
  219.0 4.1 copy-start.20
  223.2 4.2 copy-start.4
  223.2 4.2 copy-start.6
  227.4 0.9 copy-start.7
  233.1 4.7 copy-start.19
  242.5 4.7 copy-start.21
  242.5 4.7 copy-start.5
  242.5 4.7 copy-start.8
  247.2 0.7 copy-start.9
  300.6 22.3 %copy-start.22 = (f32[4,512]{1,0:T(4,128)S(1)}, f32[4,512]{1,0:T(4,128)}, u32[]{:S(2)}) copy-start(f32[4,512]{1,0:T(4,128)} %copy-done.21) | copy-start | bytes 24580 | tf_op jit(solution)/shard_map/while
  340.8 4.1 copy-start.20
  344.9 4.2 copy-start.4
  344.9 4.2 copy-start.6
  349.2 0.9 copy-start.7
  350.1 81.3 %copy-start.13 = (f32[2048]{0:T(1024)S(1)}, f32[2048]{0:T(1024)}, u32[]{:S(2)}) copy-start(f32[2048]{0:T(1024)} %copy-done.12) | copy-start | bytes 24580
  350.1 81.3 %copy-start.18 = (f32[512]{0:T(512)S(1)}, f32[512]{0:T(512)}, u32[]{:S(2)}) copy-start(f32[512]{0:T(512)} %param.13) | copy-start | bytes 6148
  353.3 166.1 %all-reduce.12.cloned.1.call-start = ((), (), s32[]{:S(2)}) async-start(), calls=%async_computation.1 | async-start | bytes 786432 | tf_op jit(solution)/shard_map/psum | solution.py:208
  360.4 74.6 %copy-start.16 = (pred[2048]{0:T(1024)(128)(4,1)S(1)}, pred[2048]{0:T(1024)(128)(4,1)}, u32[]{:S(2)}) copy-start(pred[2048]{0:T(1024)(128)(4,1)} %copy-done.15) | copy-start | bytes 6148
  437.7 84.3 %collective-permute-start.2 = (bf16[1024,64]{1,0:T(8,128)(2,1)S(1)}, bf16[1024,64]{1,0:T(8,128)(2,1)S(1)}, u32[]{:S(2)}, u32[]{:S(2)}) collective-permute-start(bf16[1024,64]{1,0:T(8,128)(2,1)S(1)} %fusion.128), channel_id=1, source_target_pairs={{0,8},{8,16},{16,24},{24,32},{32,40},{40,48},{48,56},{56,64},{64,7... | collective-permute-start | bytes 393224 | tf_op jit(solution)/shard_map/ppermute | solution.py:28
Sparse Core Ops, SparseCore 0:
  353.4 77.8 all-reduce.9
  435.3 84.0 all-reduce.11
where the time goes:
time: 534 us; the launch traced here: 533 us
  matrix products  251 us (47%)
  waiting for transfers between devices  149 us (28%)
  blocking collectives  55.3 us (10%)
  local copies, waits for them, and re-layouts  29 us (5%)
  other arithmetic  25.3 us (5%)
  between operations  17.2 us (3%)
  starting transfers between devices  6.06 us (1%)
    dot_general x4, matrix products, attend_block(): jnp.einsum('hqk,hke->hqe', dscore, key_rows, preferred_element_type=jnp.f...  85.6 us
    dot_general x4, matrix products, attend_block(): jnp.einsum('hqk,hqe->hke', dscore, query_rows, preferred_element_type=jnp...  80.3 us
    psum x1, waiting for transfers between devices, on_device(): lax.psum(qkv_local.astype(jnp.bfloat16), 'space').astype(jnp.float32)  78.3 us
    psum x1, waiting for transfers between devices, on_device(): dunit = lax.psum(du_part.astype(jnp.bfloat16), 'mp').astype(jnp.float32)  70.9 us
    unnamed x1, blocking collectives  55.3 us
    sub x4, matrix products, attend_block(): exp_scores = jnp.exp(scores - row_max)  18.9 us
    dot_general x4, matrix products, attend_block(): jnp.einsum('hqk,hke->hqe', probs_low, value_rows, preferred_element_type=...  18.7 us
    dot_general x4, matrix products, attend_block(): jnp.einsum('hqe,hke->hqk', up_rows, value_rows, preferred_element_type=jn...  18.1 us
  transfers between devices with their start and end apart: 5, of which 2 were waited for; matrix products, arithmetic and copies ran while one was open for 6% of the time, Pallas kernels for 0%

commit v1 on v0

v1 whole, which is shorter than its diff:
```python
import functools

import jax
import jax.numpy as jnp
from jax import lax
from jax.experimental import pallas as pl
from jax.experimental.pallas import tpu as pltpu
from jax.sharding import PartitionSpec as P

H = 32
PATCH = 1024
EPS = 1e-05
MASKED = -1e30
HEAD = 16
GROUP = 64
LANES = 256
BLOCK = 256
SHIFT = 128
MIB = 1024 * 1024

BF = jnp.bfloat16
F32 = jnp.float32
NT = (((1,), (1,)), ((), ()))
TN = (((0,), (0,)), ((), ()))


def dot(a, b):
    return jnp.dot(a, b, preferred_element_type=F32)


def dot_nt(a, b):
    return lax.dot_general(a, b, NT, preferred_element_type=F32)


def dot_tn(a, b):
    return lax.dot_general(a, b, TN, preferred_element_type=F32)


def iota(shape, axis):
    return lax.broadcasted_iota(jnp.int32, shape, axis)


def onehot(mask):
    return jnp.where(mask, 1.0, 0.0).astype(BF)


def split(value):
    high = value.astype(BF)
    return high, (value - high.astype(F32)).astype(BF)


def project_kernel(
    sc_ref, x_ref, dy_ref, gain_ref, wqkv_ref, wproj_ref, spread_ref,
    qkvu_ref, unit_ref, own_ref, stat_ref, wide_ref, wg_ref, wup_ref,
):
    rows = x_ref.shape[0]
    width = x_ref.shape[1]
    gain = gain_ref[...]

    @pl.when(pl.program_id(0) == 0)
    def _():
        wide = dot(wqkv_ref[...], spread_ref[...]).astype(BF)
        wide_ref[...] = wide
        lane = iota((LANES, GROUP), 0)
        part = iota((LANES, GROUP), 1)
        up = onehot(lane == (part // HEAD) * GROUP + 3 * HEAD + part % HEAD)
        wup_ref[...] = dot(up, wproj_ref[...]).astype(BF)
        gain_high, gain_low = split(jnp.broadcast_to(gain, (16, width)))
        wg = dot(gain_high, wide) + dot(gain_low, wide)
        wg_high, wg_low = split(wg)
        row = iota((16, LANES), 0)
        zero = jnp.zeros((16, LANES), F32)
        wg_ref[...] = jnp.where(
            row == 0, wg_high.astype(F32), jnp.where(row == 1, wg_low.astype(F32), zero)
        ).astype(BF)

    x_low = x_ref[...]
    x = x_low.astype(F32)
    mean = jnp.mean(x, axis=-1, keepdims=True)
    center = x - mean
    spread = lax.rsqrt(jnp.mean(center * center, axis=-1, keepdims=True) + EPS)
    unit = (center * spread * gain).astype(BF)
    unit_ref[...] = unit
    dy = dy_ref[...]
    qkvu_ref[...] = (dot(unit, wide_ref[...]) + dot_nt(dy, wup_ref[...])).astype(BF)
    own_cols = own_ref.shape[0] // 2
    pick = onehot(
        iota((own_cols, width), 1) == iota((own_cols, width), 0) + sc_ref[4] * own_cols
    )
    own_ref[:own_cols, :] = dot_nt(pick, x_low).astype(BF)
    own_ref[own_cols:, :] = dot_nt(pick, dy).astype(BF)
    both = jnp.where(iota((rows, 128), 1) < 4, mean, spread)
    stat_ref[...] = both.T[:8, :]


def shift_rows(src_ref, total, first, low, high):
    base = jnp.clip((first // SHIFT) * SHIFT, 0, total - 2 * SHIFT)
    base = pl.multiple_of(base, SHIFT)
    row = iota((SHIFT, 2 * SHIFT), 0) + first
    col = iota((SHIFT, 2 * SHIFT), 1) + base
    pick = onehot((row == col) & (row >= low) & (row < high))
    return dot(pick, src_ref[pl.ds(base, 2 * SHIFT), :])


def attend_kernel(
    spanning, sc_ref, own_ref, next_ref, *rest
):
    if spanning:
        out_ref, out_next_ref = rest[:2]
        rest = rest[2:]
    else:
        out_ref = rest[0]
        rest = rest[1:]
    x_ref, keys_ref, moved_ref, flip_ref, score_ref, pair_ref, right_ref, sum_ref, turn_ref, done_ref = rest
    slots = own_ref.shape[0]
    head_len = sc_ref[0]
    count = sc_ref[1]
    n_patch = sc_ref[2]
    tail_len = sc_ref[3]

    def work():
        first = head_len + (PATCH * (n_patch - 1) if spanning else 0)

        def gather(i, carry):
            start = pl.multiple_of(i * SHIFT, SHIFT)
            piece = shift_rows(own_ref, slots, first + start, 0, count)
            if spanning:
                piece = piece + shift_rows(next_ref, PATCH, first + start - count, 0, tail_len)
            x_ref[pl.ds(start, SHIFT), :] = piece.astype(BF)
            return carry

        lax.fori_loop(0, PATCH // SHIFT, gather, 0)
        x = x_ref[...]
        if spanning:
            valid = count - first + tail_len
            row = iota((PATCH, LANES), 0)
            lane = iota((PATCH, LANES), 1)
            bias = jnp.where(row < valid, 0.0, MASKED)
            keys_ref[...] = jnp.where(lane == 3 * HEAD, bias, x.astype(F32)).astype(BF)
        lhs_ref = keys_ref if spanning else x_ref
        src = iota((LANES, LANES), 0)
        dst = iota((LANES, LANES), 1)
        sub = dst & (GROUP - 1)
        is_k = (sub >= HEAD) & (sub < 2 * HEAD)
        is_v = (sub >= 2 * HEAD) & (sub < 3 * HEAD)
        is_q = sub < HEAD
        is_u = sub >= 3 * HEAD
        move = onehot((is_k & (src == dst - HEAD)) | (is_v & (src == dst + HEAD)))
        moved_ref[...] = dot(x, move).astype(BF)
        scale = HEAD ** (-0.5)
        flip = jnp.where(src == dst, jnp.where(is_q | is_u, scale, 1.0), 0.0).astype(BF)
        flip_ref[...] = dot_nt(flip, x).astype(BF)
        sum_ref[...] = jnp.zeros_like(sum_ref)
        turn_ref[...] = jnp.zeros_like(turn_ref)

        def placed(piece, at):
            parts = []
            if at:
                parts.append(jnp.zeros((at, BLOCK), BF))
            parts.append(piece)
            if at + HEAD < LANES:
                parts.append(jnp.zeros((LANES - at - HEAD, BLOCK), BF))
            return jnp.concatenate(parts, axis=0)

        ones_row = onehot(
            (iota((LANES, BLOCK), 0) == 3 * HEAD)
        )

        def block(step, carry):
            start = pl.multiple_of(step * BLOCK, BLOCK)
            here = pl.ds(start, BLOCK)
            tops = []
            for h in range(4):
                at = h * GROUP
                right = placed(flip_ref[at : at + HEAD, here], at + HEAD)
                if spanning:
                    right = right + ones_row
                scores = dot(lhs_ref[...], right)
                score_ref[h] = scores
                tops.append(jnp.max(scores, axis=0, keepdims=True))
            for h in range(4):
                at = h * GROUP
                exps = jnp.exp(score_ref[h] - tops[h])
                inverse = 1.0 / jnp.sum(exps, axis=0, keepdims=True)
                score_ref[h] = exps
                probs = score_ref[h] * inverse
                low = probs.astype(BF)
                pair_ref[:, 2 * h * BLOCK : (2 * h + 1) * BLOCK] = low
                attended = dot(flip_ref[at + 2 * HEAD : at + 3 * HEAD, :], low)
                turn_ref[at + 3 * HEAD : at + 4 * HEAD, here] = attended
                up = flip_ref[at + 3 * HEAD : at + 4 * HEAD, here]
                delta = jnp.sum(up.astype(F32) * attended, axis=0, keepdims=True)
                dprob = dot(lhs_ref[...], placed(up, at + 2 * HEAD))
                dscore = (score_ref[h] * inverse * (dprob - delta)).astype(BF)
                pair_ref[:, (2 * h + 1) * BLOCK : (2 * h + 2) * BLOCK] = dscore
                grad_q = dot(flip_ref[at + HEAD : at + 2 * HEAD, :], dscore)
                turn_ref[at : at + HEAD, here] = grad_q
            moved = moved_ref[here, :]
            lane = iota((BLOCK, LANES), 1)
            zero = jnp.zeros((BLOCK, LANES), BF)
            for h in range(4):
                at = h * GROUP
                in_k = (lane >= at + HEAD) & (lane < at + 2 * HEAD)
                in_v = (lane >= at + 2 * HEAD) & (lane < at + 3 * HEAD)
                right_ref[2 * h * BLOCK : (2 * h + 1) * BLOCK, :] = jnp.where(in_v, moved, zero)
                right_ref[(2 * h + 1) * BLOCK : (2 * h + 2) * BLOCK, :] = jnp.where(in_k, moved, zero)
            sum_ref[...] += dot(pair_ref[...], right_ref[...])
            return carry

        lax.fori_loop(0, PATCH // BLOCK, block, 0)
        done_ref[...] = (sum_ref[...] + turn_ref[...].T).astype(BF)

        def scatter(i, carry):
            start = pl.multiple_of(i * SHIFT, SHIFT)
            piece = shift_rows(done_ref, PATCH, start - first, 0, jnp.minimum(PATCH, count - first))
            out_ref[pl.ds(start, SHIFT), :] = piece.astype(BF)
            return carry

        lax.fori_loop(0, slots // SHIFT, scatter, 0)
        if spanning:
            def scatter_next(i, carry):
                start = pl.multiple_of(i * SHIFT, SHIFT)
                piece = shift_rows(
                    done_ref, PATCH, start + count - first, 0, count - first + tail_len
                )
                out_next_ref[pl.ds(start, SHIFT), :] = piece.astype(BF)
                return carry

            lax.fori_loop(0, PATCH // SHIFT, scatter_next, 0)

    if spanning:
        work()
    else:
        pl.when(n_patch == 2)(work)

        @pl.when(n_patch < 2)
        def _():
            out_ref[...] = jnp.zeros_like(out_ref)


def weight_kernel(
    sc_ref, one_ref, two_ref, got_ref, unit_ref, dy_ref, qkvu_ref, wide_ref, wg_ref,
    keep_ref, send_ref, grads_ref, turned_ref, gu_ref, gy_ref,
):
    step = pl.program_id(0)
    steps = pl.num_programs(0)
    rows = one_ref.shape[0]
    core = sc_ref[5]
    cols = wide_ref.shape[0] // 8

    @pl.when(step == 0)
    def _():
        gu_ref[...] = jnp.zeros_like(gu_ref)
        gy_ref[...] = jnp.zeros_like(gy_ref)
        for side in range(2):
            for x in range(4):
                from_row = pl.multiple_of((2 * x + (core ^ side)) * cols, cols)
                to_row = (side * 4 + x) * cols
                turned_ref[to_row : to_row + cols, :] = wide_ref[pl.ds(from_row, cols), :]

    got = jnp.where(step < PATCH // rows, got_ref[...].astype(F32), 0.0)
    total = (one_ref[...].astype(F32) + two_ref[...].astype(F32) + got).astype(BF)
    gu_ref[...] += dot_tn(unit_ref[...], total)
    gy_ref[...] += dot_tn(dy_ref[...], total)
    du = dot_nt(turned_ref[...], total).astype(BF)
    half = 4 * cols
    keep_ref[:half, :] = du[:half]
    send_ref[:half, :] = du[half:]
    lane = iota((rows, LANES), 1) & (GROUP - 1)
    product = jnp.where(lane < 3 * HEAD, total.astype(F32) * qkvu_ref[...].astype(F32), 0.0)
    high, low = split(product)
    ones = jnp.ones((16, LANES), BF)
    second = (dot_nt(ones, high) + dot_nt(ones, low))[:1]
    first_rows = dot_nt(wg_ref[...], total)
    first = first_rows[:1] + first_rows[1:2]
    stats = pack_stats(first, second, rows)
    keep_ref[half:, :] = stats
    send_ref[half:, :] = stats

    @pl.when(step == steps - 1)
    def _():
        lane = iota(gu_ref.shape, 1) & (GROUP - 1)
        grads_ref[...] = jnp.where(lane < 3 * HEAD, gu_ref[...], gy_ref[...]).astype(BF)


def pack_stats(first, second, rows):
    row = iota((16, rows), 0)
    first_high = first.astype(BF).astype(F32)
    second_high = second.astype(BF).astype(F32)
    return jnp.where(
        row == 0,
        first_high,
        jnp.where(
            row == 1,
            first - first_high,
            jnp.where(row == 2, second_high, jnp.where(row == 3, second - second_high, 0.0)),
        ),
    ).astype(BF)


def pair_kernel(sc_ref, keep_ref, got_ref, out0_ref, out1_ref, out2_ref, out3_ref):
    x = sc_ref[6]
    rows = keep_ref.shape[1]
    half = keep_ref.shape[0] - 16
    cols = half // 4
    stats = keep_ref[half:, :].astype(F32) + got_ref[half:, :].astype(F32)
    packed = pack_stats(stats[0:1] + stats[1:2], stats[2:3] + stats[3:4], rows)
    for d, out_ref in enumerate((out0_ref, out1_ref, out2_ref, out3_ref)):
        at = pl.ds(pl.multiple_of(((x + d) % 4) * cols, cols), cols)
        out_ref[:cols, :] = (keep_ref[at, :].astype(F32) + got_ref[at, :].astype(F32)).astype(BF)
        out_ref[cols:, :] = packed


def finish_kernel(
    sc_ref, a_ref, b_ref, c_ref, d_ref, own_ref, stat_ref, gain_ref, grads_ref,
    points_ref, qkv_ref, proj_ref,
):
    step = pl.program_id(0)
    rows = a_ref.shape[1]
    cols = own_ref.shape[0] // 2
    width = gain_ref.shape[0]
    parts = [ref[...].astype(F32) for ref in (a_ref, b_ref, c_ref, d_ref)]
    total = (parts[0] + parts[1]) + (parts[2] + parts[3])
    gain = gain_ref[pl.ds(pl.multiple_of(sc_ref[4] * cols, cols), cols), :]
    mean = stat_ref[0:1, :]
    spread = stat_ref[4:5, :]
    normed = (own_ref[:cols, :].astype(F32) - mean) * spread
    first = (total[cols : cols + 1] + total[cols + 1 : cols + 2]) * (1.0 / width)
    second = (total[cols + 2 : cols + 3] + total[cols + 3 : cols + 4]) * (1.0 / width)
    dnorm = spread * (total[:cols] * gain - first - normed * second)
    out = own_ref[cols:, :].astype(F32) + dnorm
    slot = iota((cols, rows), 1) + step * rows
    out = jnp.where(slot < sc_ref[1], out, 0.0)
    points_ref[...] = out.T.astype(BF)

    @pl.when(step == 0)
    def _():
        grads = jnp.sum(grads_ref[...].astype(F32), axis=0)
        qkv_ref[...] = jnp.concatenate(
            [grads[:, h * GROUP : h * GROUP + 3 * HEAD] for h in range(4)], axis=1
        )
        proj = jnp.concatenate(
            [grads[:, h * GROUP + 3 * HEAD : (h + 1) * GROUP] for h in range(4)], axis=1
        )
        proj_ref[...] = proj.T


def whole(shape):
    return pl.BlockSpec(shape, lambda *_: (0,) * len(shape))


def call(kernel, sc, args, grid, in_specs, out_specs, out_shape, scratch, limit=48):
    return pl.pallas_call(
        kernel,
        grid_spec=pltpu.PrefetchScalarGridSpec(
            num_scalar_prefetch=1,
            grid=grid,
            in_specs=in_specs,
            out_specs=out_specs,
            scratch_shapes=scratch,
        ),
        out_shape=out_shape,
        compiler_params=pltpu.CompilerParams(vmem_limit_bytes=limit * MIB),
    )(sc, *args)


def project(sc, points, cotangent, gain, w_qkv, w_proj, spread):
    slots, width = points.shape
    cols = width // 8
    rows = 256
    shape = jax.ShapeDtypeStruct
    return call(
        project_kernel,
        sc,
        (points, cotangent, gain, w_qkv, w_proj, spread),
        (slots // rows,),
        [
            pl.BlockSpec((rows, width), lambda i, s: (i, 0)),
            pl.BlockSpec((rows, width), lambda i, s: (i, 0)),
            whole(gain.shape),
            whole(w_qkv.shape),
            whole(w_proj.shape),
            whole(spread.shape),
        ],
        [
            pl.BlockSpec((rows, LANES), lambda i, s: (i, 0)),
            pl.BlockSpec((rows, width), lambda i, s: (i, 0)),
            pl.BlockSpec((2 * cols, rows), lambda i, s: (0, i)),
            pl.BlockSpec((8, rows), lambda i, s: (0, i)),
            whole((width, LANES)),
            whole((16, LANES)),
        ],
        [
            shape((slots, LANES), BF),
            shape((slots, width), BF),
            shape((2 * cols, slots), BF),
            shape((8, slots), F32),
            shape((width, LANES), BF),
            shape((16, LANES), BF),
        ],
        [pltpu.VMEM((LANES, width), BF)],
    )


def attend(spanning, sc, own, following):
    slots = own.shape[0]
    shape = jax.ShapeDtypeStruct
    args = (own, following) if spanning else (own, own)
    outs = [shape((slots, LANES), BF)] + ([shape((PATCH, LANES), BF)] if spanning else [])
    result = call(
        functools.partial(attend_kernel, spanning),
        sc,
        args,
        (1,),
        [whole((slots, LANES)), whole((PATCH, LANES))],
        [whole(o.shape) for o in outs],
        outs,
        [
            pltpu.VMEM((PATCH, LANES), BF),
            pltpu.VMEM((PATCH, LANES), BF),
            pltpu.VMEM((PATCH, LANES), BF),
            pltpu.VMEM((LANES, PATCH), BF),
            pltpu.VMEM((4, PATCH, BLOCK), F32),
            pltpu.VMEM((PATCH, 8 * BLOCK), BF),
            pltpu.VMEM((8 * BLOCK, LANES), BF),
            pltpu.VMEM((PATCH, LANES), F32),
            pltpu.VMEM((LANES, PATCH), F32),
            pltpu.VMEM((PATCH, LANES), BF),
        ],
    )
    return result


def weights(sc, one, two, got, unit, dy, qkvu, wide, wg):
    slots, width = unit.shape
    rows = 256
    half = width // 2 + 16
    shape = jax.ShapeDtypeStruct
    by_rows = lambda i, s: (i, 0)
    last = PATCH // rows - 1
    return call(
        weight_kernel,
        sc,
        (one, two, got, unit, dy, qkvu, wide, wg),
        (slots // rows,),
        [
            pl.BlockSpec((rows, LANES), by_rows),
            pl.BlockSpec((rows, LANES), by_rows),
            pl.BlockSpec((rows, LANES), lambda i, s: (jnp.minimum(i, last), 0)),
            pl.BlockSpec((rows, width), by_rows),
            pl.BlockSpec((rows, width), by_rows),
            pl.BlockSpec((rows, LANES), by_rows),
            whole(wide.shape),
            whole(wg.shape),
        ],
        [
            pl.BlockSpec((half, rows), lambda i, s: (0, i)),
            pl.BlockSpec((half, rows), lambda i, s: (0, i)),
            whole((width, LANES)),
        ],
        [
            shape((half, slots), BF),
            shape((half, slots), BF),
            shape((width, LANES), BF),
        ],
        [
            pltpu.VMEM((width, LANES), BF),
            pltpu.VMEM((width, LANES), F32),
            pltpu.VMEM((width, LANES), F32),
        ],
    )


def pair_sum(sc, keep, got):
    total, slots = keep.shape
    cols = (total - 16) // 4 + 16
    rows = 512
    shape = jax.ShapeDtypeStruct((cols, slots), BF)
    spec = pl.BlockSpec((total, rows), lambda i, s: (0, i))
    out = pl.BlockSpec((cols, rows), lambda i, s: (0, i))
    return call(
        pair_kernel, sc, (keep, got), (slots // rows,), [spec] * 2, [out] * 4, [shape] * 4, []
    )


def finish(sc, parts, own, stat, gain_col, grads):
    cols, slots = own.shape
    cols //= 2
    n_space, weight_rows = grads.shape[:2]
    rows = 512
    shape = jax.ShapeDtypeStruct
    by_lanes = lambda i, s: (0, i)
    return call(
        finish_kernel,
        sc,
        (*parts, own, stat, gain_col, grads),
        (slots // rows,),
        [pl.BlockSpec((cols + 16, rows), by_lanes)] * 4
        + [
            pl.BlockSpec((2 * cols, rows), by_lanes),
            pl.BlockSpec((8, rows), by_lanes),
            whole(gain_col.shape),
            whole(grads.shape),
        ],
        [
            pl.BlockSpec((rows, cols), lambda i, s: (i, 0)),
            whole((weight_rows, 3 * GROUP)),
            whole((GROUP, weight_rows)),
        ],
        [
            shape((slots, cols), BF),
            shape((weight_rows, 3 * GROUP), F32),
            shape((GROUP, weight_rows), F32),
        ],
        [],
    )


def prefix(part, axis):
    size = lax.axis_size(axis)
    state = part
    step = 1
    while step < size:
        route = [(i, i + step) for i in range(size - step)]
        state = state + lax.ppermute(state, axis, route)
        step *= 2
    return state - part


def spread_matrix():
    column = jnp.arange(3 * GROUP)
    target = (column // (3 * HEAD)) * GROUP + column % (3 * HEAD)
    return (target[:, None] == jnp.arange(LANES)[None, :]).astype(BF)


def on_device(points, cotangent, cell_counts, norm_gain, w_qkv, w_proj):
    slots, width = points.shape
    n_space = lax.axis_size("space")
    n_mp = lax.axis_size("mp")
    place = lax.axis_index("space")
    member = lax.axis_index("mp")
    live = jnp.sum(cell_counts, dtype=jnp.int32)
    start = prefix(live.reshape(1), "space")[0]
    zero = jnp.zeros((), jnp.int32)
    where_i_am = jnp.stack([zero, zero, zero, zero, member, member % 2, member // 2, zero])
    qkvu, unit, own, stat, wide, wg = project(
        where_i_am, points, cotangent, norm_gain.reshape(1, width), w_qkv, w_proj, spread_matrix()
    )
    back = [(i + 1, i) for i in range(n_space - 1)]
    onward = [(i, i + 1) for i in range(n_space - 1)]
    following = lax.ppermute(qkvu[:PATCH], "space", back)
    head_len = (PATCH - start % PATCH) % PATCH
    tail_len = jnp.where(place == n_space - 1, 0, (PATCH - (start + live) % PATCH) % PATCH)
    n_patch = (live - head_len + PATCH - 1) // PATCH
    sc = jnp.stack(
        [head_len, live, n_patch, tail_len, member, member % 2, member // 2, zero]
    ).astype(jnp.int32)
    one, spill = attend(True, sc, qkvu, following)
    got = lax.ppermute(spill, "space", onward)
    two = attend(False, sc, qkvu, qkvu)[0]
    keep, send, grads = weights(sc, one, two, got, unit, cotangent, qkvu, wide, wg)
    swap = [(i, i ^ 1) for i in range(n_mp)]
    other = lax.ppermute(send, "mp", swap)
    grads = lax.all_to_all(
        grads.reshape(n_space, width // n_space, LANES), "space", 0, 0
    )
    parts = pair_sum(sc, keep, other)
    n_x = n_mp // 2
    received = [parts[0]]
    for d in range(1, n_x):
        route = [(i, (i + 2 * d) % n_mp) for i in range(n_mp)]
        received.append(lax.ppermute(parts[d], "mp", route))
    return tuple(finish(sc, received, own, stat, norm_gain.reshape(width, 1), grads))


def solution(mesh):
    return jax.shard_map(
        on_device,
        mesh=mesh,
        in_specs=(
            P("space", None),
            P("space", None),
            P("space"),
            P(),
            P(None, "mp"),
            P("mp", None),
        ),
        out_specs=(P("space", "mp"), P("space", "mp"), P("mp", "space")),
        check_vma=False,
    )
```

time: 534 us -> 146 us (0.27)
  matrix products: 251 us -> 0 us
  waiting for transfers between devices: 149 us -> 12.4 us
  Pallas kernels: 0 us -> 73 us
  blocking collectives: 55.3 us -> 0 us
  starting transfers between devices: 6.06 us -> 45.2 us
  other arithmetic: 25.3 us -> 0.74 us
  local copies, waits for them, and re-layouts: 29 us -> 6.5 us
  between operations: 17.2 us -> 5.99 us
    dot_general x25 -> x0, matrix products: 232 us -> none  [the longest x4 85.6 us: attend_block(): jnp.einsum('hqk,hke->hqe', dscore, key_rows, preferred_element_type=jnp.f...]
    psum x2 -> x0, waiting for transfers between devices: 149 us -> none  [the longest x1 78.3 us: on_device(): lax.psum(qkv_local.astype(jnp.bfloat16), 'space').astype(jnp.float32)]
    pallas_call x0 -> x6, Pallas kernels: none -> 73 us  [call(): pl.pallas_call(kernel, grid_spec=pltpu.PrefetchScalarGridSpec(num_scalar_...]
    unnamed x1 -> x0, blocking collectives: 55.3 us -> none
    ppermute x3 -> x10, starting transfers between devices: 5.98 us -> 38.9 us  [the longest x4 30.7 us: prefix(): state = state + lax.ppermute(state, axis, route)]
    sub x4 -> x0, matrix products: 18.9 us -> none  [attend_block(): exp_scores = jnp.exp(scores - row_max)]
    dynamic_update_slice x2 -> x0, local copies, waits for them, and re-layouts: 12.7 us -> none  [join_rows(): lax.dynamic_update_slice_in_dim(jnp.zeros((row_limit + extra, width), own...]
    reduce_sum x4 -> x1, other arithmetic: 9.59 us -> 0.63 us  [on_device(): live = jnp.sum(cell_counts, dtype=jnp.int32)]
  transfers between devices with their start and end apart: 5 -> 11, of which waited for: 2 -> 3; matrix products, arithmetic and copies ran while one was open for 6% -> 1% of each run, Pallas kernels for 0% -> 17%
where the time goes in v1:
time: 146 us; the launch traced here: 144 us
  Pallas kernels  73 us (50%)
  starting transfers between devices  45.2 us (31%)
  waiting for transfers between devices  12.4 us (8%)
  local copies, waits for them, and re-layouts  6.5 us (4%)
  between operations  5.99 us (4%)
    pallas_call x6, Pallas kernels, call(): pl.pallas_call(kernel, grid_spec=pltpu.PrefetchScalarGridSpec(num_scalar_...  73 us
    ppermute x4, starting transfers between devices, prefix(): state = state + lax.ppermute(state, axis, route)  30.7 us
    all_to_all x1, waiting for transfers between devices, on_device(): lax.all_to_all(grads.reshape(n_space, width // n_space, LANES), 'space',...  8.53 us
    all_to_all x1, starting transfers between devices, on_device(): lax.all_to_all(grads.reshape(n_space, width // n_space, LANES), 'space',...  6.28 us
    ppermute x3, starting transfers between devices, on_device(): received.append(lax.ppermute(parts[d], 'mp', route))  5.65 us
    unnamed x11, local copies, waits for them, and re-layouts  3.92 us
    ppermute x1, waiting for transfers between devices, on_device(): other = lax.ppermute(send, 'mp', swap)  2.96 us
  transfers between devices with their start and end apart: 11, of which 3 were waited for; matrix products, arithmetic and copies ran while one was open for 1% of the time, Pallas kernels for 17%

profile of v1, /device:TPU:0, one launch (start us, length us, event | category | flops | bytes accessed | tf_op | source)
XLA Modules:
  0.0 143.9 jit_solution(17428044887126438039)
XLA Ops:
  0.7 1.1 copy.12.wqkv_ref
  1.7 0.1 fusion.spread_ref
  1.9 0.1 stack.35.sc_ref
  1.9 0.0 copy-start.1
  1.9 0.8 copy-done.1
  2.8 0.0 copy-start.2
  2.8 0.7 copy-done.2
  3.5 0.0 copy-start.4
  3.5 8.3 %shard_map.85 = (bf16[2048,256]{1,0:T(8,128)(2,1)S(1)}, bf16[2048,512]{1,0:T(8,128)(2,1)S(1)}, bf16[128,2048]{1,0:T(8,128)(2,1)S(1)}, f32[8,2048]{1,0:T(8,128)S(...) custom-call(s32[8]{0:T(128)S(1)} %stack.35.sc_ref, bf16[2048,512]{1,0:T(8,128)(2,1)} %x_ref.1, ...), custom_call_target="tpu_custom_call" | custom-call | tf_op jit(solution)/shard_map/pallas_call | solution.py:353
  11.8 0.0 copy-start
  11.8 1.3 copy-done
  13.2 1.3 collective-permute-start.4
  14.5 0.0 copy-done.4
  14.5 0.6 reduce_sum.9
  15.1 5.1 %collective-permute-start = (s32[1]{0:T(128)}, s32[1]{0:T(128)}, u32[]{:S(2)}, u32[]{:S(2)}) collective-permute-start(s32[1]{0:T(128)} %bitcast), channel_id=1, source_target_pairs={{0,8},{8,16},{16,24},{24,32},{32,40},{40,48},{48,56},{56,64},{64,7... | collective-permute-start | bytes 20 | tf_op jit(solution)/shard_map/ppermute | solution.py:525
  20.2 0.9 collective-permute-done
  22.4 7.2 %collective-permute-start.1 = (s32[1]{0:T(128)}, s32[1]{0:T(128)}, u32[]{:S(2)}, u32[]{:S(2)}) collective-permute-start(s32[1]{0:T(128)} %add.60), channel_id=1, source_target_pairs={{0,16},{8,24},{16,32},{24,40},{32,48},{40,56},{48,64},{56,72},{64,... | collective-permute-start | bytes 20 | tf_op jit(solution)/shard_map/ppermute | solution.py:525
  29.6 0.0 collective-permute-done.1
  30.2 10.9 %collective-permute-start.2 = (s32[1]{0:T(128)}, s32[1]{0:T(128)}, u32[]{:S(2)}, u32[]{:S(2)}) collective-permute-start(s32[1]{0:T(128)} %add.61), channel_id=1, source_target_pairs={{0,32},{8,40},{16,48},{24,56},{32,64},{40,72},{48,80},{56,88},{64,... | collective-permute-start | bytes 20 | tf_op jit(solution)/shard_map/ppermute | solution.py:525
  41.1 0.0 collective-permute-done.2
  41.8 7.5 %collective-permute-start.3 = (s32[1]{0:T(128)}, s32[1]{0:T(128)}, u32[]{:S(2)}, u32[]{:S(2)}) collective-permute-start(s32[1]{0:T(128)} %add.62), channel_id=1, source_target_pairs={{0,64},{8,72},{16,80},{24,88},{32,96},{40,104},{48,112},{56,120},{... | collective-permute-start | bytes 20 | tf_op jit(solution)/shard_map/ppermute | solution.py:525
  49.2 0.0 collective-permute-done.3
  51.9 0.7 stack.34.sc_ref
  52.6 0.0 collective-permute-done.4.next_ref
  52.6 27.5 %shard_map.86 = (bf16[2048,256]{1,0:T(8,128)(2,1)S(1)}, bf16[1024,256]{1,0:T(8,128)(2,1)S(1)}) custom-call(s32[8]{0:T(128)S(1)} %stack.34.sc_ref, bf16[2048,256]{1,0:T(8,128)(2,1)S(1)} %get-tuple-element.18.own_ref.next_ref.qkvu_ref, bf16[1024,256]{1,0:T(8,128)(2,1)S(1)} %collective-permute-done.4.next_ref), custom_call_target="tpu_custom_call" | custom-call | tf_op jit(solution)/shard_map/pallas_call | solution.py:353
  80.2 1.3 collective-permute-start.5
  81.5 24.1 %shard_map.87.two_ref = bf16[2048,256]{1,0:T(8,128)(2,1)S(1)} custom-call(s32[8]{0:T(128)S(1)} %stack.34.sc_ref, bf16[2048,256]{1,0:T(8,128)(2,1)S(1)} %get-tuple-element.18.own_ref.next_ref.qkvu_ref, bf16[2048,256]{1,0:T(8,128)(2,1)S(1)} %get-tuple-element.18.own_ref.next_ref.qkvu_ref), custom_call_target="tpu_custom_call" | custom-call | tf_op jit(solution)/shard_map/pallas_call | solution.py:353
  105.6 0.0 collective-permute-done.5.got_ref
  105.6 8.4 %shard_map.88 = (bf16[272,2048]{1,0:T(8,128)(2,1)S(1)}, bf16[272,2048]{1,0:T(8,128)(2,1)}, bf16[512,256]{1,0:T(8,128)(2,1)}) custom-call(s32[8]{0:T(128)S(1)} %stack.34.sc_ref, bf16[2048,256]{1,0:T(8,128)(2,1)S(1)} %get-tuple-element.19.one_ref, bf16[2048,256]{1,0:T(8,128)(2,1)S(1)} %shard_map.87.two_ref, ...), custom_call_target="tpu_custom_call" | custom-call | tf_op jit(solution)/shard_map/pallas_call | solution.py:353
  114.1 0.0 copy-start.3
  114.1 0.0 collective-permute-start.6
  114.1 3.0 %collective-permute-done.6.got_ref = bf16[272,2048]{1,0:T(8,128)(2,1)S(1)} collective-permute-done((bf16[272,2048]{1,0:T(8,128)(2,1)}, bf16[272,2048]{1,0:T(8,128)(2,1)S(1)}, u32[]{:S(2)}, u32[]{:S(2)}) %collective-permute-start.6) | collective-permute-done | bytes 1114144 | tf_op jit(solution)/shard_map/ppermute | solution.py:563
  117.1 2.3 %shard_map.89 = (bf16[80,2048]{1,0:T(8,128)(2,1)S(1)}, bf16[80,2048]{1,0:T(8,128)(2,1)}, bf16[80,2048]{1,0:T(8,128)(2,1)S(1)}, bf16[80,2048]{1,0:T(8,128)(2,1)S(1)}) custom-call(s32[8]{0:T(128)S(1)} %stack.34.sc_ref, bf16[272,2048]{1,0:T(8,128)(2,1)S(1)} %get-tuple-element.24.keep_ref, bf16[272,2048]{1,0:T(8,128)(2,1)S(1)} %collective-permute-done.6.got_ref), custom_call_target="tpu_custom_call" | custom-call | tf_op jit(solution)/shard_map/pallas_call | solution.py:353
  119.3 1.5 %collective-permute-start.7 = (bf16[80,2048]{1,0:T(8,128)(2,1)}, bf16[80,2048]{1,0:T(8,128)(2,1)S(1)}, u32[]{:S(2)}, u32[]{:S(2)}) collective-permute-start(bf16[80,2048]{1,0:T(8,128)(2,1)} %get-tuple-element.27), channel_id=1, source_target_pairs={{0,2},{1,3},{2,4},{3,5},{4,6},{5,7},{6,0},{7,1},{8,10},{9,11},{10,... | collective-permute-start | bytes 983048 | tf_op jit(solution)/shard_map/ppermute | solution.py:572
  120.8 2.7 %collective-permute-start.8 = (bf16[80,2048]{1,0:T(8,128)(2,1)S(1)}, bf16[80,2048]{1,0:T(8,128)(2,1)S(1)}, u32[]{:S(2)}, u32[]{:S(2)}) collective-permute-start(bf16[80,2048]{1,0:T(8,128)(2,1)S(1)} %get-tuple-element.28), channel_id=1, source_target_pairs={{0,4},{1,5},{2,6},{3,7},{4,0},{5,1},{6,2},{7,3},{8,12},{9,13},{10,... | collective-permute-start | bytes 983048 | tf_op jit(solution)/shard_map/ppermute | solution.py:572
  123.5 1.4 collective-permute-start.9
  125.0 6.3 %all-to-all-start = ((bf16[16,32,256]{2,1,0:T(8,128)(2,1)}), bf16[16,32,256]{2,1,0:T(8,128)(2,1)S(1)}, u32[]{:S(2)}, u32[]{:S(2)}) async-start(bf16[16,32,256]{2,1,0:T(8,128)(2,1)} %bitcast.10), calls=%async_computation | async-start | bytes 524288 | tf_op jit(solution)/shard_map/all_to_all | solution.py:564
  131.3 0.0 copy-done.3
  131.3 0.1 copy.13.gain_ref
  131.4 8.5 %all-to-all-done.grads_ref = bf16[16,32,256]{2,1,0:T(8,128)(2,1)S(1)} async-done(((bf16[16,32,256]{2,1,0:T(8,128)(2,1)}), bf16[16,32,256]{2,1,0:T(8,128)(2,1)S(1)}, u32[]{:S(2)}, u32[]{:S(2)}) %all-to-all-start) | async-done | bytes 262176 | tf_op jit(solution)/shard_map/all_to_all | solution.py:564
  140.0 0.0 collective-permute-done.7.b_ref
  140.0 0.0 collective-permute-done.8.c_ref
  140.0 0.0 collective-permute-done.9.d_ref
  140.0 2.3 %shard_map.90 = (bf16[2048,64]{1,0:T(8,128)(2,1)S(1)}, f32[32,192]{1,0:T(8,128)}, f32[64,32]{1,0:T(8,128)S(1)}) custom-call(s32[8]{0:T(128)S(1)} %stack.34.sc_ref, bf16[80,2048]{1,0:T(8,128)(2,1)S(1)} %get-tuple-element.26.a_ref, bf16[80,2048]{1,0:T(8,128)(2,1)S(1)} %collective-permute-done.7.b_ref, bf16[80,2048]{1,0:T(8,128)(2,1)S(1)} %collective-permute-done.8.c_ref, ...), custom_call_target="tpu_custom_call" | custom-call | tf_op jit(solution)/shard_map/pallas_call | solution.py:353
  142.3 0.9 copy.14
  143.2 0.7 copy.15
  (3 shorter events, 0.0 us)
Async XLA Ops:
  1.9 0.8 copy-start.1
  2.8 0.7 copy-start.2
  3.5 11.0 %copy-start.4 = (s32[128]{0:T(128)S(1)}, s32[128]{0:T(128)}, u32[]{:S(2)}) copy-start(s32[128]{0:T(128)} %param.8) | copy-start | bytes 1540
  11.8 1.3 copy-start
  13.2 39.4 %collective-permute-start.4 = (bf16[1024,256]{1,0:T(8,128)(2,1)S(1)}, bf16[1024,256]{1,0:T(8,128)(2,1)S(1)}, u32[]{:S(2)}, u32[]{:S(2)}) collective-permute-start(bf16[1024,256]{1,0:T(8,128)(2,1)S(1)} %slice.3), channel_id=1, source_target_pairs={{8,0},{16,8},{24,16},{32,24},{40,32},{48,40},{56,48},{64,56},{72,6... | collective-permute-start | bytes 1572872 | tf_op jit(solution)/shard_map/ppermute | solution.py:551
  15.1 6.0 %collective-permute-start = (s32[1]{0:T(128)}, s32[1]{0:T(128)}, u32[]{:S(2)}, u32[]{:S(2)}) collective-permute-start(s32[1]{0:T(128)} %bitcast), channel_id=1, source_target_pairs={{0,8},{8,16},{16,24},{24,32},{32,40},{40,48},{48,56},{56,64},{64,7... | collective-permute-start | bytes 20 | tf_op jit(solution)/shard_map/ppermute | solution.py:525
  22.4 7.2 %collective-permute-start.1 = (s32[1]{0:T(128)}, s32[1]{0:T(128)}, u32[]{:S(2)}, u32[]{:S(2)}) collective-permute-start(s32[1]{0:T(128)} %add.60), channel_id=1, source_target_pairs={{0,16},{8,24},{16,32},{24,40},{32,48},{40,56},{48,64},{56,72},{64,... | collective-permute-start | bytes 20 | tf_op jit(solution)/shard_map/ppermute | solution.py:525
  30.2 10.9 %collective-permute-start.2 = (s32[1]{0:T(128)}, s32[1]{0:T(128)}, u32[]{:S(2)}, u32[]{:S(2)}) collective-permute-start(s32[1]{0:T(128)} %add.61), channel_id=1, source_target_pairs={{0,32},{8,40},{16,48},{24,56},{32,64},{40,72},{48,80},{56,88},{64,... | collective-permute-start | bytes 20 | tf_op jit(solution)/shard_map/ppermute | solution.py:525
  41.8 7.5 %collective-permute-start.3 = (s32[1]{0:T(128)}, s32[1]{0:T(128)}, u32[]{:S(2)}, u32[]{:S(2)}) collective-permute-start(s32[1]{0:T(128)} %add.62), channel_id=1, source_target_pairs={{0,64},{8,72},{16,80},{24,88},{32,96},{40,104},{48,112},{56,120},{... | collective-permute-start | bytes 20 | tf_op jit(solution)/shard_map/ppermute | solution.py:525
  80.2 25.5 %collective-permute-start.5 = (bf16[1024,256]{1,0:T(8,128)(2,1)S(1)}, bf16[1024,256]{1,0:T(8,128)(2,1)S(1)}, u32[]{:S(2)}, u32[]{:S(2)}) collective-permute-start(bf16[1024,256]{1,0:T(8,128)(2,1)S(1)} %get-tuple-element.20), channel_id=1, source_target_pairs={{0,8},{8,16},{16,24},{24,32},{32,40},{40,48},{48,56},{56,64},{64,7... | collective-permute-start | bytes 1572872 | tf_op jit(solution)/shard_map/ppermute | solution.py:559
  114.1 17.2 %copy-start.3 = (f32[512]{0:T(512)S(1)}, f32[512]{0:T(512)}, u32[]{:S(2)}) copy-start(f32[512]{0:T(512)} %param.9) | copy-start | bytes 6148
  114.1 3.0 %collective-permute-start.6 = (bf16[272,2048]{1,0:T(8,128)(2,1)}, bf16[272,2048]{1,0:T(8,128)(2,1)S(1)}, u32[]{:S(2)}, u32[]{:S(2)}) collective-permute-start(bf16[272,2048]{1,0:T(8,128)(2,1)} %get-tuple-element.25), channel_id=1, source_target_pairs={{0,1},{1,0},{2,3},{3,2},{4,5},{5,4},{6,7},{7,6},{8,9},{9,8},{10,11... | collective-permute-start | bytes 3342344 | tf_op jit(solution)/shard_map/ppermute | solution.py:563
  119.3 20.6 %collective-permute-start.7 = (bf16[80,2048]{1,0:T(8,128)(2,1)}, bf16[80,2048]{1,0:T(8,128)(2,1)S(1)}, u32[]{:S(2)}, u32[]{:S(2)}) collective-permute-start(bf16[80,2048]{1,0:T(8,128)(2,1)} %get-tuple-element.27), channel_id=1, source_target_pairs={{0,2},{1,3},{2,4},{3,5},{4,6},{5,7},{6,0},{7,1},{8,10},{9,11},{10,... | collective-permute-start | bytes 983048 | tf_op jit(solution)/shard_map/ppermute | solution.py:572
  120.8 19.1 %collective-permute-start.8 = (bf16[80,2048]{1,0:T(8,128)(2,1)S(1)}, bf16[80,2048]{1,0:T(8,128)(2,1)S(1)}, u32[]{:S(2)}, u32[]{:S(2)}) collective-permute-start(bf16[80,2048]{1,0:T(8,128)(2,1)S(1)} %get-tuple-element.28), channel_id=1, source_target_pairs={{0,4},{1,5},{2,6},{3,7},{4,0},{5,1},{6,2},{7,3},{8,12},{9,13},{10,... | collective-permute-start | bytes 983048 | tf_op jit(solution)/shard_map/ppermute | solution.py:572
  123.5 16.4 %collective-permute-start.9 = (bf16[80,2048]{1,0:T(8,128)(2,1)S(1)}, bf16[80,2048]{1,0:T(8,128)(2,1)S(1)}, u32[]{:S(2)}, u32[]{:S(2)}) collective-permute-start(bf16[80,2048]{1,0:T(8,128)(2,1)S(1)} %get-tuple-element.29), channel_id=1, source_target_pairs={{0,6},{1,7},{2,0},{3,1},{4,2},{5,3},{6,4},{7,5},{8,14},{9,15},{10,... | collective-permute-start | bytes 983048 | tf_op jit(solution)/shard_map/ppermute | solution.py:572
  125.0 15.0 %all-to-all-start = ((bf16[16,32,256]{2,1,0:T(8,128)(2,1)}), bf16[16,32,256]{2,1,0:T(8,128)(2,1)S(1)}, u32[]{:S(2)}, u32[]{:S(2)}) async-start(bf16[16,32,256]{2,1,0:T(8,128)(2,1)} %bitcast.10), calls=%async_computation | async-start | bytes 524288 | tf_op jit(solution)/shard_map/all_to_all | solution.py:564

commit v2 on v1

v2 whole, which is shorter than its diff:
```python
import functools

import jax
import jax.numpy as jnp
from jax import lax
from jax.experimental import pallas as pl
from jax.experimental.pallas import tpu as pltpu
from jax.sharding import PartitionSpec as P

H = 32
PATCH = 1024
EPS = 1e-05
MASKED = -1e30
HEAD = 16
GROUP = 64
LANES = 256
PAIR = 128
BLOCK = 256
SHIFT = 128
MIB = 1024 * 1024
LOG2E = 1.4426950408889634
SAFE = 40.0

BF = jnp.bfloat16
F32 = jnp.float32
NT = (((1,), (1,)), ((), ()))
TN = (((0,), (0,)), ((), ()))


def dot(a, b):
    return jnp.dot(a, b, preferred_element_type=F32)


def dot_nt(a, b):
    return lax.dot_general(a, b, NT, preferred_element_type=F32)


def dot_tn(a, b):
    return lax.dot_general(a, b, TN, preferred_element_type=F32)


def iota(shape, axis):
    return lax.broadcasted_iota(jnp.int32, shape, axis)


def onehot(mask):
    return jnp.where(mask, 1.0, 0.0).astype(BF)


def split(value):
    high = value.astype(BF)
    return high, (value - high.astype(F32)).astype(BF)


def project_kernel(lead, sc_ref, x_ref, dy_ref, gain_ref, *rest):
    if lead:
        wqkv_ref, wproj_ref, spread_ref = rest[:3]
        outs = rest[4:]
        wide_ref, side_ref, wg_ref = outs[5:8]
    else:
        wide_ref, side_ref = rest[:2]
        outs = rest[8:]
    one_ref, two_ref, unit_ref, own_ref, stat_ref = outs[:5]
    rows, width = x_ref.shape
    cols = own_ref.shape[0] // 2
    gain = gain_ref[...]

    if lead:
        @pl.when(pl.program_id(0) == 0)
        def _():
            wide = dot_tn(wqkv_ref[...], spread_ref[...]).astype(BF)
            wide_ref[...] = wide
            part = iota((GROUP, LANES), 0)
            lane = iota((GROUP, LANES), 1)
            up = onehot(lane == (part // HEAD) * GROUP + 3 * HEAD + part % HEAD)
            side_ref[:, :LANES] = dot_tn(wproj_ref[...], up).astype(BF)
            row = iota((width, cols), 0)
            col = iota((width, cols), 1)
            pick = onehot(row == col + sc_ref[4] * cols)
            none = jnp.zeros((width, cols), BF)
            side_ref[:, LANES:] = jnp.concatenate([none, pick, pick, none], axis=1)
            gain_high, gain_low = split(jnp.broadcast_to(gain, (16, width)))
            wg = dot(gain_high, wide) + dot(gain_low, wide)
            wg_high, wg_low = split(wg)
            row = iota((16, LANES), 0)
            wg_ref[...] = jnp.where(
                row == 0, wg_high.astype(F32), jnp.where(row == 1, wg_low.astype(F32), 0.0)
            ).astype(BF)

    x_low = x_ref[...]
    x = x_low.astype(F32)
    mean = jnp.mean(x, axis=-1, keepdims=True)
    center = x - mean
    spread = lax.rsqrt(jnp.mean(center * center, axis=-1, keepdims=True) + EPS)
    unit = (center * spread * gain).astype(BF)
    unit_ref[...] = unit
    from_dy = dot(dy_ref[...], side_ref[:, : LANES + PAIR])
    qkvu = (dot(unit, wide_ref[...]) + from_dy[:, :LANES]).astype(BF)
    one_ref[...] = qkvu[:, :PAIR]
    two_ref[...] = qkvu[:, PAIR:]
    own = dot(x_low, side_ref[:, LANES + PAIR :]) + from_dy[:, LANES:]
    own_ref[...] = own.T.astype(BF)
    both = jnp.where(iota((rows, 128), 1) < 4, mean, spread)
    stat_ref[...] = both.T[:8, :]


def shift_rows(src_ref, total, first, low, high):
    base = jnp.clip((first // SHIFT) * SHIFT, 0, total - 2 * SHIFT)
    base = pl.multiple_of(base, SHIFT)
    row = iota((SHIFT, 2 * SHIFT), 0) + first
    col = iota((SHIFT, 2 * SHIFT), 1) + base
    pick = onehot((row == col) & (row >= low) & (row < high))
    return dot(pick, src_ref[pl.ds(base, 2 * SHIFT), :])


def attend_kernel(spanning, extra_args, sc_ref, own_ref, *rest):
    if spanning:
        next_ref = rest[0]
        out_ref, out_next_ref = rest[1 + extra_args : 3 + extra_args]
        rest = rest[3 + extra_args :]
    else:
        out_ref = rest[extra_args]
        rest = rest[1 + extra_args :]
    (x_ref, left_ref, flip_ref, value_ref, top_ref, exp_ref, low_ref, grad_ref, right_ref, sum_ref,
     turn_ref, done_ref) = rest
    slots = own_ref.shape[0]
    head_len = sc_ref[0]
    count = sc_ref[1]
    n_patch = sc_ref[2]
    tail_len = sc_ref[3]
    scale = HEAD ** (-0.5)

    def work():
        first = head_len + (PATCH * (n_patch - 1) if spanning else 0)

        def gather(i, carry):
            start = pl.multiple_of(i * SHIFT, SHIFT)
            piece = shift_rows(own_ref, slots, first + start, 0, count)
            if spanning:
                piece = piece + shift_rows(next_ref, PATCH, first + start - count, 0, tail_len)
            x_ref[pl.ds(start, SHIFT), :] = piece.astype(BF)
            return carry

        lax.fori_loop(0, PATCH // SHIFT, gather, 0, unroll=True)
        x = x_ref[...]
        src = iota((PAIR, PAIR), 0)
        dst = iota((PAIR, PAIR), 1)
        sub = dst & (GROUP - 1)
        keys = sub < 2 * HEAD
        move = onehot(
            ((sub < HEAD) & (src == dst + HEAD))
            | ((sub >= HEAD) & (sub < 3 * HEAD) & (src == dst))
        )
        lane = iota((PATCH, PAIR), 1) & (GROUP - 1)
        fixed = jnp.where((lane > 3 * HEAD) & (lane < 3 * HEAD + 4), 1.0, 0.0)
        if spanning:
            valid = count - first + tail_len
            row = iota((PATCH, PAIR), 0)
            fixed = jnp.where((lane == 3 * HEAD) & (row >= valid), MASKED, fixed)
        left_ref[...] = (dot(x, move) + fixed).astype(BF)
        flip = dot_nt(onehot(src == dst), x)
        flip_ref[...] = flip.astype(BF)
        square = flip * flip
        bounded = True
        for h in range(2):
            at = h * GROUP
            value_ref[h, :HEAD, :] = flip_ref[at + 2 * HEAD : at + 3 * HEAD, :]
            value_ref[h, HEAD:, :] = jnp.ones((HEAD, PATCH), BF)
            most_q = jnp.max(jnp.sum(square[at : at + HEAD], axis=0))
            most_k = jnp.max(jnp.sum(square[at + HEAD : at + 2 * HEAD], axis=0))
            bounded &= most_q * most_k * scale * scale <= SAFE * SAFE
        sum_ref[...] = jnp.zeros_like(sum_ref)
        turn_ref[...] = jnp.zeros_like(turn_ref)
        right_ref[...] = jnp.zeros_like(right_ref)
        top_ref[...] = jnp.zeros_like(top_ref)
        row = iota((HEAD, BLOCK), 0)

        def placed(pieces, h):
            zero = jnp.zeros((GROUP, BLOCK), BF)
            group = jnp.concatenate(pieces, axis=0)
            return jnp.concatenate([group, zero] if h % 2 == 0 else [zero, group], axis=0)

        nothing = jnp.zeros((HEAD, BLOCK), BF)

        def score_right(h, here, top):
            query = flip_ref[h * GROUP : h * GROUP + HEAD, here].astype(F32) * (scale * LOG2E)
            high, low = split(query)
            if top is None:
                extra = jnp.where(row == 0, 1.0, 0.0)
            else:
                top_high = top.astype(BF).astype(F32)
                top_mid = (top - top_high).astype(BF).astype(F32)
                top_low = top - top_high - top_mid
                extra = jnp.where(
                    row == 0,
                    1.0,
                    jnp.where(
                        row == 1,
                        -top_high,
                        jnp.where(row == 2, -top_mid, jnp.where(row == 3, -top_low, 0.0)),
                    ),
                )
            return placed([high, low, nothing, extra.astype(BF)], h)

        def block(step, carry):
            here = [
                pl.ds(pl.multiple_of((step * 2 + t // 2) * BLOCK, BLOCK), BLOCK) for t in range(4)
            ]

            @pl.when(jnp.logical_not(bounded))
            def _():
                for t in range(4):
                    scores = dot(left_ref[...], score_right(t % 2, here[t], None))
                    top_ref[t : t + 1, :] = jnp.max(scores, axis=0, keepdims=True)

            inverses = [None] * 4
            rights = [None] * 4
            spans = [slice(t * BLOCK, (t + 1) * BLOCK) for t in range(4)]

            def stage_exp(t):
                scores = dot(left_ref[...], score_right(t % 2, here[t], top_ref[t : t + 1, :]))
                exps = jnp.exp2(scores)
                exp_ref[t] = exps
                low_ref[:, spans[t]] = exps.astype(BF)

            def stage_sum(t):
                at = (t % 2) * GROUP
                result = dot(value_ref[t % 2], low_ref[:, spans[t]])
                inverse = 1.0 / result[HEAD : HEAD + 1]
                inverses[t] = inverse
                attended = result[:HEAD] * inverse
                turn_ref[at + 3 * HEAD : at + 4 * HEAD, here[t]] = attended
                up = flip_ref[at + 3 * HEAD : at + 4 * HEAD, here[t]].astype(F32)
                scaled = up * scale
                delta = jnp.sum(scaled * attended, axis=0, keepdims=True)
                delta_high = delta.astype(BF).astype(F32)
                extra = jnp.where(
                    row == 1, -delta_high, jnp.where(row == 2, delta_high - delta, 0.0)
                ).astype(BF)
                rights[t] = placed([nothing, nothing, scaled.astype(BF), extra], t % 2)
                query = flip_ref[at : at + HEAD, here[t]].astype(F32)
                right_ref[at + 2 * HEAD : at + 3 * HEAD, spans[t]] = (up * inverse).astype(BF)
                right_ref[
                    at + HEAD : at + 2 * HEAD, (4 + t) * BLOCK : (5 + t) * BLOCK
                ] = (query * inverse).astype(BF)

            def stage_grad(t):
                dprob = dot(left_ref[...], rights[t])
                grad_ref[:, spans[t]] = (exp_ref[t] * dprob).astype(BF)

            def stage_query(t):
                at = (t % 2) * GROUP
                result = dot(flip_ref[at + HEAD : at + 2 * HEAD, :], grad_ref[:, spans[t]])
                turn_ref[at : at + HEAD, here[t]] = result * inverses[t]

            for stage in (stage_exp, stage_sum, stage_grad, stage_query):
                for t in range(4):
                    stage(t)
            sum_ref[...] += dot_nt(low_ref[...], right_ref[:, : 4 * BLOCK]) + dot_nt(
                grad_ref[...], right_ref[:, 4 * BLOCK :]
            )
            return carry

        lax.fori_loop(0, PATCH // (2 * BLOCK), block, 0)
        done_ref[...] = (sum_ref[...] + turn_ref[...].T).astype(BF)

        def scatter(i, carry):
            start = pl.multiple_of(i * SHIFT, SHIFT)
            piece = shift_rows(done_ref, PATCH, start - first, 0, jnp.minimum(PATCH, count - first))
            out_ref[pl.ds(start, SHIFT), :] = piece.astype(BF)
            return carry

        lax.fori_loop(0, slots // SHIFT, scatter, 0, unroll=True)
        if spanning:
            def scatter_next(i, carry):
                start = pl.multiple_of(i * SHIFT, SHIFT)
                piece = shift_rows(
                    done_ref, PATCH, start + count - first, 0, count - first + tail_len
                )
                out_next_ref[pl.ds(start, SHIFT), :] = piece.astype(BF)
                return carry

            lax.fori_loop(0, PATCH // SHIFT, scatter_next, 0, unroll=True)

    if spanning:
        work()
    else:
        pl.when(n_patch == 2)(work)

        @pl.when(n_patch < 2)
        def _():
            out_ref[...] = jnp.zeros_like(out_ref)


def product_kernel(
    sc_ref, a_ref, b_ref, c_ref, d_ref, e_ref, f_ref, one_ref, two_ref, wide_ref, wg_ref,
    keep_ref, send_ref, total_ref, turned_ref,
):
    step = pl.program_id(0)
    rows = a_ref.shape[0]
    core = sc_ref[5]
    cols = wide_ref.shape[0] // 8

    @pl.when(step == 0)
    def _():
        for side in range(2):
            for x in range(4):
                from_row = pl.multiple_of((2 * x + (core ^ side)) * cols, cols)
                to_row = (side * 4 + x) * cols
                turned_ref[to_row : to_row + cols, :] = wide_ref[pl.ds(from_row, cols), :]

    here = step < PATCH // rows
    sums = []
    for refs in ((a_ref, c_ref, e_ref), (b_ref, d_ref, f_ref)):
        got = jnp.where(here, refs[2][...].astype(F32), 0.0)
        sums.append(refs[0][...].astype(F32) + refs[1][...].astype(F32) + got)
    wide_total = jnp.concatenate(sums, axis=1)
    total = wide_total.astype(BF)
    total_ref[...] = total
    du = dot_nt(turned_ref[...], total).astype(BF)
    half = 4 * cols
    keep_ref[:half, :] = du[:half]
    send_ref[:half, :] = du[half:]
    lane = iota((rows, LANES), 1) & (GROUP - 1)
    qkvu = jnp.concatenate([one_ref[...], two_ref[...]], axis=1).astype(F32)
    product = jnp.where(lane < 3 * HEAD, wide_total * qkvu, 0.0)
    high, low = split(product)
    ones = jnp.ones((16, LANES), BF)
    second = (dot_nt(ones, high) + dot_nt(ones, low))[:1]
    first_rows = dot_nt(wg_ref[...], total)
    first = first_rows[:1] + first_rows[1:2]
    stats = pack_stats(first, second, rows)
    keep_ref[half:, :] = stats
    send_ref[half:, :] = stats


def weight_kernel(sc_ref, total_ref, unit_ref, dy_ref, after_ref, grads_ref, gu_ref, gy_ref):
    step = pl.program_id(0)

    @pl.when(step == 0)
    def _():
        gu_ref[...] = jnp.zeros_like(gu_ref)
        gy_ref[...] = jnp.zeros_like(gy_ref)

    total = total_ref[...]
    gu_ref[...] += dot_tn(total, unit_ref[...])
    gy_ref[...] += dot_tn(total, dy_ref[...])

    @pl.when(step == pl.num_programs(0) - 1)
    def _():
        row = iota(gu_ref.shape, 0) & (GROUP - 1)
        grads_ref[...] = jnp.where(row < 3 * HEAD, gu_ref[...], gy_ref[...]).T.astype(BF)


def pack_stats(first, second, rows):
    row = iota((16, rows), 0)
    first_high = first.astype(BF).astype(F32)
    second_high = second.astype(BF).astype(F32)
    return jnp.where(
        row == 0,
        first_high,
        jnp.where(
            row == 1,
            first - first_high,
            jnp.where(row == 2, second_high, jnp.where(row == 3, second - second_high, 0.0)),
        ),
    ).astype(BF)


def pair_kernel(sc_ref, keep_ref, got_ref, after_ref, out0_ref, out1_ref, out2_ref, out3_ref):
    x = sc_ref[6]
    rows = keep_ref.shape[1]
    half = keep_ref.shape[0] - 16
    cols = half // 4
    stats = keep_ref[half:, :].astype(F32) + got_ref[half:, :].astype(F32)
    packed = pack_stats(stats[0:1] + stats[1:2], stats[2:3] + stats[3:4], rows)
    for d, out_ref in enumerate((out0_ref, out1_ref, out2_ref, out3_ref)):
        at = pl.ds(pl.multiple_of(((x + d) % 4) * cols, cols), cols)
        out_ref[:cols, :] = (keep_ref[at, :].astype(F32) + got_ref[at, :].astype(F32)).astype(BF)
        out_ref[cols:, :] = packed


def finish_kernel(
    sc_ref, a_ref, b_ref, c_ref, d_ref, own_ref, stat_ref, gain_ref, grads_ref,
    points_ref, qkv_ref, proj_ref,
):
    step = pl.program_id(0)
    rows = a_ref.shape[1]
    cols = own_ref.shape[0] // 2
    width = gain_ref.shape[1]
    parts = [ref[...].astype(F32) for ref in (a_ref, b_ref, c_ref, d_ref)]
    total = (parts[0] + parts[1]) + (parts[2] + parts[3])
    mine = iota((cols, width), 1) == iota((cols, width), 0) + sc_ref[4] * cols
    gain = jnp.sum(jnp.where(mine, gain_ref[...], 0.0), axis=1, keepdims=True)
    mean = stat_ref[0:1, :]
    spread = stat_ref[4:5, :]
    normed = (own_ref[:cols, :].astype(F32) - mean) * spread
    first = (total[cols : cols + 1] + total[cols + 1 : cols + 2]) * (1.0 / width)
    second = (total[cols + 2 : cols + 3] + total[cols + 3 : cols + 4]) * (1.0 / width)
    dnorm = spread * (total[:cols] * gain - first - normed * second)
    out = own_ref[cols:, :].astype(F32) + dnorm
    slot = iota((cols, rows), 1) + step * rows
    points_ref[...] = jnp.where(slot < sc_ref[1], out, 0.0).astype(BF)

    @pl.when(step == 0)
    def _():
        grads = jnp.sum(grads_ref[...].astype(F32), axis=0)
        qkv_ref[...] = jnp.concatenate(
            [grads[:, h * GROUP : h * GROUP + 3 * HEAD] for h in range(4)], axis=1
        )
        proj_ref[...] = jnp.concatenate(
            [grads[:, h * GROUP + 3 * HEAD : (h + 1) * GROUP] for h in range(4)], axis=1
        )


def whole(shape):
    return pl.BlockSpec(shape, lambda *_: (0,) * len(shape))


ANY = pl.BlockSpec(memory_space=pl.ANY)
shape = jax.ShapeDtypeStruct


def call(kernel, sc, args, grid, in_specs, out_specs, out_shape, scratch, limit, micros, aliases={}):
    return pl.pallas_call(
        kernel,
        grid_spec=pltpu.PrefetchScalarGridSpec(
            num_scalar_prefetch=1,
            grid=grid,
            in_specs=in_specs,
            out_specs=out_specs,
            scratch_shapes=scratch,
        ),
        out_shape=out_shape,
        input_output_aliases=aliases,
        cost_estimate=pl.CostEstimate(
            flops=int(micros * 1.1e9), bytes_accessed=0, transcendentals=0
        ),
        compiler_params=pltpu.CompilerParams(vmem_limit_bytes=limit * MIB),
    )(sc, *args)


def project(sc, points, cotangent, gain, w_qkv, w_proj, spread, after):
    slots, width = points.shape
    cols = width // 8
    rows = 256
    steps = slots // (2 * rows)
    outs = [
        shape((slots, PAIR), BF),
        shape((slots, PAIR), BF),
        shape((slots, width), BF),
        shape((2 * cols, slots), BF),
        shape((8, slots), F32),
    ]
    extra = [shape((width, LANES), BF), shape((width, LANES + 2 * PAIR), BF), shape((16, LANES), BF)]

    def specs(offset):
        down = lambda i, s: (i + offset, 0)
        across = lambda i, s: (0, i + offset)
        return (
            [pl.BlockSpec((rows, width), down)] * 2 + [whole(gain.shape)],
            [pl.BlockSpec((rows, PAIR), down)] * 2
            + [
                pl.BlockSpec((rows, width), down),
                pl.BlockSpec((2 * cols, rows), across),
                pl.BlockSpec((8, rows), across),
            ],
        )

    ins, out_specs = specs(0)
    results = call(
        functools.partial(project_kernel, True),
        sc,
        (points, cotangent, gain, w_qkv, w_proj, spread, after[0]),
        (steps,),
        ins + [whole(w_qkv.shape), whole(w_proj.shape), whole(spread.shape), ANY],
        out_specs + [whole(e.shape) for e in extra],
        outs + extra,
        [],
        16,
        4.5,
    )
    ins, out_specs = specs(steps)
    again = call(
        functools.partial(project_kernel, False),
        sc,
        (points, cotangent, gain, results[5], results[6], *results[:5], after[1]),
        (steps,),
        ins + [whole(e.shape) for e in extra[:2]] + [ANY] * 6,
        out_specs,
        outs,
        [],
        16,
        4.0,
        {6 + i: i for i in range(5)},
    )
    return (*again, results[5], results[7])


def attend(spanning, sc, own, following, after):
    slots = own.shape[0]
    args = ((own, following) if spanning else (own,)) + tuple(after)
    outs = [shape((slots, PAIR), BF)] + ([shape((PATCH, PAIR), BF)] if spanning else [])
    return call(
        functools.partial(attend_kernel, spanning, len(after)),
        sc,
        args,
        (1,),
        [whole((slots, PAIR))] + ([whole((PATCH, PAIR))] if spanning else []) + [ANY] * len(after),
        [whole(o.shape) for o in outs],
        outs,
        [
            pltpu.VMEM((PATCH, PAIR), BF),
            pltpu.VMEM((PATCH, PAIR), BF),
            pltpu.VMEM((PAIR, PATCH), BF),
            pltpu.VMEM((2, 2 * HEAD, PATCH), BF),
            pltpu.VMEM((8, BLOCK), F32),
            pltpu.VMEM((4, PATCH, BLOCK), F32),
            pltpu.VMEM((PATCH, 4 * BLOCK), BF),
            pltpu.VMEM((PATCH, 4 * BLOCK), BF),
            pltpu.VMEM((PAIR, 8 * BLOCK), BF),
            pltpu.VMEM((PATCH, PAIR), F32),
            pltpu.VMEM((PAIR, PATCH), F32),
            pltpu.VMEM((PATCH, PAIR), BF),
        ],
        24,
        7.5,
    )


def products(sc, ones, twos, gots, heads, wide, wg):
    slots = ones[0].shape[0]
    width = wide.shape[0]
    rows = 256
    half = width // 2 + 16
    last = PATCH // rows - 1
    down = pl.BlockSpec((rows, PAIR), lambda i, s: (i, 0))
    first = pl.BlockSpec((rows, PAIR), lambda i, s: (jnp.minimum(i, last), 0))
    across = pl.BlockSpec((half, rows), lambda i, s: (0, i))
    return call(
        product_kernel,
        sc,
        (*ones, *twos, *gots, *heads, wide, wg),
        (slots // rows,),
        [down] * 4 + [first] * 2 + [down] * 2 + [whole(wide.shape), whole(wg.shape)],
        [across, across, pl.BlockSpec((rows, LANES), lambda i, s: (i, 0))],
        [shape((half, slots), BF), shape((half, slots), BF), shape((slots, LANES), BF)],
        [pltpu.VMEM((width, LANES), BF)],
        16,
        4.0,
    )


def weights(sc, total, unit, dy, after):
    slots, width = unit.shape
    rows = 512
    down = lambda i, s: (i, 0)
    return call(
        weight_kernel,
        sc,
        (total, unit, dy, after),
        (slots // rows,),
        [
            pl.BlockSpec((rows, LANES), down),
            pl.BlockSpec((rows, width), down),
            pl.BlockSpec((rows, width), down),
            ANY,
        ],
        [whole((width, LANES))],
        [shape((width, LANES), BF)],
        [pltpu.VMEM((LANES, width), F32), pltpu.VMEM((LANES, width), F32)],
        16,
        4.0,
    )[0]


def pair_sum(sc, keep, got, after):
    total, slots = keep.shape
    cols = (total - 16) // 4 + 16
    rows = 512
    spec = pl.BlockSpec((total, rows), lambda i, s: (0, i))
    out = pl.BlockSpec((cols, rows), lambda i, s: (0, i))
    return call(
        pair_kernel,
        sc,
        (keep, got, after),
        (slots // rows,),
        [spec] * 2 + [ANY],
        [out] * 4,
        [shape((cols, slots), BF)] * 4,
        [],
        16,
        2.3,
    )


def finish(sc, parts, own, stat, gain, grads):
    cols, slots = own.shape
    cols //= 2
    weight_rows = grads.shape[1]
    rows = 512
    across = lambda i, s: (0, i)
    points, qkv, proj = call(
        finish_kernel,
        sc,
        (*parts, own, stat, gain, grads),
        (slots // rows,),
        [pl.BlockSpec((cols + 16, rows), across)] * 4
        + [
            pl.BlockSpec((2 * cols, rows), across),
            pl.BlockSpec((8, rows), across),
            whole(gain.shape),
            whole(grads.shape),
        ],
        [
            pl.BlockSpec((cols, rows), across),
            whole((weight_rows, 3 * GROUP)),
            whole((weight_rows, GROUP)),
        ],
        [
            shape((cols, slots), BF),
            shape((weight_rows, 3 * GROUP), F32),
            shape((weight_rows, GROUP), F32),
        ],
        [],
        16,
        2.3,
    )
    return points.T, qkv, proj.T


def spread_matrix():
    column = jnp.arange(3 * GROUP)
    target = (column // (3 * HEAD)) * GROUP + column % (3 * HEAD)
    return (target[:, None] == jnp.arange(LANES)[None, :]).astype(BF)


def on_device(points, cotangent, cell_counts, norm_gain, w_qkv, w_proj):
    slots, width = points.shape
    n_space = lax.axis_size("space")
    n_mp = lax.axis_size("mp")
    place = lax.axis_index("space")
    member = lax.axis_index("mp")
    live = jnp.sum(cell_counts, dtype=jnp.int32)
    states = [live.reshape(1)]
    step = 1
    while step < n_space:
        route = [(i, i + step) for i in range(n_space - step)]
        states.append(states[-1] + lax.ppermute(states[-1], "space", route))
        step *= 2
    start = states[-1][0] - live
    zero = jnp.zeros((), jnp.int32)
    where_i_am = jnp.stack([zero, zero, zero, zero, member, member % 2, member // 2, zero])
    gain = norm_gain.reshape(1, width)
    one, two, unit, own, stat, wide, wg = project(
        where_i_am, points, cotangent, gain, w_qkv.T, w_proj, spread_matrix(), states[:2]
    )
    head_len = (PATCH - start % PATCH) % PATCH
    tail_len = jnp.where(place == n_space - 1, 0, (PATCH - (start + live) % PATCH) % PATCH)
    n_patch = (live - head_len + PATCH - 1) // PATCH
    sc = jnp.stack(
        [head_len, live, n_patch, tail_len, member, member % 2, member // 2, zero]
    ).astype(jnp.int32)
    back = [(i + 1, i) for i in range(n_space - 1)]
    onward = [(i, i + 1) for i in range(n_space - 1)]
    at = jnp.minimum(start, 0)
    following = [
        lax.ppermute(lax.dynamic_slice(rows, (at, zero), (PATCH, PAIR)), "space", back)
        for rows in (one, two)
    ]
    local_a = attend(False, sc, one, None, [])[0]
    mine_a, spill_a = attend(True, sc, one, following[0], [local_a])
    got_a = lax.ppermute(spill_a, "space", onward)
    mine_b, spill_b = attend(True, sc, two, following[1], [mine_a])
    got_b = lax.ppermute(spill_b, "space", onward)
    local_b = attend(False, sc, two, None, [mine_b])[0]
    keep, send, total = products(
        sc, (mine_a, mine_b), (local_a, local_b), (got_a, got_b), (one, two), wide, wg
    )
    swap = [(i, i ^ 1) for i in range(n_mp)]
    other = lax.ppermute(send, "mp", swap)
    grads = weights(sc, total, unit, cotangent, keep)
    gathered = lax.all_to_all(
        grads.reshape(n_space, width // n_space, LANES), "space", 0, 0
    )
    parts = pair_sum(sc, keep, other, grads)
    received = [parts[0]]
    for d in range(1, n_mp // 2):
        route = [(i, (i + 2 * d) % n_mp) for i in range(n_mp)]
        received.append(lax.ppermute(parts[d], "mp", route))
    return finish(sc, received, own, stat, gain, gathered)


def solution(mesh):
    return jax.shard_map(
        on_device,
        mesh=mesh,
        in_specs=(
            P("space", None),
            P("space", None),
            P("space"),
            P(),
            P(None, "mp"),
            P("mp", None),
        ),
        out_specs=(P("space", "mp"), P("space", "mp"), P("mp", "space")),
        check_vma=False,
    )
```

time: 146 us -> 127 us (0.87)
  Pallas kernels: 73 us -> 49.9 us
  blocking collectives: 0 us -> 13.9 us
  waiting for transfers between devices: 12.4 us -> 0.86 us
    pallas_call x6 -> x10, Pallas kernels: 73 us -> 49.9 us  [call(): pl.pallas_call(kernel, grid_spec=pltpu.PrefetchScalarGridSpec(num_scalar_...]
    all_to_all x0 -> x1, blocking collectives: none -> 13.9 us  [on_device(): lax.all_to_all(grads.reshape(n_space, width // n_space, LANES), 'space',...]
    all_to_all x1 -> x0, waiting for transfers between devices: 8.53 us -> none  [on_device(): lax.all_to_all(grads.reshape(n_space, width // n_space, LANES), 'space',...]
    all_to_all x1 -> x0, starting transfers between devices: 6.28 us -> none  [on_device(): lax.all_to_all(grads.reshape(n_space, width // n_space, LANES), 'space',...]
    ppermute x3, starting transfers between devices: 5.65 us -> 11.3 us  [on_device(): received.append(lax.ppermute(parts[d], 'mp', route))]
    unnamed x11 -> x18, local copies, waits for them, and re-layouts: 3.92 us -> 6.97 us
    ppermute x1, waiting for transfers between devices: 2.96 us -> 0.07 us  [on_device(): other = lax.ppermute(send, 'mp', swap)]
    pallas_call x2 -> x0, local copies, waits for them, and re-layouts: 1.58 us -> none  [call(): pl.pallas_call(kernel, grid_spec=pltpu.PrefetchScalarGridSpec(num_scalar_...]
  transfers between devices with their start and end apart: 11 -> 12, of which waited for: 3 -> 2; matrix products, arithmetic and copies ran while one was open for 1% -> 1% of each run, Pallas kernels for 17% -> 34%
where the time goes in v2:
time: 127 us; the launch traced here: 124 us
  Pallas kernels  49.9 us (39%)
  starting transfers between devices  44.7 us (35%)
  blocking collectives  13.9 us (11%)
  local copies, waits for them, and re-layouts  7.95 us (6%)
  between operations  5.52 us (4%)
  other arithmetic  1.4 us (1%)
    pallas_call x10, Pallas kernels, call(): pl.pallas_call(kernel, grid_spec=pltpu.PrefetchScalarGridSpec(num_scalar_...  49.9 us
    ppermute x4, starting transfers between devices, on_device(): states.append(states[-1] + lax.ppermute(states[-1], 'space', route))  22.3 us
    all_to_all x1, blocking collectives, on_device(): lax.all_to_all(grads.reshape(n_space, width // n_space, LANES), 'space',...  13.9 us
    ppermute x3, starting transfers between devices, on_device(): received.append(lax.ppermute(parts[d], 'mp', route))  11.3 us
    unnamed x18, local copies, waits for them, and re-layouts  6.97 us
    ppermute x1, starting transfers between devices, on_device(): got_b = lax.ppermute(spill_b, 'space', onward)  5.59 us
    ppermute x1, starting transfers between devices, on_device(): got_a = lax.ppermute(spill_a, 'space', onward)  2.77 us
    ppermute x2, starting transfers between devices, on_device(): lax.ppermute(lax.dynamic_slice(rows, (at, zero), (PATCH, PAIR)), 'space',...  2.58 us
  transfers between devices with their start and end apart: 12, of which 2 were waited for; matrix products, arithmetic and copies ran while one was open for 1% of the time, Pallas kernels for 34%

profile of v2, /device:TPU:0, one launch (start us, length us, event | category | flops | bytes accessed | tf_op | source)
XLA Modules:
  0.0 124.2 jit_solution(230695576582570573)
XLA Ops:
  0.6 1.3 %reduce_sum.9 = s32[]{:T(128)} reduce(s32[128]{0:T(128)} %param.8, s32[]{:T(128)} %constant.84.clone.1), dimensions={0}, to_apply=%region_0.0 | reduce | flops 127 | bytes 520 | tf_op jit(solution)/shard_map/reduce_sum | solution.py:644
  1.9 4.1 %collective-permute-start = (s32[1]{0:T(128)}, s32[1]{0:T(128)}, u32[]{:S(2)}, u32[]{:S(2)}) collective-permute-start(s32[1]{0:T(128)} %bitcast.rest_3_), channel_id=1, source_target_pairs={{0,8},{8,16},{16,24},{24,32},{32,40},{40,48},{48,56},{56,64},{64,7... | collective-permute-start | bytes 20 | tf_op jit(solution)/shard_map/ppermute | solution.py:649
  6.1 0.1 fusion.rest_2_
  6.2 0.1 stack.35.sc_ref
  6.3 1.6 %copy-done = bf16[2048,512]{1,0:T(8,128)(2,1)S(1)} copy-done((bf16[2048,512]{1,0:T(8,128)(2,1)S(1)}, bf16[2048,512]{1,0:T(8,128)(2,1)}, u32[]{:S(2)}) %copy-start) | copy-done | bytes 2097176
  7.9 1.6 %copy-done.1 = bf16[2048,512]{1,0:T(8,128)(2,1)S(1)} copy-done((bf16[2048,512]{1,0:T(8,128)(2,1)S(1)}, bf16[2048,512]{1,0:T(8,128)(2,1)}, u32[]{:S(2)}) %copy-start.1) | copy-done | bytes 2097176
  9.5 0.9 copy-done.3
  10.4 0.8 copy-done.4
  11.3 0.7 copy-done.5
  11.9 4.0 %shard_map.85 = (bf16[2048,128]{1,0:T(8,128)(2,1)S(1)}, bf16[2048,128]{1,0:T(8,128)(2,1)S(1)}, bf16[2048,512]{1,0:T(8,128)(2,1)S(1)}, bf16[128,2048]{1,0:T(8,128...) custom-call(s32[8]{0:T(128)S(1)} %stack.35.sc_ref, ...), custom_call_target="tpu_custom_call" | custom-call | flops 4950000128 | tf_op jit(solution)/shard_map/pallas_call | solution.py:425
  15.9 0.0 collective-permute-done
  17.3 5.5 %collective-permute-start.1 = (s32[1]{0:T(128)}, s32[1]{0:T(128)}, u32[]{:S(2)}, u32[]{:S(2)}) collective-permute-start(s32[1]{0:T(128)} %add.62.rest_7_), channel_id=1, source_target_pairs={{0,16},{8,24},{16,32},{24,40},{32,48},{40,56},{48,64},{56,72},{64,... | collective-permute-start | bytes 20 | tf_op jit(solution)/shard_map/ppermute | solution.py:649
  22.8 2.7 %shard_map.86 = (bf16[2048,128]{1,0:T(8,128)(2,1)S(1)}, bf16[2048,128]{1,0:T(8,128)(2,1)S(1)}, bf16[2048,512]{1,0:T(8,128)(2,1)S(1)}, bf16[128,2048]{1,0:T(8,128)(2,1)S(1)}, f32[8,2048]{1,0:T(8,128)S(1)}) custom-call(s32[8]{0:T(128)S(1)} %stack.35.sc_ref, ...), custom_call_target="tpu_custom_call", output_to_operand_aliasing={{0}: (6, {}), {1}: (7, {}), {2}: (8, {}), {3}: (9, {}), {4}... | custom-call | flops 4400000000 | tf_op jit(solution)/shard_map/pallas_call | solution.py:425
  25.5 0.0 copy-start.7
  25.5 1.3 %copy-done.7 = bf16[2048,512]{1,0:T(8,128)(2,1)} copy-done((bf16[2048,512]{1,0:T(8,128)(2,1)}, bf16[2048,512]{1,0:T(8,128)(2,1)S(1)}, u32[]{:S(2)}) %copy-start.7) | copy-done | bytes 2097176
  27.5 5.1 %collective-permute-start.2 = (s32[1]{0:T(128)}, s32[1]{0:T(128)}, u32[]{:S(2)}, u32[]{:S(2)}) collective-permute-start(s32[1]{0:T(128)} %add.63), channel_id=1, source_target_pairs={{0,32},{8,40},{16,48},{24,56},{32,64},{40,72},{48,80},{56,88},{64,... | collective-permute-start | bytes 20 | tf_op jit(solution)/shard_map/ppermute | solution.py:649
  33.2 7.5 %collective-permute-start.3 = (s32[1]{0:T(128)}, s32[1]{0:T(128)}, u32[]{:S(2)}, u32[]{:S(2)}) collective-permute-start(s32[1]{0:T(128)} %add.64), channel_id=1, source_target_pairs={{0,64},{8,72},{16,80},{24,88},{32,96},{40,104},{48,112},{56,120},{... | collective-permute-start | bytes 20 | tf_op jit(solution)/shard_map/ppermute | solution.py:649
  42.7 0.1 constant_dynamic-slice_fusion.1
  42.8 0.1 constant_dynamic-slice_fusion
  42.9 1.3 %collective-permute-start.5 = (bf16[1024,128]{1,0:T(8,128)(2,1)S(1)}, bf16[1024,128]{1,0:T(8,128)(2,1)S(1)}, u32[]{:S(2)}, u32[]{:S(2)}) collective-permute-start(bf16[1024,128]{1,0:T(8,128)(2,1)S(1)} %constant_dynamic-slice_fusion), channel_id=1, source_target_pairs={{8,0},{16,8},{24,16},{32,24},{40,32},{48,40},{56,48},{64,56},{72,6... | collective-permute-start | bytes 786440 | tf_op jit(solution)/shard_map/ppermute | solution.py:668
  44.2 1.3 %collective-permute-start.4 = (bf16[1024,128]{1,0:T(8,128)(2,1)S(1)}, bf16[1024,128]{1,0:T(8,128)(2,1)S(1)}, u32[]{:S(2)}, u32[]{:S(2)}) collective-permute-start(bf16[1024,128]{1,0:T(8,128)(2,1)S(1)} %constant_dynamic-slice_fusion.1), channel_id=1, source_target_pairs={{8,0},{16,8},{24,16},{32,24},{40,32},{48,40},{56,48},{64,56},{72,6... | collective-permute-start | bytes 786440 | tf_op jit(solution)/shard_map/ppermute | solution.py:668
  45.5 0.7 stack.34.sc_ref
  46.3 8.1 %shard_map.87.rest_1_.c_ref = bf16[2048,128]{1,0:T(8,128)(2,1)S(1)} custom-call(s32[8]{0:T(128)S(1)} %stack.34.sc_ref, bf16[2048,128]{1,0:T(8,128)(2,1)S(1)} %get-tuple-element.37.own_ref.one_ref), custom_call_target="tpu_custom_call" | custom-call | flops 8249999872 | tf_op jit(solution)/shard_map/pallas_call | solution.py:425
  54.4 0.8 collective-permute-done.4.rest_0_
  55.2 8.3 %shard_map.88 = (bf16[2048,128]{1,0:T(8,128)(2,1)S(1)}, bf16[1024,128]{1,0:T(8,128)(2,1)S(1)}) custom-call(s32[8]{0:T(128)S(1)} %stack.34.sc_ref, bf16[2048,128]{1,0:T(8,128)(2,1)S(1)} %get-tuple-element.37.own_ref.one_ref, bf16[1024,128]{1,0:T(8,128)(2,1)S(1)} %collective-permute-done.4.rest_0_, bf16[2048,128]{1,0:T(8,128)(2,1)S(1)} %shard_map.87.rest_1_.c_ref), custom_call_target="tpu_custom_call" | custom-call | flops 8249999872 | tf_op jit(solution)/shard_map/pallas_call | solution.py:425
  63.5 2.8 %collective-permute-start.6 = (bf16[1024,128]{1,0:T(8,128)(2,1)S(1)}, bf16[1024,128]{1,0:T(8,128)(2,1)S(1)}, u32[]{:S(2)}, u32[]{:S(2)}) collective-permute-start(bf16[1024,128]{1,0:T(8,128)(2,1)S(1)} %get-tuple-element.41), channel_id=1, source_target_pairs={{0,8},{8,16},{16,24},{24,32},{32,40},{40,48},{48,56},{56,64},{64,7... | collective-permute-start | bytes 786440 | tf_op jit(solution)/shard_map/ppermute | solution.py:673
  66.3 0.0 collective-permute-done.5.rest_0_
  66.3 8.3 %shard_map.89 = (bf16[2048,128]{1,0:T(8,128)(2,1)S(1)}, bf16[1024,128]{1,0:T(8,128)(2,1)S(1)}) custom-call(s32[8]{0:T(128)S(1)} %stack.34.sc_ref, bf16[2048,128]{1,0:T(8,128)(2,1)S(1)} %get-tuple-element.39.own_ref.two_ref, bf16[1024,128]{1,0:T(8,128)(2,1)S(1)} %collective-permute-done.5.rest_0_, bf16[2048,128]{1,0:T(8,128)(2,1)S(1)} %get-tuple-element.38.rest_1_.a_ref), custom_call_target="tpu_custom_call" | custom-call | flops 8249999872 | tf_op jit(solution)/shard_map/pallas_call | solution.py:425
  74.6 5.6 %collective-permute-start.7 = (bf16[1024,128]{1,0:T(8,128)(2,1)S(1)}, bf16[1024,128]{1,0:T(8,128)(2,1)S(1)}, u32[]{:S(2)}, u32[]{:S(2)}) collective-permute-start(bf16[1024,128]{1,0:T(8,128)(2,1)S(1)} %get-tuple-element.42), channel_id=1, source_target_pairs={{0,8},{8,16},{16,24},{24,32},{32,40},{40,48},{48,56},{56,64},{64,7... | collective-permute-start | bytes 786440 | tf_op jit(solution)/shard_map/ppermute | solution.py:675
  80.2 8.2 %shard_map.90.d_ref = bf16[2048,128]{1,0:T(8,128)(2,1)S(1)} custom-call(s32[8]{0:T(128)S(1)} %stack.34.sc_ref, bf16[2048,128]{1,0:T(8,128)(2,1)S(1)} %get-tuple-element.39.own_ref.two_ref, bf16[2048,128]{1,0:T(8,128)(2,1)S(1)} %get-tuple-element.40.rest_0_.b_ref), custom_call_target="tpu_custom_call" | custom-call | flops 8249999872 | tf_op jit(solution)/shard_map/pallas_call | solution.py:425
  88.4 0.0 collective-permute-done.6.e_ref
  88.4 0.0 collective-permute-done.7.f_ref
  88.4 0.0 copy-start.2
  88.5 0.0 copy-start.8
  88.5 4.0 %shard_map.91 = (bf16[272,2048]{1,0:T(8,128)(2,1)S(1)}, bf16[272,2048]{1,0:T(8,128)(2,1)S(1)}, bf16[2048,256]{1,0:T(8,128)(2,1)S(1)}) custom-call(s32[8]{0:T(128)S(1)} %stack.34.sc_ref, bf16[2048,128]{1,0:T(8,128)(2,1)S(1)} %get-tuple-element.38.rest_1_.a_ref, bf16[2048,128]{1,0:T(8,128)(2,1)S(1)} %get-tuple-element.40.rest_0_.b_ref, ...), custom_call_target="tpu_custom_call" | custom-call | flops 4400000000 | tf_op jit(solution)/shard_map/pallas_call | solution.py:425
  92.4 0.1 collective-permute-start.8
  92.6 2.6 %shard_map.92.after_ref = bf16[512,256]{1,0:T(8,128)(2,1)S(1)} custom-call(s32[8]{0:T(128)S(1)} %stack.34.sc_ref, bf16[2048,256]{1,0:T(8,128)(2,1)S(1)} %get-tuple-element.46.total_ref, bf16[2048,512]{1,0:T(8,128)(2,1)S(1)} %copy-done.8, bf16[2048,512]{1,0:T(8,128)(2,1)S(1)} %copy-done.2, bf16[272,2048]{1,0:T(8,128)(2,1)S(1)} %get-tuple-element.44.after_ref.keep_ref), custom_call_target="tpu_custom_call" | custom-call | flops 4400000000 | tf_op jit(solution)/shard_map/pallas_call | solution.py:425
  95.2 0.0 copy-start.6
  95.2 0.1 collective-permute-done.8.got_ref
  95.3 1.2 shard_map.93
  96.5 7.2 %collective-permute-start.9 = (bf16[80,2048]{1,0:T(8,128)(2,1)S(1)}, bf16[80,2048]{1,0:T(8,128)(2,1)S(1)}, u32[]{:S(2)}, u32[]{:S(2)}) collective-permute-start(bf16[80,2048]{1,0:T(8,128)(2,1)S(1)} %get-tuple-element.49), channel_id=1, source_target_pairs={{0,2},{1,3},{2,4},{3,5},{4,6},{5,7},{6,0},{7,1},{8,10},{9,11},{10,... | collective-permute-start | bytes 983048 | tf_op jit(solution)/shard_map/ppermute | solution.py:690
  103.6 2.7 %collective-permute-start.10 = (bf16[80,2048]{1,0:T(8,128)(2,1)S(1)}, bf16[80,2048]{1,0:T(8,128)(2,1)S(1)}, u32[]{:S(2)}, u32[]{:S(2)}) collective-permute-start(bf16[80,2048]{1,0:T(8,128)(2,1)S(1)} %get-tuple-element.50), channel_id=1, source_target_pairs={{0,4},{1,5},{2,6},{3,7},{4,0},{5,1},{6,2},{7,3},{8,12},{9,13},{10,... | collective-permute-start | bytes 983048 | tf_op jit(solution)/shard_map/ppermute | solution.py:690
  106.4 1.4 %collective-permute-start.11 = (bf16[80,2048]{1,0:T(8,128)(2,1)S(1)}, bf16[80,2048]{1,0:T(8,128)(2,1)S(1)}, u32[]{:S(2)}, u32[]{:S(2)}) collective-permute-start(bf16[80,2048]{1,0:T(8,128)(2,1)S(1)} %get-tuple-element.51), channel_id=1, source_target_pairs={{0,6},{1,7},{2,0},{3,1},{4,2},{5,3},{6,4},{7,5},{8,14},{9,15},{10,... | collective-permute-start | bytes 983048 | tf_op jit(solution)/shard_map/ppermute | solution.py:690
  107.8 13.9 %all_to_all.5.grads_ref = bf16[16,32,256]{2,1,0:T(8,128)(2,1)S(1)} all-to-all(bf16[16,32,256]{2,1,0:T(8,128)(2,1)S(1)} %bitcast.13), channel_id=1, replica_groups=mesh['space'=16,'mp'=8] {'space'}, dimensions={0} | all-to-all | bytes 524288 | tf_op jit(solution)/shard_map/all_to_all | solution.py:683
  121.7 0.0 collective-permute-done.9.b_ref
  121.7 0.0 collective-permute-done.10.c_ref
  121.7 0.0 collective-permute-done.11.d_ref
  121.7 2.5 %shard_map.94 = (bf16[64,2048]{1,0:T(8,128)(2,1)}, f32[32,192]{1,0:T(8,128)}, f32[32,64]{1,0:T(8,128)}) custom-call(s32[8]{0:T(128)S(1)} %stack.34.sc_ref, bf16[80,2048]{1,0:T(8,128)(2,1)S(1)} %get-tuple-element.48.a_ref, bf16[80,2048]{1,0:T(8,128)(2,1)S(1)} %collective-permute-done.9.b_ref, bf16[80,2048]{1,0:T(8,128)(2,1)S(1)} %collective-permute-done.10.c_ref, ...), custom_call_target="tpu_custom_call" | custom-call | flops 2529999872 | tf_op jit(solution)/shard_map/pallas_call | solution.py:425
  (13 shorter events, 0.0 us)
Async XLA Ops:
  1.9 14.0 %collective-permute-start = (s32[1]{0:T(128)}, s32[1]{0:T(128)}, u32[]{:S(2)}, u32[]{:S(2)}) collective-permute-start(s32[1]{0:T(128)} %bitcast.rest_3_), channel_id=1, source_target_pairs={{0,8},{8,16},{16,24},{24,32},{32,40},{40,48},{48,56},{56,64},{64,7... | collective-permute-start | bytes 20 | tf_op jit(solution)/shard_map/ppermute | solution.py:649
  6.3 1.6 %copy-start = (bf16[2048,512]{1,0:T(8,128)(2,1)S(1)}, bf16[2048,512]{1,0:T(8,128)(2,1)}, u32[]{:S(2)}) copy-start(bf16[2048,512]{1,0:T(8,128)(2,1)} %x_ref.3) | copy-start | bytes 6291460
  7.9 1.6 %copy-start.1 = (bf16[2048,512]{1,0:T(8,128)(2,1)S(1)}, bf16[2048,512]{1,0:T(8,128)(2,1)}, u32[]{:S(2)}) copy-start(bf16[2048,512]{1,0:T(8,128)(2,1)} %dy_ref.5) | copy-start | bytes 6291460
  9.5 0.9 copy-start.3
  10.4 0.8 copy-start.4
  11.3 0.7 copy-start.5
  17.3 9.6 %collective-permute-start.1 = (s32[1]{0:T(128)}, s32[1]{0:T(128)}, u32[]{:S(2)}, u32[]{:S(2)}) collective-permute-start(s32[1]{0:T(128)} %add.62.rest_7_), channel_id=1, source_target_pairs={{0,16},{8,24},{16,32},{24,40},{32,48},{40,56},{48,64},{56,72},{64,... | collective-permute-start | bytes 20 | tf_op jit(solution)/shard_map/ppermute | solution.py:649
  25.5 1.3 %copy-start.7 = (bf16[2048,512]{1,0:T(8,128)(2,1)}, bf16[2048,512]{1,0:T(8,128)(2,1)S(1)}, u32[]{:S(2)}) copy-start(bf16[2048,512]{1,0:T(8,128)(2,1)S(1)} %get-tuple-element.47.unit_ref) | copy-start | bytes 6291460
  27.5 5.1 %collective-permute-start.2 = (s32[1]{0:T(128)}, s32[1]{0:T(128)}, u32[]{:S(2)}, u32[]{:S(2)}) collective-permute-start(s32[1]{0:T(128)} %add.63), channel_id=1, source_target_pairs={{0,32},{8,40},{16,48},{24,56},{32,64},{40,72},{48,80},{56,88},{64,... | collective-permute-start | bytes 20 | tf_op jit(solution)/shard_map/ppermute | solution.py:649
  33.2 7.5 %collective-permute-start.3 = (s32[1]{0:T(128)}, s32[1]{0:T(128)}, u32[]{:S(2)}, u32[]{:S(2)}) collective-permute-start(s32[1]{0:T(128)} %add.64), channel_id=1, source_target_pairs={{0,64},{8,72},{16,80},{24,88},{32,96},{40,104},{48,112},{56,120},{... | collective-permute-start | bytes 20 | tf_op jit(solution)/shard_map/ppermute | solution.py:649
  42.9 23.4 %collective-permute-start.5 = (bf16[1024,128]{1,0:T(8,128)(2,1)S(1)}, bf16[1024,128]{1,0:T(8,128)(2,1)S(1)}, u32[]{:S(2)}, u32[]{:S(2)}) collective-permute-start(bf16[1024,128]{1,0:T(8,128)(2,1)S(1)} %constant_dynamic-slice_fusion), channel_id=1, source_target_pairs={{8,0},{16,8},{24,16},{32,24},{40,32},{48,40},{56,48},{64,56},{72,6... | collective-permute-start | bytes 786440 | tf_op jit(solution)/shard_map/ppermute | solution.py:668
  44.2 11.0 %collective-permute-start.4 = (bf16[1024,128]{1,0:T(8,128)(2,1)S(1)}, bf16[1024,128]{1,0:T(8,128)(2,1)S(1)}, u32[]{:S(2)}, u32[]{:S(2)}) collective-permute-start(bf16[1024,128]{1,0:T(8,128)(2,1)S(1)} %constant_dynamic-slice_fusion.1), channel_id=1, source_target_pairs={{8,0},{16,8},{24,16},{32,24},{40,32},{48,40},{56,48},{64,56},{72,6... | collective-permute-start | bytes 786440 | tf_op jit(solution)/shard_map/ppermute | solution.py:668
  63.5 24.9 %collective-permute-start.6 = (bf16[1024,128]{1,0:T(8,128)(2,1)S(1)}, bf16[1024,128]{1,0:T(8,128)(2,1)S(1)}, u32[]{:S(2)}, u32[]{:S(2)}) collective-permute-start(bf16[1024,128]{1,0:T(8,128)(2,1)S(1)} %get-tuple-element.41), channel_id=1, source_target_pairs={{0,8},{8,16},{16,24},{24,32},{32,40},{40,48},{48,56},{56,64},{64,7... | collective-permute-start | bytes 786440 | tf_op jit(solution)/shard_map/ppermute | solution.py:673
  74.6 13.8 %collective-permute-start.7 = (bf16[1024,128]{1,0:T(8,128)(2,1)S(1)}, bf16[1024,128]{1,0:T(8,128)(2,1)S(1)}, u32[]{:S(2)}, u32[]{:S(2)}) collective-permute-start(bf16[1024,128]{1,0:T(8,128)(2,1)S(1)} %get-tuple-element.42), channel_id=1, source_target_pairs={{0,8},{8,16},{16,24},{24,32},{32,40},{40,48},{48,56},{56,64},{64,7... | collective-permute-start | bytes 786440 | tf_op jit(solution)/shard_map/ppermute | solution.py:675
  88.4 4.1 %copy-start.2 = (bf16[2048,512]{1,0:T(8,128)(2,1)S(1)}, bf16[2048,512]{1,0:T(8,128)(2,1)}, u32[]{:S(2)}) copy-start(bf16[2048,512]{1,0:T(8,128)(2,1)} %dy_ref.5) | copy-start | bytes 6291460
  88.5 4.1 %copy-start.8 = (bf16[2048,512]{1,0:T(8,128)(2,1)S(1)}, bf16[2048,512]{1,0:T(8,128)(2,1)}, u32[]{:S(2)}) copy-start(bf16[2048,512]{1,0:T(8,128)(2,1)} %copy-done.7) | copy-start | bytes 6291460
  92.4 2.8 %collective-permute-start.8 = (bf16[272,2048]{1,0:T(8,128)(2,1)S(1)}, bf16[272,2048]{1,0:T(8,128)(2,1)S(1)}, u32[]{:S(2)}, u32[]{:S(2)}) collective-permute-start(bf16[272,2048]{1,0:T(8,128)(2,1)S(1)} %get-tuple-element.45), channel_id=1, source_target_pairs={{0,1},{1,0},{2,3},{3,2},{4,5},{5,4},{6,7},{7,6},{8,9},{9,8},{10,11... | collective-permute-start | bytes 3342344 | tf_op jit(solution)/shard_map/ppermute | solution.py:681
  95.2 26.5 %copy-start.6 = (f32[512]{0:T(512)S(1)}, f32[512]{0:T(512)}, u32[]{:S(2)}) copy-start(f32[512]{0:T(512)} %param.9) | copy-start | bytes 6148
  96.5 25.2 %collective-permute-start.9 = (bf16[80,2048]{1,0:T(8,128)(2,1)S(1)}, bf16[80,2048]{1,0:T(8,128)(2,1)S(1)}, u32[]{:S(2)}, u32[]{:S(2)}) collective-permute-start(bf16[80,2048]{1,0:T(8,128)(2,1)S(1)} %get-tuple-element.49), channel_id=1, source_target_pairs={{0,2},{1,3},{2,4},{3,5},{4,6},{5,7},{6,0},{7,1},{8,10},{9,11},{10,... | collective-permute-start | bytes 983048 | tf_op jit(solution)/shard_map/ppermute | solution.py:690
  103.6 18.0 %collective-permute-start.10 = (bf16[80,2048]{1,0:T(8,128)(2,1)S(1)}, bf16[80,2048]{1,0:T(8,128)(2,1)S(1)}, u32[]{:S(2)}, u32[]{:S(2)}) collective-permute-start(bf16[80,2048]{1,0:T(8,128)(2,1)S(1)} %get-tuple-element.50), channel_id=1, source_target_pairs={{0,4},{1,5},{2,6},{3,7},{4,0},{5,1},{6,2},{7,3},{8,12},{9,13},{10,... | collective-permute-start | bytes 983048 | tf_op jit(solution)/shard_map/ppermute | solution.py:690
  106.4 15.3 %collective-permute-start.11 = (bf16[80,2048]{1,0:T(8,128)(2,1)S(1)}, bf16[80,2048]{1,0:T(8,128)(2,1)S(1)}, u32[]{:S(2)}, u32[]{:S(2)}) collective-permute-start(bf16[80,2048]{1,0:T(8,128)(2,1)S(1)} %get-tuple-element.51), channel_id=1, source_target_pairs={{0,6},{1,7},{2,0},{3,1},{4,2},{5,3},{6,4},{7,5},{8,14},{9,15},{10,... | collective-permute-start | bytes 983048 | tf_op jit(solution)/shard_map/ppermute | solution.py:690

commit v3 on v2

v3 whole, which is shorter than its diff:
```python
import functools

import jax
import jax.numpy as jnp
from jax import lax
from jax.experimental import pallas as pl
from jax.experimental.pallas import tpu as pltpu
from jax.sharding import PartitionSpec as P

H = 32
PATCH = 1024
EPS = 1e-05
MASKED = -1e30
HEAD = 16
GROUP = 64
LANES = 256
PAIR = 128
BLOCK = 256
SHIFT = 128
MIB = 1024 * 1024
FULL = 60.5
LOG2E = 1.4426950408889634
SAFE = 40.0

BF = jnp.bfloat16
F32 = jnp.float32
NT = (((1,), (1,)), ((), ()))
TN = (((0,), (0,)), ((), ()))


def dot(a, b):
    return jnp.dot(a, b, preferred_element_type=F32)


def dot_nt(a, b):
    return lax.dot_general(a, b, NT, preferred_element_type=F32)


def dot_tn(a, b):
    return lax.dot_general(a, b, TN, preferred_element_type=F32)


def iota(shape, axis):
    return lax.broadcasted_iota(jnp.int32, shape, axis)


def onehot(mask):
    return jnp.where(mask, 1.0, 0.0).astype(BF)


def split(value):
    high = value.astype(BF)
    return high, (value - high.astype(F32)).astype(BF)


def project_kernel(
    x_hbm, dy_hbm, gain_hbm, wqkv_hbm, wproj_hbm,
    one_hbm, two_hbm, unit_hbm, head_hbm, own_ref, stat_ref, wide_ref, wg_ref,
    x_ref, dy_ref, gain_ref, wqkv_ref, wproj_ref, side_ref, qkvu_ref, unit_ref,
    row_sems, sems, out_sems,
):
    slots, width = x_ref.shape
    cols = own_ref.shape[0] // 2
    chunks = slots // BLOCK

    def rows_copy(i, which):
        src, dst = ((x_hbm, x_ref), (dy_hbm, dy_ref))[which]
        at = pl.ds(pl.multiple_of(i * BLOCK, BLOCK), BLOCK)
        return pltpu.make_async_copy(src.at[at], dst.at[at], row_sems.at[which, i])

    def out_copy(i, which):
        at = pl.ds(pl.multiple_of(i * BLOCK, BLOCK), BLOCK)
        src, dst = (
            (qkvu_ref.at[at, :PAIR], one_hbm),
            (qkvu_ref.at[at, PAIR:], two_hbm),
            (unit_ref.at[at], unit_hbm),
            (qkvu_ref.at[at], head_hbm),
        )[which]
        return pltpu.make_async_copy(src, dst.at[at], out_sems.at[which, i])

    pairs = ((wqkv_hbm, wqkv_ref), (wproj_hbm, wproj_ref), (gain_hbm, gain_ref))
    small = [pltpu.make_async_copy(src, dst, sems.at[i]) for i, (src, dst) in enumerate(pairs)]
    for copy in small:
        copy.start()
    for i in range(chunks):
        rows_copy(i, 0).start()
        rows_copy(i, 1).start()
    row = iota((width, cols), 0)
    col = iota((width, cols), 1)
    pick = onehot(row == col + lax.axis_index("mp") * cols)
    none = jnp.zeros((width, cols), BF)
    side_ref[:, LANES:] = jnp.concatenate([none, pick, pick, none], axis=1)
    for copy in small:
        copy.wait()
    gain = gain_ref[...]
    col = iota((3 * GROUP, LANES), 0)
    lane = iota((3 * GROUP, LANES), 1)
    head = sum(jnp.where(col >= 3 * HEAD * h, HEAD, 0) for h in range(1, 4))
    wide = dot_tn(wqkv_ref[...], onehot(lane == col + head)).astype(BF)
    wide_ref[...] = wide
    part = iota((GROUP, LANES), 0)
    lane = iota((GROUP, LANES), 1)
    head = sum(jnp.where(part >= HEAD * h, GROUP - HEAD, 0) for h in range(1, 4))
    up = onehot(lane == part + head + 3 * HEAD)
    side_ref[:, :LANES] = dot_tn(wproj_ref[...], up).astype(BF)
    gain_high, gain_low = split(jnp.broadcast_to(gain, (16, width)))
    wg_high, wg_low = split(dot(gain_high, wide) + dot(gain_low, wide))
    row = iota((16, LANES), 0)
    wg_ref[...] = jnp.where(
        row == 0, wg_high.astype(F32), jnp.where(row == 1, wg_low.astype(F32), 0.0)
    ).astype(BF)

    for i in range(chunks):
        rows_copy(i, 0).wait()
        rows_copy(i, 1).wait()
        at = slice(i * BLOCK, (i + 1) * BLOCK)
        x_low = x_ref[at, :]
        x = x_low.astype(F32)
        mean = jnp.mean(x, axis=-1, keepdims=True)
        center = x - mean
        spread = lax.rsqrt(jnp.mean(center * center, axis=-1, keepdims=True) + EPS)
        unit = (center * spread * gain).astype(BF)
        unit_ref[at, :] = unit
        from_dy = dot(dy_ref[at, :], side_ref[:, : LANES + PAIR])
        qkvu_ref[at, :] = (dot(unit, wide_ref[...]) + from_dy[:, :LANES]).astype(BF)
        for which in range(4 if i < PATCH // BLOCK else 3):
            out_copy(i, which).start()
        own = dot(x_low, side_ref[:, LANES + PAIR :]) + from_dy[:, LANES:]
        own_ref[:, at] = own.T.astype(BF)
        both = jnp.where(iota((BLOCK, 128), 1) < 4, mean, spread)
        stat_ref[:, at] = both.T[:8, :]
    for i in range(chunks):
        for which in range(4 if i < PATCH // BLOCK else 3):
            out_copy(i, which).wait()


def place_in_row(counts_ref):
    place = lax.axis_index("space")
    n_space = counts_ref.shape[0]
    start = jnp.int32(0)
    for i in range(n_space):
        start = start + jnp.where(i < place, counts_ref[i, 0, 0], 0)
    count = counts_ref[place, 0, 0]
    head_len = (PATCH - start % PATCH) % PATCH
    tail_len = jnp.where(place == n_space - 1, 0, (PATCH - (start + count) % PATCH) % PATCH)
    n_patch = (count - head_len + PATCH - 1) // PATCH
    return count, head_len, tail_len, n_patch


MARGIN = 2 * SHIFT


def shifter(first):
    part = first & (SHIFT - 1)
    pick = onehot(iota((SHIFT, 2 * SHIFT), 1) == iota((SHIFT, 2 * SHIFT), 0) + part)

    def block(src_ref, start):
        rows = src_ref.shape[0]
        base = jnp.clip(first - part + start + MARGIN, 0, rows - MARGIN)
        return dot(pick, src_ref[pl.ds(pl.multiple_of(base, SHIFT), 2 * SHIFT), :])

    return block


def padded(dst_ref, src_ref, limit, at):
    rows, width = src_ref.shape
    cols = slice(at, at + width)
    none = jnp.zeros((MARGIN, width), BF)
    dst_ref[:MARGIN, cols] = none
    dst_ref[MARGIN + rows :, cols] = none
    kept = iota(src_ref.shape, 0) < limit
    dst_ref[MARGIN : MARGIN + rows, cols] = jnp.where(
        kept, src_ref[...].astype(F32), 0.0
    ).astype(BF)


def attend_kernel(spanning, pairs, counts_ref, *rest):
    own_refs = rest[:pairs]
    if spanning:
        next_ref = rest[pairs]
        out_ref, out_next_ref = rest[pairs + 2 : pairs + 4]
        rest = rest[pairs + 4 :]
    else:
        out_ref = rest[pairs + 1]
        rest = rest[pairs + 2 :]
    (x_ref, left_ref, flip_ref, value_ref, top_ref, exp_ref, low_ref, grad_ref, turn_ref,
     done_ref, own_pad_ref, next_pad_ref) = rest
    slots = own_refs[0].shape[0]
    lanes = pairs * PAIR
    count, head_len, tail_len, n_patch = place_in_row(counts_ref)
    scale = HEAD ** (-0.5)

    def work():
        first = head_len + (PATCH * (n_patch - 1) if spanning else 0)

        for p in range(pairs):
            padded(own_pad_ref, own_refs[p], count, p * PAIR)
        from_own = shifter(first)
        if spanning:
            padded(next_pad_ref, next_ref, tail_len, 0)
            from_next = shifter(first - count)
        for start in range(0, PATCH, SHIFT):
            piece = from_own(own_pad_ref, start)
            if spanning:
                piece = piece + from_next(next_pad_ref, start)
            x_ref[start : start + SHIFT, :] = piece.astype(BF)
        x = x_ref[...]
        src = iota((lanes, lanes), 0)
        dst = iota((lanes, lanes), 1)
        sub = dst & (GROUP - 1)
        keys = sub < 2 * HEAD
        move = onehot(
            ((sub < HEAD) & (src == dst + HEAD))
            | ((sub >= HEAD) & (sub < 3 * HEAD) & (src == dst))
        )
        lane = iota((PATCH, lanes), 1) & (GROUP - 1)
        fixed = jnp.where((lane > 3 * HEAD) & (lane < 3 * HEAD + 4), 1.0, 0.0)
        if spanning:
            valid = count - first + tail_len
            row = iota((PATCH, lanes), 0)
            fixed = jnp.where((lane == 3 * HEAD) & (row >= valid), MASKED, fixed)
        left_ref[...] = (dot(x, move) + fixed).astype(BF)
        flip = dot_nt(onehot(src == dst), x)
        flip_ref[...] = flip.astype(BF)
        square = flip * flip
        bounded = True
        for h in range(2 * pairs):
            at = h * GROUP
            value_ref[h, :HEAD, :] = flip_ref[at + 2 * HEAD : at + 3 * HEAD, :]
            value_ref[h, HEAD:, :] = jnp.ones((HEAD, PATCH), BF)
            most_q = jnp.max(jnp.sum(square[at : at + HEAD], axis=0))
            most_k = jnp.max(jnp.sum(square[at + HEAD : at + 2 * HEAD], axis=0))
            bounded &= most_q * most_k * scale * scale <= SAFE * SAFE
        turn_ref[...] = jnp.zeros_like(turn_ref)
        top_ref[...] = jnp.zeros_like(top_ref)
        row = iota((HEAD, BLOCK), 0)

        def placed(pieces, h):
            zero = jnp.zeros((GROUP, BLOCK), BF)
            group = jnp.concatenate(pieces, axis=0)
            return jnp.concatenate([group, zero] if h % 2 == 0 else [zero, group], axis=0)

        nothing = jnp.zeros((HEAD, BLOCK), BF)

        def score_right(h, here, top):
            query = flip_ref[h * GROUP : h * GROUP + HEAD, here].astype(F32) * (scale * LOG2E)
            high, low = split(query)
            if top is None:
                extra = jnp.where(row == 0, 1.0, 0.0)
            else:
                top_high = top.astype(BF).astype(F32)
                top_mid = (top - top_high).astype(BF).astype(F32)
                top_low = top - top_high - top_mid
                extra = jnp.where(
                    row == 0,
                    1.0,
                    jnp.where(
                        row == 1,
                        -top_high,
                        jnp.where(row == 2, -top_mid, jnp.where(row == 3, -top_low, 0.0)),
                    ),
                )
            return placed([high, low, nothing, extra.astype(BF)], h)

        def block(pair, step, carry):
            left = left_ref.at[:, pair * PAIR : (pair + 1) * PAIR]
            here = [
                pl.ds(pl.multiple_of((step * 2 + t // 2) * BLOCK, BLOCK), BLOCK) for t in range(4)
            ]

            @pl.when(jnp.logical_not(bounded))
            def _():
                for t in range(4):
                    scores = dot(left[...], score_right(pair * 2 + t % 2, here[t], None))
                    top_ref[t : t + 1, :] = jnp.max(scores, axis=0, keepdims=True)

            inverses = [None] * 4
            rights = [None] * 4
            spans = [
                slice((t % 2 * 2 + t // 2) * BLOCK, (t % 2 * 2 + t // 2 + 1) * BLOCK)
                for t in range(4)
            ]
            ups = [None] * 4
            queries = [None] * 4

            def stage_exp(t):
                scores = dot(left[...], score_right(pair * 2 + t % 2, here[t], top_ref[t : t + 1, :]))
                exps = jnp.exp2(scores)
                exp_ref[t] = exps
                low_ref[:, spans[t]] = exps.astype(BF)

            def stage_sum(t):
                at = (pair * 2 + t % 2) * GROUP
                result = dot(value_ref[pair * 2 + t % 2], low_ref[:, spans[t]])
                inverse = 1.0 / result[HEAD : HEAD + 1]
                inverses[t] = inverse
                attended = result[:HEAD] * inverse
                turn_ref[at + 3 * HEAD : at + 4 * HEAD, here[t]] = attended
                up = flip_ref[at + 3 * HEAD : at + 4 * HEAD, here[t]].astype(F32)
                scaled = up * scale
                delta = jnp.sum(scaled * attended, axis=0, keepdims=True)
                delta_high = delta.astype(BF).astype(F32)
                extra = jnp.where(
                    row == 1, -delta_high, jnp.where(row == 2, delta_high - delta, 0.0)
                ).astype(BF)
                rights[t] = placed([nothing, nothing, scaled.astype(BF), extra], t % 2)
                query = flip_ref[at : at + HEAD, here[t]].astype(F32)
                ups[t] = (up * inverse).astype(BF)
                queries[t] = (query * inverse).astype(BF)

            def stage_grad(t):
                dprob = dot(left[...], rights[t])
                grad_ref[:, spans[t]] = (exp_ref[t] * dprob).astype(BF)

            def stage_query(t):
                at = (pair * 2 + t % 2) * GROUP
                result = dot(flip_ref[at + HEAD : at + 2 * HEAD, :], grad_ref[:, spans[t]])
                turn_ref[at : at + HEAD, here[t]] = result * inverses[t]

            for stage in (stage_exp, stage_sum, stage_grad, stage_query):
                for t in range(4):
                    stage(t)
            for h in range(2):
                at = (pair * 2 + h) * GROUP
                both = slice(2 * h * BLOCK, 2 * (h + 1) * BLOCK)
                turn_ref[at + 2 * HEAD : at + 3 * HEAD, :] += dot_nt(
                    jnp.concatenate([ups[h], ups[h + 2]], axis=1), low_ref[:, both]
                )
                turn_ref[at + HEAD : at + 2 * HEAD, :] += dot_nt(
                    jnp.concatenate([queries[h], queries[h + 2]], axis=1), grad_ref[:, both]
                )
            return carry

        for pair in range(pairs):
            lax.fori_loop(0, PATCH // (2 * BLOCK), functools.partial(block, pair), 0)
        done_ref[:MARGIN, :] = jnp.zeros((MARGIN, lanes), BF)
        done_ref[MARGIN + PATCH :, :] = jnp.zeros((MARGIN, lanes), BF)
        done_ref[MARGIN : MARGIN + PATCH, :] = turn_ref[...].T.astype(BF)
        row = iota((SHIFT, lanes), 0)
        to_own = shifter(-first)
        for start in range(0, slots, SHIFT):
            piece = to_own(done_ref, start)
            out_ref[start : start + SHIFT, :] = jnp.where(
                row < count - start, piece, 0.0
            ).astype(BF)
        if spanning:
            to_next = shifter(count - first)
            for start in range(0, PATCH, SHIFT):
                piece = to_next(done_ref, start)
                out_next_ref[start : start + SHIFT, :] = jnp.where(
                    row < tail_len - start, piece, 0.0
                ).astype(BF)

    if spanning:
        work()
    else:
        pl.when(n_patch == 2)(work)

        @pl.when(n_patch < 2)
        def _():
            out_ref[...] = jnp.zeros_like(out_ref)


def product_kernel(
    mine_ref, a_ref, b_ref, got_ref, one_ref, two_ref, wide_ref, wg_ref,
    keep_ref, send_ref, total_ref, turned_ref,
):
    step = pl.program_id(0)
    rows = a_ref.shape[0]
    core = lax.axis_index("mp") % 2
    cols = wide_ref.shape[0] // 8

    @pl.when(step == 0)
    def _():
        for side in range(2):
            for x in range(4):
                from_row = pl.multiple_of((2 * x + (core ^ side)) * cols, cols)
                to_row = (side * 4 + x) * cols
                turned_ref[to_row : to_row + cols, :] = wide_ref[pl.ds(from_row, cols), :]

    got = jnp.where(step < PATCH // rows, got_ref[...].astype(F32), 0.0)
    local = jnp.concatenate([a_ref[...], b_ref[...]], axis=1)
    wide_total = mine_ref[...].astype(F32) + local.astype(F32) + got
    total = wide_total.astype(BF)
    total_ref[...] = total
    du = dot_nt(turned_ref[...], total).astype(BF)
    half = 4 * cols
    keep_ref[:half, :] = du[:half]
    send_ref[:half, :] = du[half:]
    lane = iota((rows, LANES), 1) & (GROUP - 1)
    qkvu = jnp.concatenate([one_ref[...], two_ref[...]], axis=1).astype(F32)
    product = jnp.where(lane < 3 * HEAD, wide_total * qkvu, 0.0)
    high, low = split(product)
    ones = jnp.ones((16, LANES), BF)
    second = (dot_nt(ones, high) + dot_nt(ones, low))[:1]
    first_rows = dot_nt(wg_ref[...], total)
    first = first_rows[:1] + first_rows[1:2]
    stats = pack_stats(first, second, rows)
    keep_ref[half:, :] = stats
    send_ref[half:, :] = stats


def weight_kernel(total_ref, unit_ref, dy_ref, after_ref, grads_ref, gu_ref, gy_ref):
    step = pl.program_id(0)

    @pl.when(step == 0)
    def _():
        gu_ref[...] = jnp.zeros_like(gu_ref)
        gy_ref[...] = jnp.zeros_like(gy_ref)

    total = total_ref[...]
    gu_ref[...] += dot_tn(total, unit_ref[...])
    gy_ref[...] += dot_tn(total, dy_ref[...])

    @pl.when(step == pl.num_programs(0) - 1)
    def _():
        row = iota(gu_ref.shape, 0) & (GROUP - 1)
        grads_ref[...] = jnp.where(row < 3 * HEAD, gu_ref[...], gy_ref[...]).T.astype(BF)


def pack_stats(first, second, rows):
    row = iota((16, rows), 0)
    first_high = first.astype(BF).astype(F32)
    second_high = second.astype(BF).astype(F32)
    return jnp.where(
        row == 0,
        first_high,
        jnp.where(
            row == 1,
            first - first_high,
            jnp.where(row == 2, second_high, jnp.where(row == 3, second - second_high, 0.0)),
        ),
    ).astype(BF)


def pair_kernel(keep_ref, got_ref, after_ref, out0_ref, out1_ref, out2_ref, out3_ref):
    x = lax.axis_index("mp") // 2
    rows = keep_ref.shape[1]
    half = keep_ref.shape[0] - 16
    cols = half // 4
    stats = keep_ref[half:, :].astype(F32) + got_ref[half:, :].astype(F32)
    packed = pack_stats(stats[0:1] + stats[1:2], stats[2:3] + stats[3:4], rows).astype(F32)
    folded = jnp.concatenate(
        [packed[i : i + 1, j : j + 128] for i in range(4) for j in range(0, rows, 128)], axis=0
    ).astype(BF)
    for d, out_ref in enumerate((out0_ref, out1_ref, out2_ref, out3_ref)):
        at = pl.ds(pl.multiple_of(((x + d) % 4) * cols, cols), cols)
        both = keep_ref[at, :].astype(F32) + got_ref[at, :].astype(F32)
        out_ref[:, :rows] = both.astype(BF)
        out_ref[:, rows:] = folded


def finish_kernel(
    counts_ref, a_ref, b_ref, c_ref, d_ref, own_ref, stat_ref, gain_ref, grads_ref,
    points_ref, qkv_ref, proj_ref,
):
    rows = a_ref.shape[1] - 128
    cols = own_ref.shape[0] // 2
    width = gain_ref.shape[1]
    parts = [ref[...].astype(F32) for ref in (a_ref, b_ref, c_ref, d_ref)]
    total = (parts[0] + parts[1]) + (parts[2] + parts[3])
    folded = total[:, rows:]
    total = total[:, :rows]
    each = rows // 128
    firsts = (folded[:each] + folded[each : 2 * each]) * (1.0 / width)
    seconds = (folded[2 * each : 3 * each] + folded[3 * each : 4 * each]) * (1.0 / width)
    first = jnp.concatenate([firsts[i : i + 1] for i in range(each)], axis=1)
    second = jnp.concatenate([seconds[i : i + 1] for i in range(each)], axis=1)
    mine = iota((cols, width), 1) == iota((cols, width), 0) + lax.axis_index("mp") * cols
    gain = jnp.sum(jnp.where(mine, gain_ref[...], 0.0), axis=1, keepdims=True)
    mean = stat_ref[0:1, :]
    spread = stat_ref[4:5, :]
    normed = (own_ref[:cols, :].astype(F32) - mean) * spread
    dnorm = spread * (total * gain - first - normed * second)
    out = own_ref[cols:, :].astype(F32) + dnorm
    slot = iota((cols, rows), 1)
    points_ref[...] = jnp.where(slot < counts_ref[lax.axis_index("space"), 0, 0], out, 0.0).astype(BF)

    grads = jnp.sum(grads_ref[...].astype(F32), axis=0)
    qkv_ref[...] = jnp.concatenate(
        [grads[:, h * GROUP : h * GROUP + 3 * HEAD] for h in range(4)], axis=1
    )
    proj_ref[...] = jnp.concatenate(
        [grads[:, h * GROUP + 3 * HEAD : (h + 1) * GROUP] for h in range(4)], axis=1
    )


def whole(shape):
    return pl.BlockSpec(shape, lambda *_: (0,) * len(shape))


ANY = pl.BlockSpec(memory_space=pl.ANY)
shape = jax.ShapeDtypeStruct


SMEM = pl.BlockSpec(memory_space=pltpu.SMEM)


def call(kernel, args, grid, in_specs, out_specs, out_shape, scratch, limit, micros, aliases={}):
    return pl.pallas_call(
        kernel,
        grid=grid,
        in_specs=in_specs,
        out_specs=out_specs,
        scratch_shapes=scratch,
        out_shape=out_shape,
        input_output_aliases=aliases,
        cost_estimate=pl.CostEstimate(
            flops=int(micros * 1.1e9), bytes_accessed=0, transcendentals=0
        ),
        compiler_params=pltpu.CompilerParams(vmem_limit_bytes=int(limit * MIB)),
    )(*args)


def project(points, cotangent, gain, w_qkv, w_proj):
    slots, width = points.shape
    cols = width // 8
    chunks = slots // BLOCK
    outs = [
        shape((slots, PAIR), BF),
        shape((slots, PAIR), BF),
        shape((slots, width), BF),
        shape((PATCH, LANES), BF),
        shape((2 * cols, slots), BF),
        shape((8, slots), F32),
        shape((width, LANES), BF),
        shape((16, LANES), BF),
    ]
    return call(
        project_kernel,
        (points, cotangent, gain, w_qkv, w_proj),
        (1,),
        [ANY] * 5,
        [ANY] * 4 + [whole(o.shape) for o in outs[4:]],
        outs,
        [
            pltpu.VMEM((slots, width), BF),
            pltpu.VMEM((slots, width), BF),
            pltpu.VMEM(gain.shape, F32),
            pltpu.VMEM(w_qkv.shape, BF),
            pltpu.VMEM(w_proj.shape, BF),
            pltpu.VMEM((width, LANES + 2 * PAIR), BF),
            pltpu.VMEM((slots, LANES), BF),
            pltpu.VMEM((slots, width), BF),
            pltpu.SemaphoreType.DMA((2, chunks)),
            pltpu.SemaphoreType.DMA((3,)),
            pltpu.SemaphoreType.DMA((4, chunks)),
        ],
        FULL,
        6.5,
    )


def count_kernel(cells_ref, out_ref):
    total = jnp.sum(cells_ref[...].astype(F32), axis=1, keepdims=True).astype(jnp.int32)
    out_ref[...] = jnp.broadcast_to(total.reshape(1, 1, 1), out_ref.shape)


def count(cells, n_space):
    out = shape((n_space, 1, 128), jnp.int32)
    cells = cells.reshape(1, -1)
    return call(
        count_kernel, (cells,), (1,), [whole(cells.shape)], whole(out.shape), out, [], 1, 0.5
    )


def attend(spanning, counts, owns, following, after):
    slots = owns[0].shape[0]
    pairs = len(owns)
    lanes = pairs * PAIR
    outs = [shape((slots, lanes), BF)] + ([shape((PATCH, lanes), BF)] if spanning else [])
    args = (*owns, following) if spanning else tuple(owns)
    return call(
        functools.partial(attend_kernel, spanning, pairs),
        (counts, *args, after),
        (1,),
        [SMEM] + [whole(a.shape) for a in args] + [ANY],
        [whole(o.shape) for o in outs],
        outs,
        [
            pltpu.VMEM((PATCH, lanes), BF),
            pltpu.VMEM((PATCH, lanes), BF),
            pltpu.VMEM((lanes, PATCH), BF),
            pltpu.VMEM((2 * pairs, 2 * HEAD, PATCH), BF),
            pltpu.VMEM((8, BLOCK), F32),
            pltpu.VMEM((4, PATCH, BLOCK), F32),
            pltpu.VMEM((PATCH, 4 * BLOCK), BF),
            pltpu.VMEM((PATCH, 4 * BLOCK), BF),
            pltpu.VMEM((lanes, PATCH), F32),
            pltpu.VMEM((PATCH + 2 * MARGIN, lanes), BF),
            pltpu.VMEM((slots + 2 * MARGIN, lanes), BF),
            pltpu.VMEM((PATCH + 2 * MARGIN, lanes), BF),
        ],
        24,
        7.5 * pairs,
    )


def products(mine, locals_, got, heads, wide, wg):
    slots = mine.shape[0]
    width = wide.shape[0]
    rows = 256
    half = width // 2 + 16
    last = PATCH // rows - 1
    down = pl.BlockSpec((rows, PAIR), lambda i: (i, 0))
    full = pl.BlockSpec((rows, LANES), lambda i: (i, 0))
    first = pl.BlockSpec((rows, LANES), lambda i: (jnp.minimum(i, last), 0))
    across = pl.BlockSpec((half, rows), lambda i: (0, i))
    return call(
        product_kernel,
        (mine, *locals_, got, *heads, wide, wg),
        (slots // rows,),
        [full, down, down, first, down, down] + [whole(wide.shape), whole(wg.shape)],
        [across, across, pl.BlockSpec((rows, LANES), lambda i: (i, 0))],
        [shape((half, slots), BF), shape((half, slots), BF), shape((slots, LANES), BF)],
        [pltpu.VMEM((width, LANES), BF)],
        24,
        4.0,
    )


def weights(total, unit, dy, after):
    slots, width = unit.shape
    rows = 512
    down = lambda i: (i, 0)
    return call(
        weight_kernel,
        (total, unit, dy, after),
        (slots // rows,),
        [
            pl.BlockSpec((rows, LANES), down),
            pl.BlockSpec((rows, width), down),
            pl.BlockSpec((rows, width), down),
            ANY,
        ],
        [whole((width, LANES))],
        [shape((width, LANES), BF)],
        [pltpu.VMEM((LANES, width), F32), pltpu.VMEM((LANES, width), F32)],
        24,
        4.0,
    )[0]


def pair_sum(keep, got, after):
    total, slots = keep.shape
    out = shape(((total - 16) // 4, slots + 128), BF)
    return call(
        pair_kernel,
        (keep, got, after),
        (1,),
        [whole(keep.shape)] * 2 + [ANY],
        [whole(out.shape)] * 4,
        [out] * 4,
        [],
        24,
        2.3,
    )


def finish(counts, parts, own, stat, gain, grads):
    cols, slots = own.shape
    rows = grads.shape[1]
    outs = [
        shape((cols // 2, slots), BF),
        shape((rows, 3 * GROUP), F32),
        shape((rows, GROUP), F32),
    ]
    args = (*parts, own, stat, gain, grads)
    points, qkv, proj = call(
        finish_kernel,
        (counts, *args),
        (1,),
        [SMEM] + [whole(a.shape) for a in args],
        [whole(o.shape) for o in outs],
        outs,
        [],
        24,
        2.3,
    )
    return points.T, qkv, proj.T


def on_device(points, cotangent, cell_counts, norm_gain, w_qkv, w_proj):
    slots, width = points.shape
    n_space = lax.axis_size("space")
    n_mp = lax.axis_size("mp")
    counts = lax.all_to_all(count(cell_counts, n_space), "space", 0, 0)
    gain = norm_gain.reshape(1, width)
    one, two, unit, head, own, stat, wide, wg = project(
        points, cotangent, gain, w_qkv.T, w_proj
    )
    back = [(i + 1, i) for i in range(n_space - 1)]
    onward = [(i, i + 1) for i in range(n_space - 1)]
    following = lax.ppermute(head, "space", back)
    local_a = attend(False, counts, (one,), None, wg)[0]
    mine, spill = attend(True, counts, (one, two), following, local_a)
    got = lax.ppermute(spill, "space", onward)
    local_b = attend(False, counts, (two,), None, mine)[0]
    keep, send, total = products(mine, (local_a, local_b), got, (one, two), wide, wg)
    swap = [(i, i ^ 1) for i in range(n_mp)]
    other = lax.ppermute(send, "mp", swap)
    grads = weights(total, unit, cotangent, keep)
    gathered = lax.all_to_all(
        grads.reshape(n_space, width // n_space, LANES), "space", 0, 0
    )
    parts = pair_sum(keep, other, grads)
    received = [parts[0]]
    for d in range(1, n_mp // 2):
        route = [(i, (i + 2 * d) % n_mp) for i in range(n_mp)]
        received.append(lax.ppermute(parts[d], "mp", route))
    return finish(counts, received, own, stat, gain, gathered)


def solution(mesh):
    return jax.shard_map(
        on_device,
        mesh=mesh,
        in_specs=(
            P("space", None),
            P("space", None),
            P("space"),
            P(),
            P(None, "mp"),
            P("mp", None),
        ),
        out_specs=(P("space", "mp"), P("space", "mp"), P("mp", "space")),
        check_vma=False,
    )
```

time: 127 us -> 97.4 us (0.77); the launches traced: 124 us -> 97.1 us
  starting transfers between devices: 44.7 us -> 19.6 us
  waiting for transfers between devices: 0.86 us -> 8.35 us
  local copies, waits for them, and re-layouts: 7.95 us -> 2.42 us
  between operations: 5.52 us -> 0.81 us
  blocking collectives: 13.9 us -> 18 us
  Pallas kernels: 49.9 us -> 47.9 us
  other arithmetic: 1.4 us -> 0 us
    ppermute x8 -> x2, starting transfers between devices: 33.2 us -> 4.87 us  [the longest x1 3.58 us: on_device(): got = lax.ppermute(spill, 'space', onward)]
    all_to_all x0 -> x1, starting transfers between devices: none -> 8.13 us  [on_device(): counts = lax.all_to_all(count(cell_counts, n_space), 'space', 0, 0)]
    ppermute x8 -> x2, waiting for transfers between devices: 0.78 us -> 8.05 us  [the longest x1 4.23 us: on_device(): following = lax.ppermute(head, 'space', back)]
    ppermute x3, starting transfers between devices: 11.3 us -> 6.16 us  [on_device(): received.append(lax.ppermute(parts[d], 'mp', route))]
    unnamed x18 -> x22, local copies, waits for them, and re-layouts: 6.97 us -> 2.42 us
    all_to_all x1, blocking collectives: 13.9 us -> 18 us  [on_device(): lax.all_to_all(grads.reshape(n_space, width // n_space, LANES), 'space',...]
    pallas_call x10 -> x9, Pallas kernels: 49.9 us -> 47.9 us  [call(): pl.pallas_call(kernel, grid=grid, in_specs=in_specs, out_specs=out_specs,...]
    reduce_sum x1 -> x0, other arithmetic: 1.29 us -> none  [on_device(): live = jnp.sum(cell_counts, dtype=jnp.int32)]
  transfers between devices with their start and end apart: 12 -> 7, of which waited for: 2 -> 3; matrix products, arithmetic and copies ran while one was open for 1% -> 0% of each run, Pallas kernels for 34% -> 28%
where the time goes in v3:
time: 97.4 us; the launch traced here: 97.1 us
  Pallas kernels  47.9 us (49%)
  starting transfers between devices  19.6 us (20%)
  blocking collectives  18 us (18%)
  waiting for transfers between devices  8.35 us (9%)
  local copies, waits for them, and re-layouts  2.42 us (2%)
    pallas_call x9, Pallas kernels, call(): pl.pallas_call(kernel, grid=grid, in_specs=in_specs, out_specs=out_specs,...  47.9 us
    all_to_all x1, blocking collectives, on_device(): lax.all_to_all(grads.reshape(n_space, width // n_space, LANES), 'space',...  18 us
    all_to_all x1, starting transfers between devices, on_device(): counts = lax.all_to_all(count(cell_counts, n_space), 'space', 0, 0)  8.13 us
    ppermute x3, starting transfers between devices, on_device(): received.append(lax.ppermute(parts[d], 'mp', route))  6.16 us
    ppermute x1, waiting for transfers between devices, on_device(): following = lax.ppermute(head, 'space', back)  4.23 us
    ppermute x1, waiting for transfers between devices, on_device(): got = lax.ppermute(spill, 'space', onward)  3.81 us
    ppermute x1, starting transfers between devices, on_device(): got = lax.ppermute(spill, 'space', onward)  3.58 us
    unnamed x22, local copies, waits for them, and re-layouts  2.42 us
  transfers between devices with their start and end apart: 7, of which 3 were waited for; matrix products, arithmetic and copies ran while one was open for 0% of the time, Pallas kernels for 28%

profile of v3, /device:TPU:0, one launch (start us, length us, event | category | flops | bytes accessed | tf_op | source)
XLA Modules:
  0.0 97.1 jit_solution(4369264858259186327)
XLA Ops:
  0.6 0.0 copy-start.2
  0.6 0.6 copy-done.2
  1.3 0.7 shard_map.85
  2.0 8.1 %all-to-all-start = ((s32[16,1,128]{2,1,0:T(1,128)}), s32[16,1,128]{2,1,0:T(1,128)S(1)}, u32[]{:S(2)}, u32[]{:S(2)}) async-start(s32[16,1,128]{2,1,0:T(1,128)} %shard_map.85), calls=%async_computation | async-start | bytes 16384 | tf_op jit(solution)/shard_map/all_to_all | solution.py:687
  10.1 8.7 %shard_map.86 = (bf16[2048,128]{1,0:T(8,128)(2,1)}, bf16[2048,128]{1,0:T(8,128)(2,1)}, bf16[2048,512]{1,0:T(8,128)(2,1)}, bf16[1024,256]{1,0:T(8,128)(2,1)}, bf1...) custom-call(bf16[2048,512]{1,0:T(8,128)(2,1)} %x_hbm.1, ...), custom_call_target="tpu_custom_call" | custom-call | flops 7150000128 | tf_op jit(solution)/shard_map/pallas_call | solution.py:500
  18.8 1.3 %collective-permute-start = (bf16[1024,256]{1,0:T(8,128)(2,1)}, bf16[1024,256]{1,0:T(8,128)(2,1)S(1)}, u32[]{:S(2)}, u32[]{:S(2)}) collective-permute-start(bf16[1024,256]{1,0:T(8,128)(2,1)} %get-tuple-element.25), channel_id=1, source_target_pairs={{8,0},{16,8},{24,16},{32,24},{40,32},{48,40},{56,48},{64,56},{72,6... | collective-permute-start | bytes 1572872 | tf_op jit(solution)/shard_map/ppermute | solution.py:694
  20.1 0.0 all-to-all-done.counts_ref
  20.1 0.0 copy-start.5
  20.1 1.0 %copy-done.5 = bf16[2048,128]{1,0:T(8,128)(2,1)S(1)} copy-done((bf16[2048,128]{1,0:T(8,128)(2,1)S(1)}, bf16[2048,128]{1,0:T(8,128)(2,1)}, u32[]{:S(2)}) %copy-start.5) | copy-done | bytes 524312
  21.1 0.0 copy-start.10
  21.1 0.7 copy-done.10
  21.8 0.0 copy-start.7
  21.8 8.2 %shard_map.87.rest_3_.a_ref = bf16[2048,128]{1,0:T(8,128)(2,1)S(1)} custom-call(s32[16,1,128]{2,1,0:T(1,128)S(1)} %all-to-all-done.counts_ref, bf16[2048,128]{1,0:T(8,128)(2,1)S(1)} %copy-done.5, bf16[16,256]{1,0:T(8,128)(2,1)S(1)} %copy-done.10), custom_call_target="tpu_custom_call" | custom-call | flops 8249999872 | tf_op jit(solution)/shard_map/pallas_call | solution.py:500
  30.0 4.2 %collective-permute-done.rest_2_ = bf16[1024,256]{1,0:T(8,128)(2,1)S(1)} collective-permute-done((bf16[1024,256]{1,0:T(8,128)(2,1)}, bf16[1024,256]{1,0:T(8,128)(2,1)S(1)}, u32[]{:S(2)}, u32[]{:S(2)}) %collective-permute-start) | collective-permute-done | bytes 524320 | tf_op jit(solution)/shard_map/ppermute | solution.py:694
  34.3 0.0 copy-done.7
  34.3 14.6 %shard_map.88 = (bf16[2048,256]{1,0:T(8,128)(2,1)S(1)}, bf16[1024,256]{1,0:T(8,128)(2,1)S(1)}) custom-call(s32[16,1,128]{2,1,0:T(1,128)S(1)} %all-to-all-done.counts_ref, bf16[2048,128]{1,0:T(8,128)(2,1)S(1)} %copy-done.5, bf16[2048,128]{1,0:T(8,128)(2,1)S(1)} %copy-done.7, bf16[1024,256]{1,0:T(8,128)(2,1)S(1)} %collective-permute-done.rest_2_, ...), custom_call_target="tpu_custom_call" | custom-call | flops 16499999744 | tf_op jit(solution)/shard_map/pallas_call | solution.py:500
  48.8 3.6 %collective-permute-start.1 = (bf16[1024,256]{1,0:T(8,128)(2,1)S(1)}, bf16[1024,256]{1,0:T(8,128)(2,1)S(1)}, u32[]{:S(2)}, u32[]{:S(2)}) collective-permute-start(bf16[1024,256]{1,0:T(8,128)(2,1)S(1)} %get-tuple-element.28), channel_id=1, source_target_pairs={{0,8},{8,16},{16,24},{24,32},{32,40},{40,48},{48,56},{56,64},{64,7... | collective-permute-start | bytes 1572872 | tf_op jit(solution)/shard_map/ppermute | solution.py:697
  52.4 0.0 copy-start.6
  52.4 0.0 copy-start.8
  52.5 8.2 %shard_map.89.b_ref = bf16[2048,128]{1,0:T(8,128)(2,1)S(1)} custom-call(s32[16,1,128]{2,1,0:T(1,128)S(1)} %all-to-all-done.counts_ref, bf16[2048,128]{1,0:T(8,128)(2,1)S(1)} %copy-done.7, bf16[2048,256]{1,0:T(8,128)(2,1)S(1)} %get-tuple-element.27.rest_1_.mine_ref), custom_call_target="tpu_custom_call" | custom-call | flops 8249999872 | tf_op jit(solution)/shard_map/pallas_call | solution.py:500
  60.7 3.8 %collective-permute-done.1.got_ref = bf16[1024,256]{1,0:T(8,128)(2,1)S(1)} collective-permute-done((bf16[1024,256]{1,0:T(8,128)(2,1)S(1)}, bf16[1024,256]{1,0:T(8,128)(2,1)S(1)}, u32[]{:S(2)}, u32[]{:S(2)}) %collective-permute-start.1) | collective-permute-done | bytes 524320 | tf_op jit(solution)/shard_map/ppermute | solution.py:697
  64.5 0.0 copy-done.6
  64.5 0.0 copy-done.8
  64.5 0.0 copy-start
  64.5 0.0 copy-start.3
  64.5 3.4 %shard_map.90 = (bf16[272,2048]{1,0:T(8,128)(2,1)S(1)}, bf16[272,2048]{1,0:T(8,128)(2,1)S(1)}, bf16[2048,256]{1,0:T(8,128)(2,1)S(1)}) custom-call(bf16[2048,256]{1,0:T(8,128)(2,1)S(1)} %get-tuple-element.27.rest_1_.mine_ref, bf16[2048,128]{1,0:T(8,128)(2,1)S(1)} %shard_map.87.rest_3_.a_ref, bf16[2048,128]{1,0:T(8,128)(2,1)S(1)} %shard_map.89.b_ref, ...), custom_call_target="tpu_custom_call" | custom-call | flops 4400000000 | tf_op jit(solution)/shard_map/pallas_call | solution.py:500
  68.0 0.4 collective-permute-start.2
  68.4 0.0 copy-done
  68.4 0.0 copy-done.3
  68.4 2.1 %shard_map.91.after_ref = bf16[512,256]{1,0:T(8,128)(2,1)S(1)} custom-call(bf16[2048,256]{1,0:T(8,128)(2,1)S(1)} %get-tuple-element.32.total_ref, bf16[2048,512]{1,0:T(8,128)(2,1)S(1)} %copy-done.3, bf16[2048,512]{1,0:T(8,128)(2,1)S(1)} %copy-done, bf16[272,2048]{1,0:T(8,128)(2,1)S(1)} %get-tuple-element.30.after_ref.keep_ref), custom_call_target="tpu_custom_call" | custom-call | flops 4400000000 | tf_op jit(solution)/shard_map/pallas_call | solution.py:500
  70.5 0.0 copy-start.1
  70.5 0.0 copy-start.4
  70.5 0.0 copy-start.9
  70.5 0.3 collective-permute-done.2.got_ref
  70.8 0.3 shard_map.92
  71.1 2.0 %collective-permute-start.3 = (bf16[64,2176]{1,0:T(8,128)(2,1)S(1)}, bf16[64,2176]{1,0:T(8,128)(2,1)S(1)}, u32[]{:S(2)}, u32[]{:S(2)}) collective-permute-start(bf16[64,2176]{1,0:T(8,128)(2,1)S(1)} %get-tuple-element.35), channel_id=1, source_target_pairs={{0,2},{1,3},{2,4},{3,5},{4,6},{5,7},{6,0},{7,1},{8,10},{9,11},{10,... | collective-permute-start | bytes 835592 | tf_op jit(solution)/shard_map/ppermute | solution.py:710
  73.1 2.7 %collective-permute-start.4 = (bf16[64,2176]{1,0:T(8,128)(2,1)S(1)}, bf16[64,2176]{1,0:T(8,128)(2,1)S(1)}, u32[]{:S(2)}, u32[]{:S(2)}) collective-permute-start(bf16[64,2176]{1,0:T(8,128)(2,1)S(1)} %get-tuple-element.36), channel_id=1, source_target_pairs={{0,4},{1,5},{2,6},{3,7},{4,0},{5,1},{6,2},{7,3},{8,12},{9,13},{10,... | collective-permute-start | bytes 835592 | tf_op jit(solution)/shard_map/ppermute | solution.py:710
  75.8 1.4 %collective-permute-start.5 = (bf16[64,2176]{1,0:T(8,128)(2,1)S(1)}, bf16[64,2176]{1,0:T(8,128)(2,1)S(1)}, u32[]{:S(2)}, u32[]{:S(2)}) collective-permute-start(bf16[64,2176]{1,0:T(8,128)(2,1)S(1)} %get-tuple-element.37), channel_id=1, source_target_pairs={{0,6},{1,7},{2,0},{3,1},{4,2},{5,3},{6,4},{7,5},{8,14},{9,15},{10,... | collective-permute-start | bytes 835592 | tf_op jit(solution)/shard_map/ppermute | solution.py:710
  77.3 18.0 %all_to_all.10.grads_ref = bf16[16,32,256]{2,1,0:T(8,128)(2,1)S(1)} all-to-all(bf16[16,32,256]{2,1,0:T(8,128)(2,1)S(1)} %bitcast.6), channel_id=1, replica_groups=mesh['space'=16,'mp'=8] {'space'}, dimensions={0} | all-to-all | bytes 524288 | tf_op jit(solution)/shard_map/all_to_all | solution.py:703
  95.2 0.0 collective-permute-done.3.b_ref
  95.2 0.0 collective-permute-done.4.c_ref
  95.2 0.0 collective-permute-done.5.d_ref
  95.3 0.0 copy-done.1
  95.3 0.0 copy-done.4
  95.3 0.0 copy-done.9
  95.3 1.8 %shard_map.93 = (bf16[64,2048]{1,0:T(8,128)(2,1)}, f32[32,192]{1,0:T(8,128)}, f32[32,64]{1,0:T(8,128)}) custom-call(s32[16,1,128]{2,1,0:T(1,128)S(1)} %all-to-all-done.counts_ref, bf16[64,2176]{1,0:T(8,128)(2,1)S(1)} %get-tuple-element.34.a_ref, bf16[64,2176]{1,0:T(8,128)(2,1)S(1)} %collective-permute-done.3.b_ref, ...), custom_call_target="tpu_custom_call" | custom-call | flops 2529999872 | tf_op jit(solution)/shard_map/pallas_call | solution.py:500
Async XLA Ops:
  0.6 0.7 copy-start.2
  2.0 18.1 %all-to-all-start = ((s32[16,1,128]{2,1,0:T(1,128)}), s32[16,1,128]{2,1,0:T(1,128)S(1)}, u32[]{:S(2)}, u32[]{:S(2)}) async-start(s32[16,1,128]{2,1,0:T(1,128)} %shard_map.85), calls=%async_computation | async-start | bytes 16384 | tf_op jit(solution)/shard_map/all_to_all | solution.py:687
  18.8 15.5 %collective-permute-start = (bf16[1024,256]{1,0:T(8,128)(2,1)}, bf16[1024,256]{1,0:T(8,128)(2,1)S(1)}, u32[]{:S(2)}, u32[]{:S(2)}) collective-permute-start(bf16[1024,256]{1,0:T(8,128)(2,1)} %get-tuple-element.25), channel_id=1, source_target_pairs={{8,0},{16,8},{24,16},{32,24},{40,32},{48,40},{56,48},{64,56},{72,6... | collective-permute-start | bytes 1572872 | tf_op jit(solution)/shard_map/ppermute | solution.py:694
  20.1 1.0 %copy-start.5 = (bf16[2048,128]{1,0:T(8,128)(2,1)S(1)}, bf16[2048,128]{1,0:T(8,128)(2,1)}, u32[]{:S(2)}) copy-start(bf16[2048,128]{1,0:T(8,128)(2,1)} %get-tuple-element.23.rest_0_.one_ref) | copy-start | bytes 1572868
  21.1 0.7 copy-start.10
  21.8 12.4 %copy-start.7 = (bf16[2048,128]{1,0:T(8,128)(2,1)S(1)}, bf16[2048,128]{1,0:T(8,128)(2,1)}, u32[]{:S(2)}) copy-start(bf16[2048,128]{1,0:T(8,128)(2,1)} %get-tuple-element.24.rest_1_.rest_0_.two_ref) | copy-start | bytes 1572868
  48.8 15.7 %collective-permute-start.1 = (bf16[1024,256]{1,0:T(8,128)(2,1)S(1)}, bf16[1024,256]{1,0:T(8,128)(2,1)S(1)}, u32[]{:S(2)}, u32[]{:S(2)}) collective-permute-start(bf16[1024,256]{1,0:T(8,128)(2,1)S(1)} %get-tuple-element.28), channel_id=1, source_target_pairs={{0,8},{8,16},{16,24},{24,32},{32,40},{40,48},{48,56},{56,64},{64,7... | collective-permute-start | bytes 1572872 | tf_op jit(solution)/shard_map/ppermute | solution.py:697
  52.4 12.1 %copy-start.6 = (bf16[2048,128]{1,0:T(8,128)(2,1)S(1)}, bf16[2048,128]{1,0:T(8,128)(2,1)}, u32[]{:S(2)}) copy-start(bf16[2048,128]{1,0:T(8,128)(2,1)} %get-tuple-element.23.rest_0_.one_ref) | copy-start | bytes 1572868
  52.4 12.1 %copy-start.8 = (bf16[512,256]{1,0:T(8,128)(2,1)S(1)}, bf16[512,256]{1,0:T(8,128)(2,1)}, u32[]{:S(2)}) copy-start(bf16[512,256]{1,0:T(8,128)(2,1)} %get-tuple-element.29.wide_ref) | copy-start | bytes 786436
  64.5 3.9 %copy-start = (bf16[2048,512]{1,0:T(8,128)(2,1)S(1)}, bf16[2048,512]{1,0:T(8,128)(2,1)}, u32[]{:S(2)}) copy-start(bf16[2048,512]{1,0:T(8,128)(2,1)} %dy_ref.1) | copy-start | bytes 6291460
  64.5 3.9 %copy-start.3 = (bf16[2048,512]{1,0:T(8,128)(2,1)S(1)}, bf16[2048,512]{1,0:T(8,128)(2,1)}, u32[]{:S(2)}) copy-start(bf16[2048,512]{1,0:T(8,128)(2,1)} %get-tuple-element.33.unit_ref) | copy-start | bytes 6291460
  68.0 2.8 %collective-permute-start.2 = (bf16[272,2048]{1,0:T(8,128)(2,1)S(1)}, bf16[272,2048]{1,0:T(8,128)(2,1)S(1)}, u32[]{:S(2)}, u32[]{:S(2)}) collective-permute-start(bf16[272,2048]{1,0:T(8,128)(2,1)S(1)} %get-tuple-element.31), channel_id=1, source_target_pairs={{0,1},{1,0},{2,3},{3,2},{4,5},{5,4},{6,7},{7,6},{8,9},{9,8},{10,11... | collective-permute-start | bytes 3342344 | tf_op jit(solution)/shard_map/ppermute | solution.py:701
  70.5 24.8 %copy-start.1 = (f32[512]{0:T(512)S(1)}, f32[512]{0:T(512)}, u32[]{:S(2)}) copy-start(f32[512]{0:T(512)} %param.9) | copy-start | bytes 6148
  70.5 24.8 %copy-start.4 = (bf16[128,2048]{1,0:T(8,128)(2,1)S(1)}, bf16[128,2048]{1,0:T(8,128)(2,1)}, u32[]{:S(2)}) copy-start(bf16[128,2048]{1,0:T(8,128)(2,1)} %get-tuple-element.38.own_ref) | copy-start | bytes 1572868
  70.5 24.8 %copy-start.9 = (f32[8,2048]{1,0:T(8,128)S(1)}, f32[8,2048]{1,0:T(8,128)}, u32[]{:S(2)}) copy-start(f32[8,2048]{1,0:T(8,128)} %get-tuple-element.39.stat_ref) | copy-start | bytes 196612
  71.1 24.2 %collective-permute-start.3 = (bf16[64,2176]{1,0:T(8,128)(2,1)S(1)}, bf16[64,2176]{1,0:T(8,128)(2,1)S(1)}, u32[]{:S(2)}, u32[]{:S(2)}) collective-permute-start(bf16[64,2176]{1,0:T(8,128)(2,1)S(1)} %get-tuple-element.35), channel_id=1, source_target_pairs={{0,2},{1,3},{2,4},{3,5},{4,6},{5,7},{6,0},{7,1},{8,10},{9,11},{10,... | collective-permute-start | bytes 835592 | tf_op jit(solution)/shard_map/ppermute | solution.py:710
  73.1 22.2 %collective-permute-start.4 = (bf16[64,2176]{1,0:T(8,128)(2,1)S(1)}, bf16[64,2176]{1,0:T(8,128)(2,1)S(1)}, u32[]{:S(2)}, u32[]{:S(2)}) collective-permute-start(bf16[64,2176]{1,0:T(8,128)(2,1)S(1)} %get-tuple-element.36), channel_id=1, source_target_pairs={{0,4},{1,5},{2,6},{3,7},{4,0},{5,1},{6,2},{7,3},{8,12},{9,13},{10,... | collective-permute-start | bytes 835592 | tf_op jit(solution)/shard_map/ppermute | solution.py:710
  75.8 19.4 %collective-permute-start.5 = (bf16[64,2176]{1,0:T(8,128)(2,1)S(1)}, bf16[64,2176]{1,0:T(8,128)(2,1)S(1)}, u32[]{:S(2)}, u32[]{:S(2)}) collective-permute-start(bf16[64,2176]{1,0:T(8,128)(2,1)S(1)} %get-tuple-element.37), channel_id=1, source_target_pairs={{0,6},{1,7},{2,0},{3,1},{4,2},{5,3},{6,4},{7,5},{8,14},{9,15},{10,... | collective-permute-start | bytes 835592 | tf_op jit(solution)/shard_map/ppermute | solution.py:710

commit v4 on v3

--- a/solution.py
+++ b/solution.py
@@ -17,6 +17,7 @@
 PAIR = 128
 BLOCK = 256
 SHIFT = 128
+CHUNK = 512
 MIB = 1024 * 1024
 FULL = 60.5
 LOG2E = 1.4426950408889634
@@ -53,67 +54,90 @@
     return high, (value - high.astype(F32)).astype(BF)
 
 
-def project_kernel(
-    x_hbm, dy_hbm, gain_hbm, wqkv_hbm, wproj_hbm,
-    one_hbm, two_hbm, unit_hbm, head_hbm, own_ref, stat_ref, wide_ref, wg_ref,
-    x_ref, dy_ref, gain_ref, wqkv_ref, wproj_ref, side_ref, qkvu_ref, unit_ref,
-    row_sems, sems, out_sems,
-):
-    slots, width = x_ref.shape
+def project_kernel(lead, x_hbm, dy_hbm, gain_hbm, *rest):
+    if lead:
+        wqkv_hbm, wproj_hbm = rest[:2]
+        one_hbm, two_hbm, unit_hbm, own_hbm, stat_hbm, head_hbm = rest[2:8]
+        wide_ref, side_ref, wg_ref = rest[8:11]
+        wqkv_ref, wproj_ref = rest[11:13]
+        rest = rest[13:]
+        pairs = ((wqkv_hbm, wqkv_ref), (wproj_hbm, wproj_ref))
+    else:
+        wide_hbm, side_hbm = rest[:2]
+        one_hbm, two_hbm, unit_hbm, own_hbm, stat_hbm = rest[8:13]
+        wide_ref, side_ref = rest[13:15]
+        rest = rest[15:]
+        pairs = ((wide_hbm, wide_ref), (side_hbm, side_ref))
+    x_ref, dy_ref, gain_ref, qkvu_ref, unit_ref, own_ref, stat_ref, row_sems, sems, out_sems = rest
+    half, width = x_ref.shape
     cols = own_ref.shape[0] // 2
-    chunks = slots // BLOCK
+    chunks = half // CHUNK
+    base = 0 if lead else half
 
     def rows_copy(i, which):
         src, dst = ((x_hbm, x_ref), (dy_hbm, dy_ref))[which]
-        at = pl.ds(pl.multiple_of(i * BLOCK, BLOCK), BLOCK)
-        return pltpu.make_async_copy(src.at[at], dst.at[at], row_sems.at[which, i])
+        return pltpu.make_async_copy(
+            src.at[pl.ds(base + i * CHUNK, CHUNK)],
+            dst.at[pl.ds(i * CHUNK, CHUNK)],
+            row_sems.at[which, i],
+        )
 
     def out_copy(i, which):
-        at = pl.ds(pl.multiple_of(i * BLOCK, BLOCK), BLOCK)
-        src, dst = (
-            (qkvu_ref.at[at, :PAIR], one_hbm),
-            (qkvu_ref.at[at, PAIR:], two_hbm),
-            (unit_ref.at[at], unit_hbm),
-            (qkvu_ref.at[at], head_hbm),
-        )[which]
-        return pltpu.make_async_copy(src, dst.at[at], out_sems.at[which, i])
-
-    pairs = ((wqkv_hbm, wqkv_ref), (wproj_hbm, wproj_ref), (gain_hbm, gain_ref))
+        at = pl.ds(i * CHUNK, CHUNK)
+        to = pl.ds(base + i * CHUNK, CHUNK)
+        if which == 0:
+            src, dst = qkvu_ref.at[at, :PAIR], one_hbm.at[to]
+        elif which == 1:
+            src, dst = qkvu_ref.at[at, PAIR:], two_hbm.at[to]
+        elif which == 2:
+            src, dst = unit_ref.at[at], unit_hbm.at[to]
+        elif which == 3:
+            src, dst = own_ref.at[:, at], own_hbm.at[:, to]
+        elif which == 4:
+            src, dst = stat_ref.at[:, at], stat_hbm.at[:, to]
+        else:
+            src, dst = qkvu_ref.at[at], head_hbm.at[to]
+        return pltpu.make_async_copy(src, dst, out_sems.at[which, i])
+
+    pairs = (*pairs, (gain_hbm, gain_ref))
     small = [pltpu.make_async_copy(src, dst, sems.at[i]) for i, (src, dst) in enumerate(pairs)]
     for copy in small:
         copy.start()
     for i in range(chunks):
         rows_copy(i, 0).start()
         rows_copy(i, 1).start()
-    row = iota((width, cols), 0)
-    col = iota((width, cols), 1)
-    pick = onehot(row == col + lax.axis_index("mp") * cols)
-    none = jnp.zeros((width, cols), BF)
-    side_ref[:, LANES:] = jnp.concatenate([none, pick, pick, none], axis=1)
+    if lead:
+        row = iota((width, cols), 0)
+        col = iota((width, cols), 1)
+        pick = onehot(row == col + lax.axis_index("mp") * cols)
+        none = jnp.zeros((width, cols), BF)
+        side_ref[:, LANES:] = jnp.concatenate([none, pick, pick, none], axis=1)
     for copy in small:
         copy.wait()
     gain = gain_ref[...]
-    col = iota((3 * GROUP, LANES), 0)
-    lane = iota((3 * GROUP, LANES), 1)
-    head = sum(jnp.where(col >= 3 * HEAD * h, HEAD, 0) for h in range(1, 4))
-    wide = dot_tn(wqkv_ref[...], onehot(lane == col + head)).astype(BF)
-    wide_ref[...] = wide
-    part = iota((GROUP, LANES), 0)
-    lane = iota((GROUP, LANES), 1)
-    head = sum(jnp.where(part >= HEAD * h, GROUP - HEAD, 0) for h in range(1, 4))
-    up = onehot(lane == part + head + 3 * HEAD)
-    side_ref[:, :LANES] = dot_tn(wproj_ref[...], up).astype(BF)
-    gain_high, gain_low = split(jnp.broadcast_to(gain, (16, width)))
-    wg_high, wg_low = split(dot(gain_high, wide) + dot(gain_low, wide))
-    row = iota((16, LANES), 0)
-    wg_ref[...] = jnp.where(
-        row == 0, wg_high.astype(F32), jnp.where(row == 1, wg_low.astype(F32), 0.0)
-    ).astype(BF)
-
+    if lead:
+        col = iota((3 * GROUP, LANES), 0)
+        lane = iota((3 * GROUP, LANES), 1)
+        head = sum(jnp.where(col >= 3 * HEAD * h, HEAD, 0) for h in range(1, 4))
+        wide = dot_tn(wqkv_ref[...], onehot(lane == col + head)).astype(BF)
+        wide_ref[...] = wide
+        part = iota((GROUP, LANES), 0)
+        lane = iota((GROUP, LANES), 1)
+        head = sum(jnp.where(part >= HEAD * h, GROUP - HEAD, 0) for h in range(1, 4))
+        up = onehot(lane == part + head + 3 * HEAD)
+        side_ref[:, :LANES] = dot_tn(wproj_ref[...], up).astype(BF)
+        gain_high, gain_low = split(jnp.broadcast_to(gain, (16, width)))
+        wg_high, wg_low = split(dot(gain_high, wide) + dot(gain_low, wide))
+        row = iota((16, LANES), 0)
+        wg_ref[...] = jnp.where(
+            row == 0, wg_high.astype(F32), jnp.where(row == 1, wg_low.astype(F32), 0.0)
+        ).astype(BF)
+
+    copies = []
     for i in range(chunks):
         rows_copy(i, 0).wait()
         rows_copy(i, 1).wait()
-        at = slice(i * BLOCK, (i + 1) * BLOCK)
+        at = slice(i * CHUNK, (i + 1) * CHUNK)
         x_low = x_ref[at, :]
         x = x_low.astype(F32)
         mean = jnp.mean(x, axis=-1, keepdims=True)
@@ -123,15 +147,15 @@
         unit_ref[at, :] = unit
         from_dy = dot(dy_ref[at, :], side_ref[:, : LANES + PAIR])
         qkvu_ref[at, :] = (dot(unit, wide_ref[...]) + from_dy[:, :LANES]).astype(BF)
-        for which in range(4 if i < PATCH // BLOCK else 3):
-            out_copy(i, which).start()
         own = dot(x_low, side_ref[:, LANES + PAIR :]) + from_dy[:, LANES:]
         own_ref[:, at] = own.T.astype(BF)
-        both = jnp.where(iota((BLOCK, 128), 1) < 4, mean, spread)
+        both = jnp.where(iota((CHUNK, 128), 1) < 4, mean, spread)
         stat_ref[:, at] = both.T[:8, :]
-    for i in range(chunks):
-        for which in range(4 if i < PATCH // BLOCK else 3):
-            out_copy(i, which).wait()
+        for which in range(6 if lead else 5):
+            copies.append(out_copy(i, which))
+            copies[-1].start()
+    for copy in copies:
+        copy.wait()
 
 
 def place_in_row(counts_ref):
@@ -515,40 +539,54 @@
 def project(points, cotangent, gain, w_qkv, w_proj):
     slots, width = points.shape
     cols = width // 8
-    chunks = slots // BLOCK
+    half = slots // 2
+    chunks = half // CHUNK
     outs = [
         shape((slots, PAIR), BF),
         shape((slots, PAIR), BF),
         shape((slots, width), BF),
-        shape((PATCH, LANES), BF),
         shape((2 * cols, slots), BF),
         shape((8, slots), F32),
-        shape((width, LANES), BF),
-        shape((16, LANES), BF),
     ]
-    return call(
-        project_kernel,
+    head = shape((half, LANES), BF)
+    extra = [shape((width, LANES), BF), shape((width, LANES + 2 * PAIR), BF), shape((16, LANES), BF)]
+    scratch = [
+        pltpu.VMEM((half, width), BF),
+        pltpu.VMEM((half, width), BF),
+        pltpu.VMEM(gain.shape, F32),
+        pltpu.VMEM((half, LANES), BF),
+        pltpu.VMEM((half, width), BF),
+        pltpu.VMEM((2 * cols, half), BF),
+        pltpu.VMEM((8, half), F32),
+        pltpu.SemaphoreType.DMA((2, chunks)),
+        pltpu.SemaphoreType.DMA((3,)),
+        pltpu.SemaphoreType.DMA((6, chunks)),
+    ]
+    results = call(
+        functools.partial(project_kernel, True),
         (points, cotangent, gain, w_qkv, w_proj),
         (1,),
         [ANY] * 5,
-        [ANY] * 4 + [whole(o.shape) for o in outs[4:]],
+        [ANY] * 6 + [whole(e.shape) for e in extra],
+        outs + [head] + extra,
+        [pltpu.VMEM(w_qkv.shape, BF), pltpu.VMEM(w_proj.shape, BF)] + scratch,
+        FULL,
+        4.5,
+    )
+    head, wide, side, wg = results[5:]
+    again = call(
+        functools.partial(project_kernel, False),
+        (points, cotangent, gain, wide, side, *results[:5], head),
+        (1,),
+        [ANY] * 11,
+        [ANY] * 5,
         outs,
-        [
-            pltpu.VMEM((slots, width), BF),
-            pltpu.VMEM((slots, width), BF),
-            pltpu.VMEM(gain.shape, F32),
-            pltpu.VMEM(w_qkv.shape, BF),
-            pltpu.VMEM(w_proj.shape, BF),
-            pltpu.VMEM((width, LANES + 2 * PAIR), BF),
-            pltpu.VMEM((slots, LANES), BF),
-            pltpu.VMEM((slots, width), BF),
-            pltpu.SemaphoreType.DMA((2, chunks)),
-            pltpu.SemaphoreType.DMA((3,)),
-            pltpu.SemaphoreType.DMA((4, chunks)),
-        ],
+        [pltpu.VMEM(e.shape, BF) for e in extra[:2]] + scratch,
         FULL,
-        6.5,
-    )
+        3.0,
+        {5 + i: i for i in range(5)},
+    )
+    return (*again, head, wide, wg)
 
 
 def count_kernel(cells_ref, out_ref):
@@ -686,13 +724,13 @@
     n_mp = lax.axis_size("mp")
     counts = lax.all_to_all(count(cell_counts, n_space), "space", 0, 0)
     gain = norm_gain.reshape(1, width)
-    one, two, unit, head, own, stat, wide, wg = project(
+    one, two, unit, own, stat, head, wide, wg = project(
         points, cotangent, gain, w_qkv.T, w_proj
     )
     back = [(i + 1, i) for i in range(n_space - 1)]
     onward = [(i, i + 1) for i in range(n_space - 1)]
     following = lax.ppermute(head, "space", back)
-    local_a = attend(False, counts, (one,), None, wg)[0]
+    local_a = attend(False, counts, (one,), None, one)[0]
     mine, spill = attend(True, counts, (one, two), following, local_a)
     got = lax.ppermute(spill, "space", onward)
     local_b = attend(False, counts, (two,), None, mine)[0]

time: 97.4 us -> 96 us (0.986)
  waiting for transfers between devices: 8.35 us -> 4.88 us
  blocking collectives: 18 us -> 20.8 us
    ppermute x1, waiting for transfers between devices: 4.23 us -> 0.76 us  [on_device(): following = lax.ppermute(head, 'space', back)]
    all_to_all x1, blocking collectives: 18 us -> 20.8 us  [on_device(): lax.all_to_all(grads.reshape(n_space, width // n_space, LANES), 'space',...]
    pallas_call x9 -> x10, Pallas kernels: 47.9 us -> 48.8 us  [call(): pl.pallas_call(kernel, grid=grid, in_specs=in_specs, out_specs=out_specs,...]
  transfers between devices with their start and end apart: 7 -> 7, of which waited for: 3 -> 3; matrix products, arithmetic and copies ran while one was open for 0% -> 0% of each run, Pallas kernels for 28% -> 29%
where the time goes in v4:
time: 96 us; the launch traced here: 96.6 us
  Pallas kernels  48.8 us (51%)
  blocking collectives  20.8 us (22%)
  starting transfers between devices  19.6 us (20%)
  waiting for transfers between devices  4.88 us (5%)
  local copies, waits for them, and re-layouts  1.73 us (2%)
    pallas_call x10, Pallas kernels, call(): pl.pallas_call(kernel, grid=grid, in_specs=in_specs, out_specs=out_specs,...  48.8 us
    all_to_all x1, blocking collectives, on_device(): lax.all_to_all(grads.reshape(n_space, width // n_space, LANES), 'space',...  20.8 us
    all_to_all x1, starting transfers between devices, on_device(): counts = lax.all_to_all(count(cell_counts, n_space), 'space', 0, 0)  8.13 us
    ppermute x3, starting transfers between devices, on_device(): received.append(lax.ppermute(parts[d], 'mp', route))  6.19 us
    ppermute x1, waiting for transfers between devices, on_device(): got = lax.ppermute(spill, 'space', onward)  3.79 us
    ppermute x1, starting transfers between devices, on_device(): got = lax.ppermute(spill, 'space', onward)  3.59 us
  transfers between devices with their start and end apart: 7, of which 3 were waited for; matrix products, arithmetic and copies ran while one was open for 0% of the time, Pallas kernels for 29%

profile of v4, /device:TPU:0, one launch (start us, length us, event | category | flops | bytes accessed | tf_op | source)
XLA Modules:
  0.0 96.6 jit_solution(15048015306158164994)
XLA Ops:
  0.6 0.0 copy-start.2
  0.6 0.6 copy-done.2
  1.3 0.7 shard_map.85
  2.0 8.1 %all-to-all-start = ((s32[16,1,128]{2,1,0:T(1,128)}), s32[16,1,128]{2,1,0:T(1,128)S(1)}, u32[]{:S(2)}, u32[]{:S(2)}) async-start(s32[16,1,128]{2,1,0:T(1,128)} %shard_map.85), calls=%async_computation | async-start | bytes 16384 | tf_op jit(solution)/shard_map/all_to_all | solution.py:725
  10.1 5.4 %shard_map.86 = (bf16[2048,128]{1,0:T(8,128)(2,1)}, bf16[2048,128]{1,0:T(8,128)(2,1)}, bf16[2048,512]{1,0:T(8,128)(2,1)}, bf16[128,2048]{1,0:T(8,128)(2,1)}, f32...) custom-call(bf16[2048,512]{1,0:T(8,128)(2,1)} %x_hbm.3, ...), custom_call_target="tpu_custom_call" | custom-call | flops 4950000128 | tf_op jit(solution)/shard_map/pallas_call | solution.py:524
  15.5 1.3 %collective-permute-start = (bf16[1024,256]{1,0:T(8,128)(2,1)}, bf16[1024,256]{1,0:T(8,128)(2,1)S(1)}, u32[]{:S(2)}, u32[]{:S(2)}) collective-permute-start(bf16[1024,256]{1,0:T(8,128)(2,1)} %get-tuple-element.36.rest_7_), channel_id=1, source_target_pairs={{8,0},{16,8},{24,16},{32,24},{40,32},{48,40},{56,48},{64,56},{72,6... | collective-permute-start | bytes 1572872 | tf_op jit(solution)/shard_map/ppermute | solution.py:732
  16.8 4.2 %shard_map.87 = (bf16[2048,128]{1,0:T(8,128)(2,1)}, bf16[2048,128]{1,0:T(8,128)(2,1)}, bf16[2048,512]{1,0:T(8,128)(2,1)}, bf16[128,2048]{1,0:T(8,128)(2,1)}, f32[8,2048]{1,0:T(8,128)}) custom-call(bf16[2048,512]{1,0:T(8,128)(2,1)} %x_hbm.3, bf16[2048,512]{1,0:T(8,128)(2,1)} %dy_ref.1, ...), custom_call_target="tpu_custom_call", output_to_operand_aliasing={{0}: (5, {}), {1}: (6, {}), {2}: (7, {}), {3}: (8, {}), {4}... | custom-call | flops 3300000000 | tf_op jit(solution)/shard_map/pallas_call | solution.py:524
  21.0 0.0 all-to-all-done.counts_ref
  21.0 0.0 copy-start.4
  21.0 1.0 %copy-done.4 = bf16[2048,128]{1,0:T(8,128)(2,1)S(1)} copy-done((bf16[2048,128]{1,0:T(8,128)(2,1)S(1)}, bf16[2048,128]{1,0:T(8,128)(2,1)}, u32[]{:S(2)}) %copy-start.4) | copy-done | bytes 524312
  22.0 0.0 copy-start.6
  22.0 8.2 %shard_map.88.rest_3_.a_ref = bf16[2048,128]{1,0:T(8,128)(2,1)S(1)} custom-call(s32[16,1,128]{2,1,0:T(1,128)S(1)} %all-to-all-done.counts_ref, bf16[2048,128]{1,0:T(8,128)(2,1)S(1)} %copy-done.4, bf16[2048,128]{1,0:T(8,128)(2,1)S(1)} %copy-done.4), custom_call_target="tpu_custom_call" | custom-call | flops 8249999872 | tf_op jit(solution)/shard_map/pallas_call | solution.py:524
  30.2 0.8 collective-permute-done.rest_2_
  31.0 0.0 copy-done.6
  31.0 14.6 %shard_map.89 = (bf16[2048,256]{1,0:T(8,128)(2,1)S(1)}, bf16[1024,256]{1,0:T(8,128)(2,1)S(1)}) custom-call(s32[16,1,128]{2,1,0:T(1,128)S(1)} %all-to-all-done.counts_ref, bf16[2048,128]{1,0:T(8,128)(2,1)S(1)} %copy-done.4, bf16[2048,128]{1,0:T(8,128)(2,1)S(1)} %copy-done.6, bf16[1024,256]{1,0:T(8,128)(2,1)S(1)} %collective-permute-done.rest_2_, ...), custom_call_target="tpu_custom_call" | custom-call | flops 16499999744 | tf_op jit(solution)/shard_map/pallas_call | solution.py:524
  45.5 3.6 %collective-permute-start.1 = (bf16[1024,256]{1,0:T(8,128)(2,1)S(1)}, bf16[1024,256]{1,0:T(8,128)(2,1)S(1)}, u32[]{:S(2)}, u32[]{:S(2)}) collective-permute-start(bf16[1024,256]{1,0:T(8,128)(2,1)S(1)} %get-tuple-element.40), channel_id=1, source_target_pairs={{0,8},{8,16},{16,24},{24,32},{32,40},{40,48},{48,56},{56,64},{64,7... | collective-permute-start | bytes 1572872 | tf_op jit(solution)/shard_map/ppermute | solution.py:735
  49.1 0.0 copy-start.5
  49.1 0.0 copy-start.8
  49.2 0.0 copy-start.10
  49.2 8.2 %shard_map.90.b_ref = bf16[2048,128]{1,0:T(8,128)(2,1)S(1)} custom-call(s32[16,1,128]{2,1,0:T(1,128)S(1)} %all-to-all-done.counts_ref, bf16[2048,128]{1,0:T(8,128)(2,1)S(1)} %copy-done.6, bf16[2048,256]{1,0:T(8,128)(2,1)S(1)} %get-tuple-element.39.rest_1_.mine_ref), custom_call_target="tpu_custom_call" | custom-call | flops 8249999872 | tf_op jit(solution)/shard_map/pallas_call | solution.py:524
  57.4 3.8 %collective-permute-done.1.got_ref = bf16[1024,256]{1,0:T(8,128)(2,1)S(1)} collective-permute-done((bf16[1024,256]{1,0:T(8,128)(2,1)S(1)}, bf16[1024,256]{1,0:T(8,128)(2,1)S(1)}, u32[]{:S(2)}, u32[]{:S(2)}) %collective-permute-start.1) | collective-permute-done | bytes 524320 | tf_op jit(solution)/shard_map/ppermute | solution.py:735
  61.2 0.0 copy-done.5
  61.2 0.0 copy-done.8
  61.2 0.0 copy-done.10
  61.2 0.0 copy-start
  61.2 0.0 copy-start.3
  61.2 3.4 %shard_map.91 = (bf16[272,2048]{1,0:T(8,128)(2,1)S(1)}, bf16[272,2048]{1,0:T(8,128)(2,1)S(1)}, bf16[2048,256]{1,0:T(8,128)(2,1)S(1)}) custom-call(bf16[2048,256]{1,0:T(8,128)(2,1)S(1)} %get-tuple-element.39.rest_1_.mine_ref, bf16[2048,128]{1,0:T(8,128)(2,1)S(1)} %shard_map.88.rest_3_.a_ref, bf16[2048,128]{1,0:T(8,128)(2,1)S(1)} %shard_map.90.b_ref, ...), custom_call_target="tpu_custom_call" | custom-call | flops 4400000000 | tf_op jit(solution)/shard_map/pallas_call | solution.py:524
  64.7 0.4 collective-permute-start.2
  65.1 0.0 copy-done
  65.1 0.0 copy-done.3
  65.1 2.1 %shard_map.92.after_ref = bf16[512,256]{1,0:T(8,128)(2,1)S(1)} custom-call(bf16[2048,256]{1,0:T(8,128)(2,1)S(1)} %get-tuple-element.44.total_ref, bf16[2048,512]{1,0:T(8,128)(2,1)S(1)} %copy-done.3, bf16[2048,512]{1,0:T(8,128)(2,1)S(1)} %copy-done, bf16[272,2048]{1,0:T(8,128)(2,1)S(1)} %get-tuple-element.42.after_ref.keep_ref), custom_call_target="tpu_custom_call" | custom-call | flops 4400000000 | tf_op jit(solution)/shard_map/pallas_call | solution.py:524
  67.1 0.0 copy-start.1
  67.2 0.0 copy-start.7
  67.2 0.0 copy-start.9
  67.2 0.3 collective-permute-done.2.got_ref
  67.5 0.3 shard_map.93
  67.8 2.0 %collective-permute-start.3 = (bf16[64,2176]{1,0:T(8,128)(2,1)S(1)}, bf16[64,2176]{1,0:T(8,128)(2,1)S(1)}, u32[]{:S(2)}, u32[]{:S(2)}) collective-permute-start(bf16[64,2176]{1,0:T(8,128)(2,1)S(1)} %get-tuple-element.47), channel_id=1, source_target_pairs={{0,2},{1,3},{2,4},{3,5},{4,6},{5,7},{6,0},{7,1},{8,10},{9,11},{10,... | collective-permute-start | bytes 835592 | tf_op jit(solution)/shard_map/ppermute | solution.py:748
  69.8 2.7 %collective-permute-start.4 = (bf16[64,2176]{1,0:T(8,128)(2,1)S(1)}, bf16[64,2176]{1,0:T(8,128)(2,1)S(1)}, u32[]{:S(2)}, u32[]{:S(2)}) collective-permute-start(bf16[64,2176]{1,0:T(8,128)(2,1)S(1)} %get-tuple-element.48), channel_id=1, source_target_pairs={{0,4},{1,5},{2,6},{3,7},{4,0},{5,1},{6,2},{7,3},{8,12},{9,13},{10,... | collective-permute-start | bytes 835592 | tf_op jit(solution)/shard_map/ppermute | solution.py:748
  72.6 1.4 %collective-permute-start.5 = (bf16[64,2176]{1,0:T(8,128)(2,1)S(1)}, bf16[64,2176]{1,0:T(8,128)(2,1)S(1)}, u32[]{:S(2)}, u32[]{:S(2)}) collective-permute-start(bf16[64,2176]{1,0:T(8,128)(2,1)S(1)} %get-tuple-element.49), channel_id=1, source_target_pairs={{0,6},{1,7},{2,0},{3,1},{4,2},{5,3},{6,4},{7,5},{8,14},{9,15},{10,... | collective-permute-start | bytes 835592 | tf_op jit(solution)/shard_map/ppermute | solution.py:748
  74.0 20.8 %all_to_all.10.grads_ref = bf16[16,32,256]{2,1,0:T(8,128)(2,1)S(1)} all-to-all(bf16[16,32,256]{2,1,0:T(8,128)(2,1)S(1)} %bitcast.6), channel_id=1, replica_groups=mesh['space'=16,'mp'=8] {'space'}, dimensions={0} | all-to-all | bytes 524288 | tf_op jit(solution)/shard_map/all_to_all | solution.py:741
  94.8 0.0 collective-permute-done.3.b_ref
  94.8 0.0 collective-permute-done.4.c_ref
  94.8 0.0 collective-permute-done.5.d_ref
  94.8 0.0 copy-done.1
  94.8 0.0 copy-done.7
  94.8 0.0 copy-done.9
  94.8 1.8 %shard_map.94 = (bf16[64,2048]{1,0:T(8,128)(2,1)}, f32[32,192]{1,0:T(8,128)}, f32[32,64]{1,0:T(8,128)}) custom-call(s32[16,1,128]{2,1,0:T(1,128)S(1)} %all-to-all-done.counts_ref, bf16[64,2176]{1,0:T(8,128)(2,1)S(1)} %get-tuple-element.46.a_ref, bf16[64,2176]{1,0:T(8,128)(2,1)S(1)} %collective-permute-done.3.b_ref, ...), custom_call_target="tpu_custom_call" | custom-call | flops 2529999872 | tf_op jit(solution)/shard_map/pallas_call | solution.py:524
Async XLA Ops:
  0.6 0.7 copy-start.2
  2.0 19.0 %all-to-all-start = ((s32[16,1,128]{2,1,0:T(1,128)}), s32[16,1,128]{2,1,0:T(1,128)S(1)}, u32[]{:S(2)}, u32[]{:S(2)}) async-start(s32[16,1,128]{2,1,0:T(1,128)} %shard_map.85), calls=%async_computation | async-start | bytes 16384 | tf_op jit(solution)/shard_map/all_to_all | solution.py:725
  15.5 15.5 %collective-permute-start = (bf16[1024,256]{1,0:T(8,128)(2,1)}, bf16[1024,256]{1,0:T(8,128)(2,1)S(1)}, u32[]{:S(2)}, u32[]{:S(2)}) collective-permute-start(bf16[1024,256]{1,0:T(8,128)(2,1)} %get-tuple-element.36.rest_7_), channel_id=1, source_target_pairs={{8,0},{16,8},{24,16},{32,24},{40,32},{48,40},{56,48},{64,56},{72,6... | collective-permute-start | bytes 1572872 | tf_op jit(solution)/shard_map/ppermute | solution.py:732
  21.0 1.0 %copy-start.4 = (bf16[2048,128]{1,0:T(8,128)(2,1)S(1)}, bf16[2048,128]{1,0:T(8,128)(2,1)}, u32[]{:S(2)}) copy-start(bf16[2048,128]{1,0:T(8,128)(2,1)} %get-tuple-element.37.rest_0_.rest_1_.one_ref) | copy-start | bytes 1572868
  22.0 9.0 %copy-start.6 = (bf16[2048,128]{1,0:T(8,128)(2,1)S(1)}, bf16[2048,128]{1,0:T(8,128)(2,1)}, u32[]{:S(2)}) copy-start(bf16[2048,128]{1,0:T(8,128)(2,1)} %get-tuple-element.38.rest_1_.rest_0_.two_ref) | copy-start | bytes 1572868
  45.5 15.7 %collective-permute-start.1 = (bf16[1024,256]{1,0:T(8,128)(2,1)S(1)}, bf16[1024,256]{1,0:T(8,128)(2,1)S(1)}, u32[]{:S(2)}, u32[]{:S(2)}) collective-permute-start(bf16[1024,256]{1,0:T(8,128)(2,1)S(1)} %get-tuple-element.40), channel_id=1, source_target_pairs={{0,8},{8,16},{16,24},{24,32},{32,40},{40,48},{48,56},{56,64},{64,7... | collective-permute-start | bytes 1572872 | tf_op jit(solution)/shard_map/ppermute | solution.py:735
  49.1 12.1 %copy-start.5 = (bf16[2048,128]{1,0:T(8,128)(2,1)S(1)}, bf16[2048,128]{1,0:T(8,128)(2,1)}, u32[]{:S(2)}) copy-start(bf16[2048,128]{1,0:T(8,128)(2,1)} %get-tuple-element.37.rest_0_.rest_1_.one_ref) | copy-start | bytes 1572868
  49.1 12.1 %copy-start.8 = (bf16[512,256]{1,0:T(8,128)(2,1)S(1)}, bf16[512,256]{1,0:T(8,128)(2,1)}, u32[]{:S(2)}) copy-start(bf16[512,256]{1,0:T(8,128)(2,1)} %get-tuple-element.29.rest_0_.wide_ref) | copy-start | bytes 786436
  49.2 12.1 %copy-start.10 = (bf16[16,256]{1,0:T(8,128)(2,1)S(1)}, bf16[16,256]{1,0:T(8,128)(2,1)}, u32[]{:S(2)}) copy-start(bf16[16,256]{1,0:T(8,128)(2,1)} %get-tuple-element.41.wg_ref) | copy-start | bytes 24580
  61.2 3.9 %copy-start = (bf16[2048,512]{1,0:T(8,128)(2,1)S(1)}, bf16[2048,512]{1,0:T(8,128)(2,1)}, u32[]{:S(2)}) copy-start(bf16[2048,512]{1,0:T(8,128)(2,1)} %dy_ref.1) | copy-start | bytes 6291460
  61.2 3.8 %copy-start.3 = (bf16[2048,512]{1,0:T(8,128)(2,1)S(1)}, bf16[2048,512]{1,0:T(8,128)(2,1)}, u32[]{:S(2)}) copy-start(bf16[2048,512]{1,0:T(8,128)(2,1)} %get-tuple-element.45.unit_ref) | copy-start | bytes 6291460
  64.7 2.8 %collective-permute-start.2 = (bf16[272,2048]{1,0:T(8,128)(2,1)S(1)}, bf16[272,2048]{1,0:T(8,128)(2,1)S(1)}, u32[]{:S(2)}, u32[]{:S(2)}) collective-permute-start(bf16[272,2048]{1,0:T(8,128)(2,1)S(1)} %get-tuple-element.43), channel_id=1, source_target_pairs={{0,1},{1,0},{2,3},{3,2},{4,5},{5,4},{6,7},{7,6},{8,9},{9,8},{10,11... | collective-permute-start | bytes 3342344 | tf_op jit(solution)/shard_map/ppermute | solution.py:739
  67.1 27.6 %copy-start.1 = (f32[512]{0:T(512)S(1)}, f32[512]{0:T(512)}, u32[]{:S(2)}) copy-start(f32[512]{0:T(512)} %param.9) | copy-start | bytes 6148
  67.2 27.6 %copy-start.7 = (bf16[128,2048]{1,0:T(8,128)(2,1)S(1)}, bf16[128,2048]{1,0:T(8,128)(2,1)}, u32[]{:S(2)}) copy-start(bf16[128,2048]{1,0:T(8,128)(2,1)} %get-tuple-element.50.own_ref) | copy-start | bytes 1572868
  67.2 27.6 %copy-start.9 = (f32[8,2048]{1,0:T(8,128)S(1)}, f32[8,2048]{1,0:T(8,128)}, u32[]{:S(2)}) copy-start(f32[8,2048]{1,0:T(8,128)} %get-tuple-element.51.stat_ref) | copy-start | bytes 196612
  67.8 27.0 %collective-permute-start.3 = (bf16[64,2176]{1,0:T(8,128)(2,1)S(1)}, bf16[64,2176]{1,0:T(8,128)(2,1)S(1)}, u32[]{:S(2)}, u32[]{:S(2)}) collective-permute-start(bf16[64,2176]{1,0:T(8,128)(2,1)S(1)} %get-tuple-element.47), channel_id=1, source_target_pairs={{0,2},{1,3},{2,4},{3,5},{4,6},{5,7},{6,0},{7,1},{8,10},{9,11},{10,... | collective-permute-start | bytes 835592 | tf_op jit(solution)/shard_map/ppermute | solution.py:748
  69.8 24.9 %collective-permute-start.4 = (bf16[64,2176]{1,0:T(8,128)(2,1)S(1)}, bf16[64,2176]{1,0:T(8,128)(2,1)S(1)}, u32[]{:S(2)}, u32[]{:S(2)}) collective-permute-start(bf16[64,2176]{1,0:T(8,128)(2,1)S(1)} %get-tuple-element.48), channel_id=1, source_target_pairs={{0,4},{1,5},{2,6},{3,7},{4,0},{5,1},{6,2},{7,3},{8,12},{9,13},{10,... | collective-permute-start | bytes 835592 | tf_op jit(solution)/shard_map/ppermute | solution.py:748
  72.6 22.2 %collective-permute-start.5 = (bf16[64,2176]{1,0:T(8,128)(2,1)S(1)}, bf16[64,2176]{1,0:T(8,128)(2,1)S(1)}, u32[]{:S(2)}, u32[]{:S(2)}) collective-permute-start(bf16[64,2176]{1,0:T(8,128)(2,1)S(1)} %get-tuple-element.49), channel_id=1, source_target_pairs={{0,6},{1,7},{2,0},{3,1},{4,2},{5,3},{6,4},{7,5},{8,14},{9,15},{10,... | collective-permute-start | bytes 835592 | tf_op jit(solution)/shard_map/ppermute | solution.py:748

commit v5 on v4

--- a/solution.py
+++ b/solution.py
@@ -54,7 +54,7 @@
     return high, (value - high.astype(F32)).astype(BF)
 
 
-def project_kernel(lead, x_hbm, dy_hbm, gain_hbm, *rest):
+def project_rows(lead, x_hbm, dy_hbm, gain_hbm, *rest):
     if lead:
         wqkv_hbm, wproj_hbm = rest[:2]
         one_hbm, two_hbm, unit_hbm, own_hbm, stat_hbm, head_hbm = rest[2:8]
@@ -64,9 +64,9 @@
         pairs = ((wqkv_hbm, wqkv_ref), (wproj_hbm, wproj_ref))
     else:
         wide_hbm, side_hbm = rest[:2]
-        one_hbm, two_hbm, unit_hbm, own_hbm, stat_hbm = rest[8:13]
-        wide_ref, side_ref = rest[13:15]
-        rest = rest[15:]
+        one_hbm, two_hbm, unit_hbm, own_hbm, stat_hbm = rest[7:12]
+        wide_ref, side_ref = rest[12:14]
+        rest = rest[14:]
         pairs = ((wide_hbm, wide_ref), (side_hbm, side_ref))
     x_ref, dy_ref, gain_ref, qkvu_ref, unit_ref, own_ref, stat_ref, row_sems, sems, out_sems = rest
     half, width = x_ref.shape
@@ -154,6 +154,31 @@
         for which in range(6 if lead else 5):
             copies.append(out_copy(i, which))
             copies[-1].start()
+    return copies
+
+
+def project_kernel(*refs):
+    for copy in project_rows(True, *refs):
+        copy.wait()
+
+
+def front_kernel(
+    counts_ref, x_hbm, dy_hbm, gain_hbm, wide_hbm, side_hbm, head_hbm, *rest
+):
+    carried, outs, local_ref = rest[:5], rest[5:10], rest[10]
+    (wide_ref, side_ref, *project_scratch) = rest[11:23]
+    first_ref, first_sem = rest[23:25]
+    half = head_hbm.shape[0]
+    lower = pltpu.make_async_copy(head_hbm.at[:, :PAIR], first_ref.at[pl.ds(0, half)], first_sem.at[0])
+    lower.start()
+    copies = project_rows(
+        False, x_hbm, dy_hbm, gain_hbm, wide_hbm, side_hbm, *carried, *outs,
+        wide_ref, side_ref, *project_scratch,
+    )
+    qkvu_ref = project_scratch[3]
+    first_ref[half:, :] = qkvu_ref[:, :PAIR]
+    lower.wait()
+    attend_kernel(False, 1, counts_ref, first_ref, None, local_ref, *rest[25:])
     for copy in copies:
         copy.wait()
 
@@ -247,14 +272,16 @@
         flip = dot_nt(onehot(src == dst), x)
         flip_ref[...] = flip.astype(BF)
         square = flip * flip
-        bounded = True
+        most = jnp.zeros((1, 1), F32)
         for h in range(2 * pairs):
             at = h * GROUP
             value_ref[h, :HEAD, :] = flip_ref[at + 2 * HEAD : at + 3 * HEAD, :]
             value_ref[h, HEAD:, :] = jnp.ones((HEAD, PATCH), BF)
-            most_q = jnp.max(jnp.sum(square[at : at + HEAD], axis=0))
-            most_k = jnp.max(jnp.sum(square[at + HEAD : at + 2 * HEAD], axis=0))
-            bounded &= most_q * most_k * scale * scale <= SAFE * SAFE
+            most_q = jnp.sum(square[at : at + HEAD], axis=0, keepdims=True)
+            most_k = jnp.sum(square[at + HEAD : at + 2 * HEAD], axis=0, keepdims=True)
+            both = jnp.max(most_q, axis=1, keepdims=True) * jnp.max(most_k, axis=1, keepdims=True)
+            most = jnp.maximum(most, both)
+        bounded = jnp.max(most) * scale * scale <= SAFE * SAFE
         turn_ref[...] = jnp.zeros_like(turn_ref)
         top_ref[...] = jnp.zeros_like(top_ref)
         row = iota((HEAD, BLOCK), 0)
@@ -385,10 +412,11 @@
             out_ref[...] = jnp.zeros_like(out_ref)
 
 
-def product_kernel(
-    mine_ref, a_ref, b_ref, got_ref, one_ref, two_ref, wide_ref, wg_ref,
-    keep_ref, send_ref, total_ref, turned_ref,
-):
+def product_kernel(lower, mine_ref, a_ref, b_ref, one_ref, two_ref, wide_ref, wg_ref, *rest):
+    if lower:
+        got_ref = rest[0]
+        rest = rest[4:]
+    keep_ref, send_ref, total_ref, turned_ref = rest
     step = pl.program_id(0)
     rows = a_ref.shape[0]
     core = lax.axis_index("mp") % 2
@@ -402,9 +430,10 @@
                 to_row = (side * 4 + x) * cols
                 turned_ref[to_row : to_row + cols, :] = wide_ref[pl.ds(from_row, cols), :]
 
-    got = jnp.where(step < PATCH // rows, got_ref[...].astype(F32), 0.0)
     local = jnp.concatenate([a_ref[...], b_ref[...]], axis=1)
-    wide_total = mine_ref[...].astype(F32) + local.astype(F32) + got
+    wide_total = mine_ref[...].astype(F32) + local.astype(F32)
+    if lower:
+        wide_total = wide_total + got_ref[...].astype(F32)
     total = wide_total.astype(BF)
     total_ref[...] = total
     du = dot_nt(turned_ref[...], total).astype(BF)
@@ -536,15 +565,19 @@
     )(*args)
 
 
-def project(points, cotangent, gain, w_qkv, w_proj):
+def project(counts, points, cotangent, gain, w_qkv, w_proj):
     slots, width = points.shape
     cols = width // 8
     half = slots // 2
+    points, cotangent, gain, w_qkv, w_proj = (
+        pltpu.with_memory_space_constraint(a, pltpu.HBM)
+        for a in (points, cotangent, gain, w_qkv, w_proj)
+    )
     chunks = half // CHUNK
     outs = [
         shape((slots, PAIR), BF),
         shape((slots, PAIR), BF),
-        shape((slots, width), BF),
+        pltpu.HBM((slots, width), BF),
         shape((2 * cols, slots), BF),
         shape((8, slots), F32),
     ]
@@ -563,28 +596,34 @@
         pltpu.SemaphoreType.DMA((6, chunks)),
     ]
     results = call(
-        functools.partial(project_kernel, True),
+        project_kernel,
         (points, cotangent, gain, w_qkv, w_proj),
         (1,),
         [ANY] * 5,
         [ANY] * 6 + [whole(e.shape) for e in extra],
         outs + [head] + extra,
         [pltpu.VMEM(w_qkv.shape, BF), pltpu.VMEM(w_proj.shape, BF)] + scratch,
-        FULL,
+        32,
         4.5,
     )
     head, wide, side, wg = results[5:]
+    carried = list(results[:5])
+    carried[2] = pltpu.with_memory_space_constraint(carried[2], pltpu.HBM)
+    outs = outs + [shape((slots, PAIR), BF)]
     again = call(
-        functools.partial(project_kernel, False),
-        (points, cotangent, gain, wide, side, *results[:5], head),
+        front_kernel,
+        (counts, points, cotangent, gain, wide, side, head, *carried),
         (1,),
-        [ANY] * 11,
-        [ANY] * 5,
+        [SMEM] + [ANY] * 11,
+        [ANY] * 5 + [whole((slots, PAIR))],
         outs,
-        [pltpu.VMEM(e.shape, BF) for e in extra[:2]] + scratch,
-        FULL,
-        3.0,
-        {5 + i: i for i in range(5)},
+        [pltpu.VMEM(e.shape, BF) for e in extra[:2]]
+        + scratch
+        + [pltpu.VMEM((slots, PAIR), BF), pltpu.SemaphoreType.DMA((1,))]
+        + attend_scratch(slots, 1),
+        32,
+        11.0,
+        {7 + i: i for i in range(5)},
     )
     return (*again, head, wide, wg)
 
@@ -600,6 +639,24 @@
     return call(
         count_kernel, (cells,), (1,), [whole(cells.shape)], whole(out.shape), out, [], 1, 0.5
     )
+
+
+def attend_scratch(slots, pairs):
+    lanes = pairs * PAIR
+    return [
+        pltpu.VMEM((PATCH, lanes), BF),
+        pltpu.VMEM((PATCH, lanes), BF),
+        pltpu.VMEM((lanes, PATCH), BF),
+        pltpu.VMEM((2 * pairs, 2 * HEAD, PATCH), BF),
+        pltpu.VMEM((8, BLOCK), F32),
+        pltpu.VMEM((4, PATCH, BLOCK), F32),
+        pltpu.VMEM((PATCH, 4 * BLOCK), BF),
+        pltpu.VMEM((PATCH, 4 * BLOCK), BF),
+        pltpu.VMEM((lanes, PATCH), F32),
+        pltpu.VMEM((PATCH + 2 * MARGIN, lanes), BF),
+        pltpu.VMEM((slots + 2 * MARGIN, lanes), BF),
+        pltpu.VMEM((PATCH + 2 * MARGIN, lanes), BF),
+    ]
 
 
 def attend(spanning, counts, owns, following, after):
@@ -615,20 +672,7 @@
         [SMEM] + [whole(a.shape) for a in args] + [ANY],
         [whole(o.shape) for o in outs],
         outs,
-        [
-            pltpu.VMEM((PATCH, lanes), BF),
-            pltpu.VMEM((PATCH, lanes), BF),
-            pltpu.VMEM((lanes, PATCH), BF),
-            pltpu.VMEM((2 * pairs, 2 * HEAD, PATCH), BF),
-            pltpu.VMEM((8, BLOCK), F32),
-            pltpu.VMEM((4, PATCH, BLOCK), F32),
-            pltpu.VMEM((PATCH, 4 * BLOCK), BF),
-            pltpu.VMEM((PATCH, 4 * BLOCK), BF),
-            pltpu.VMEM((lanes, PATCH), F32),
-            pltpu.VMEM((PATCH + 2 * MARGIN, lanes), BF),
-            pltpu.VMEM((slots + 2 * MARGIN, lanes), BF),
-            pltpu.VMEM((PATCH + 2 * MARGIN, lanes), BF),
-        ],
+        attend_scratch(slots, pairs),
         24,
         7.5 * pairs,
     )
@@ -639,22 +683,29 @@
     width = wide.shape[0]
     rows = 256
     half = width // 2 + 16
-    last = PATCH // rows - 1
-    down = pl.BlockSpec((rows, PAIR), lambda i: (i, 0))
-    full = pl.BlockSpec((rows, LANES), lambda i: (i, 0))
-    first = pl.BlockSpec((rows, LANES), lambda i: (jnp.minimum(i, last), 0))
-    across = pl.BlockSpec((half, rows), lambda i: (0, i))
-    return call(
-        product_kernel,
-        (mine, *locals_, got, *heads, wide, wg),
-        (slots // rows,),
-        [full, down, down, first, down, down] + [whole(wide.shape), whole(wg.shape)],
-        [across, across, pl.BlockSpec((rows, LANES), lambda i: (i, 0))],
-        [shape((half, slots), BF), shape((half, slots), BF), shape((slots, LANES), BF)],
-        [pltpu.VMEM((width, LANES), BF)],
-        24,
-        4.0,
-    )
+    outs = [shape((half, slots), BF), shape((half, slots), BF), shape((slots, LANES), BF)]
+    steps = PATCH // rows
+
+    def part(offset, more, more_specs, steps, aliases):
+        down = pl.BlockSpec((rows, PAIR), lambda i: (i + offset, 0))
+        full = pl.BlockSpec((rows, LANES), lambda i: (i + offset, 0))
+        across = pl.BlockSpec((half, rows), lambda i: (0, i + offset))
+        return call(
+            functools.partial(product_kernel, bool(more)),
+            (mine, *locals_, *heads, wide, wg, *more),
+            (steps,),
+            [full, down, down, down, down, whole(wide.shape), whole(wg.shape)] + more_specs,
+            [across, across, full],
+            outs,
+            [pltpu.VMEM((width, LANES), BF)],
+            16,
+            2.0,
+            aliases,
+        )
+
+    upper = part(steps, (), [], slots // rows - steps, {})
+    row = pl.BlockSpec((rows, LANES), lambda i: (i, 0))
+    return part(0, (got, *upper), [row] + [ANY] * 3, steps, {8 + i: i for i in range(3)})
 
 
 def weights(total, unit, dy, after):
@@ -724,14 +775,13 @@
     n_mp = lax.axis_size("mp")
     counts = lax.all_to_all(count(cell_counts, n_space), "space", 0, 0)
     gain = norm_gain.reshape(1, width)
-    one, two, unit, own, stat, head, wide, wg = project(
-        points, cotangent, gain, w_qkv.T, w_proj
+    one, two, unit, own, stat, local_a, head, wide, wg = project(
+        counts, points, cotangent, gain, w_qkv.T, w_proj
     )
     back = [(i + 1, i) for i in range(n_space - 1)]
     onward = [(i, i + 1) for i in range(n_space - 1)]
     following = lax.ppermute(head, "space", back)
-    local_a = attend(False, counts, (one,), None, one)[0]
-    mine, spill = attend(True, counts, (one, two), following, local_a)
+    mine, spill = attend(True, counts, (one, two), following, one)
     got = lax.ppermute(spill, "space", onward)
     local_b = attend(False, counts, (two,), None, mine)[0]
     keep, send, total = products(mine, (local_a, local_b), got, (one, two), wide, wg)

time: 96 us -> 92.2 us (0.960); the launches traced: 96.6 us -> 91.3 us
  blocking collectives: 20.8 us -> 16.3 us
  starting transfers between devices: 19.6 us -> 22.4 us
  Pallas kernels: 48.8 us -> 47.4 us
  local copies, waits for them, and re-layouts: 1.73 us -> 0.66 us
  waiting for transfers between devices: 4.88 us -> 3.83 us
    all_to_all x1, blocking collectives: 20.8 us -> 16.3 us  [on_device(): lax.all_to_all(grads.reshape(n_space, width // n_space, LANES), 'space',...]
    ppermute x1, waiting for transfers between devices: 3.79 us -> 1.17 us  [on_device(): got = lax.ppermute(spill, 'space', onward)]
    ppermute x1, starting transfers between devices: 0.4 us -> 2.28 us  [on_device(): other = lax.ppermute(send, 'mp', swap)]
    pallas_call x10, Pallas kernels: 48.8 us -> 47.4 us  [call(): pl.pallas_call(kernel, grid=grid, in_specs=in_specs, out_specs=out_specs,...]
    all_to_all x1, waiting for transfers between devices: 0.01 us -> 1.29 us  [on_device(): counts = lax.all_to_all(count(cell_counts, n_space), 'space', 0, 0)]
    unnamed x22 -> x8, local copies, waits for them, and re-layouts: 1.73 us -> 0.66 us
  transfers between devices with their start and end apart: 7 -> 7, of which waited for: 3 -> 4; matrix products, arithmetic and copies ran while one was open for 0% -> 0% of each run, Pallas kernels for 29% -> 31%
where the time goes in v5:
time: 92.2 us; the launch traced here: 91.3 us
  Pallas kernels  47.4 us (51%)
  starting transfers between devices  22.4 us (24%)
  blocking collectives  16.3 us (18%)
  waiting for transfers between devices  3.83 us (4%)
    pallas_call x10, Pallas kernels, call(): pl.pallas_call(kernel, grid=grid, in_specs=in_specs, out_specs=out_specs,...  47.4 us
    all_to_all x1, blocking collectives, on_device(): lax.all_to_all(grads.reshape(n_space, width // n_space, LANES), 'space',...  16.3 us
    all_to_all x1, starting transfers between devices, on_device(): counts = lax.all_to_all(count(cell_counts, n_space), 'space', 0, 0)  8.13 us
    ppermute x3, starting transfers between devices, on_device(): received.append(lax.ppermute(parts[d], 'mp', route))  7.1 us
    ppermute x1, starting transfers between devices, on_device(): got = lax.ppermute(spill, 'space', onward)  3.58 us
    ppermute x1, starting transfers between devices, on_device(): other = lax.ppermute(send, 'mp', swap)  2.28 us
  transfers between devices with their start and end apart: 7, of which 4 were waited for; matrix products, arithmetic and copies ran while one was open for 0% of the time, Pallas kernels for 31%

profile of v5, /device:TPU:0, one launch (start us, length us, event | category | flops | bytes accessed | tf_op | source)
XLA Modules:
  0.0 91.3 jit_solution(12072945534530905865)
XLA Ops:
  0.6 0.0 copy-start.2
  0.6 0.6 copy-done.2
  1.3 0.7 shard_map.85
  2.0 8.1 %all-to-all-start = ((s32[16,1,128]{2,1,0:T(1,128)}), s32[16,1,128]{2,1,0:T(1,128)S(1)}, u32[]{:S(2)}, u32[]{:S(2)}) async-start(s32[16,1,128]{2,1,0:T(1,128)} %shard_map.85), calls=%async_computation | async-start | bytes 16384 | tf_op jit(solution)/shard_map/all_to_all | solution.py:776
  10.1 4.9 %shard_map.86 = (bf16[2048,128]{1,0:T(8,128)(2,1)S(1)}, bf16[2048,128]{1,0:T(8,128)(2,1)S(1)}, bf16[2048,512]{1,0:T(8,128)(2,1)}, bf16[128,2048]{1,0:T(8,128)(2,...) custom-call(bf16[2048,512]{1,0:T(8,128)(2,1)} %x_hbm.1, ...), custom_call_target="tpu_custom_call" | custom-call | flops 4950000128 | tf_op jit(solution)/shard_map/pallas_call | solution.py:553
  15.0 1.3 %collective-permute-start = (bf16[1024,256]{1,0:T(8,128)(2,1)S(1)}, bf16[1024,256]{1,0:T(8,128)(2,1)S(1)}, u32[]{:S(2)}, u32[]{:S(2)}) collective-permute-start(bf16[1024,256]{1,0:T(8,128)(2,1)S(1)} %get-tuple-element.35.head_hbm), channel_id=1, source_target_pairs={{8,0},{16,8},{24,16},{32,24},{40,32},{48,40},{56,48},{64,56},{72,6... | collective-permute-start | bytes 1572872 | tf_op jit(solution)/shard_map/ppermute | solution.py:783
  16.3 1.3 %all-to-all-done.counts_ref = s32[16,1,128]{2,1,0:T(1,128)S(1)} async-done(((s32[16,1,128]{2,1,0:T(1,128)}), s32[16,1,128]{2,1,0:T(1,128)S(1)}, u32[]{:S(2)}, u32[]{:S(2)}) %all-to-all-start) | async-done | bytes 8224 | tf_op jit(solution)/shard_map/all_to_all | solution.py:776
  17.6 11.6 %shard_map.87 = (bf16[2048,128]{1,0:T(8,128)(2,1)S(1)}, bf16[2048,128]{1,0:T(8,128)(2,1)S(1)}, bf16[2048,512]{1,0:T(8,128)(2,1)}, bf16[128,2048]{1,0:T(8,128)(2,...) custom-call(s32[16,1,128]{2,1,0:T(1,128)S(1)} %all-to-all-done.count, ...), custom_call_target="tpu_custom_call", output_to_operand_aliasing={{0}: (7, {}), {1}: (8, {}), {2}: (9, {}), {3}: (10, {}), {4... | custom-call | flops 12099999744 | tf_op jit(solution)/shard_map/pallas_call | solution.py:553
  29.2 1.1 %collective-permute-done.rest_2_ = bf16[1024,256]{1,0:T(8,128)(2,1)S(1)} collective-permute-done((bf16[1024,256]{1,0:T(8,128)(2,1)S(1)}, bf16[1024,256]{1,0:T(8,128)(2,1)S(1)}, u32[]{:S(2)}, u32[]{:S(2)}) %collective-permute-start) | collective-permute-done | bytes 524320 | tf_op jit(solution)/shard_map/ppermute | solution.py:783
  30.3 14.5 %shard_map.88 = (bf16[2048,256]{1,0:T(8,128)(2,1)S(1)}, bf16[1024,256]{1,0:T(8,128)(2,1)S(1)}) custom-call(s32[16,1,128]{2,1,0:T(1,128)S(1)} %all-to-all-done.counts_ref, bf16[2048,128]{1,0:T(8,128)(2,1)S(1)} %get-tuple-element.41.rest_0_.rest_3_.one_ref, bf16[2048,128]{1,0:T(8,128)(2,1)S(1)} %get-tuple-element.42.rest_1_.rest_0_.two_ref, ...), custom_call_target="tpu_custom_call" | custom-call | flops 16499999744 | tf_op jit(solution)/shard_map/pallas_call | solution.py:553
  44.8 3.6 %collective-permute-start.1 = (bf16[1024,256]{1,0:T(8,128)(2,1)S(1)}, bf16[1024,256]{1,0:T(8,128)(2,1)S(1)}, u32[]{:S(2)}, u32[]{:S(2)}) collective-permute-start(bf16[1024,256]{1,0:T(8,128)(2,1)S(1)} %get-tuple-element.46), channel_id=1, source_target_pairs={{0,8},{8,16},{16,24},{24,32},{32,40},{40,48},{48,56},{56,64},{64,7... | collective-permute-start | bytes 1572872 | tf_op jit(solution)/shard_map/ppermute | solution.py:785
  48.4 8.2 %shard_map.89.b_ref = bf16[2048,128]{1,0:T(8,128)(2,1)S(1)} custom-call(s32[16,1,128]{2,1,0:T(1,128)S(1)} %all-to-all-done.counts_ref, bf16[2048,128]{1,0:T(8,128)(2,1)S(1)} %get-tuple-element.42.rest_1_.rest_0_.two_ref, bf16[2048,256]{1,0:T(8,128)(2,1)S(1)} %get-tuple-element.43.rest_1_.mine_ref), custom_call_target="tpu_custom_call" | custom-call | flops 8249999872 | tf_op jit(solution)/shard_map/pallas_call | solution.py:553
  56.7 1.6 %shard_map.90 = (bf16[272,2048]{1,0:T(8,128)(2,1)S(1)}, bf16[272,2048]{1,0:T(8,128)(2,1)S(1)}, bf16[2048,256]{1,0:T(8,128)(2,1)S(1)}) custom-call(bf16[2048,256]{1,0:T(8,128)(2,1)S(1)} %get-tuple-element.43.rest_1_.mine_ref, bf16[2048,128]{1,0:T(8,128)(2,1)S(1)} %get-tuple-element.44.a_ref, bf16[2048,128]{1,0:T(8,128)(2,1)S(1)} %shard_map.89.b_ref, ...), custom_call_target="tpu_custom_call" | custom-call | flops 2200000000 | tf_op jit(solution)/shard_map/pallas_call | solution.py:553
  58.3 1.2 %collective-permute-done.1.rest_0_ = bf16[1024,256]{1,0:T(8,128)(2,1)S(1)} collective-permute-done((bf16[1024,256]{1,0:T(8,128)(2,1)S(1)}, bf16[1024,256]{1,0:T(8,128)(2,1)S(1)}, u32[]{:S(2)}, u32[]{:S(2)}) %collective-permute-start.1) | collective-permute-done | bytes 524320 | tf_op jit(solution)/shard_map/ppermute | solution.py:785
  59.5 0.0 copy-start
  59.5 0.0 copy-start.3
  59.5 1.7 %shard_map.91 = (bf16[272,2048]{1,0:T(8,128)(2,1)S(1)}, bf16[272,2048]{1,0:T(8,128)(2,1)S(1)}, bf16[2048,256]{1,0:T(8,128)(2,1)S(1)}) custom-call(bf16[2048,256]{1,0:T(8,128)(2,1)S(1)} %get-tuple-element.43.rest_1_.mine_ref, bf16[2048,128]{1,0:T(8,128)(2,1)S(1)} %get-tuple-element.44.a_ref, ...), custom_call_target="tpu_custom_call", output_to_operand_aliasing={{0}: (8, {}), {1}: (9, {}), {2}: (10, {})} | custom-call | flops 2200000000 | tf_op jit(solution)/shard_map/pallas_call | solution.py:553
  61.2 2.3 %collective-permute-start.2 = (bf16[272,2048]{1,0:T(8,128)(2,1)S(1)}, bf16[272,2048]{1,0:T(8,128)(2,1)S(1)}, u32[]{:S(2)}, u32[]{:S(2)}) collective-permute-start(bf16[272,2048]{1,0:T(8,128)(2,1)S(1)} %get-tuple-element.51), channel_id=1, source_target_pairs={{0,1},{1,0},{2,3},{3,2},{4,5},{5,4},{6,7},{7,6},{8,9},{9,8},{10,11... | collective-permute-start | bytes 3342344 | tf_op jit(solution)/shard_map/ppermute | solution.py:789
  63.4 0.0 copy-done
  63.4 0.0 copy-done.3
  63.4 2.1 %shard_map.92.after_ref = bf16[512,256]{1,0:T(8,128)(2,1)S(1)} custom-call(bf16[2048,256]{1,0:T(8,128)(2,1)S(1)} %get-tuple-element.52.total_ref, bf16[2048,512]{1,0:T(8,128)(2,1)S(1)} %copy-done.3, bf16[2048,512]{1,0:T(8,128)(2,1)S(1)} %copy-done, bf16[272,2048]{1,0:T(8,128)(2,1)S(1)} %get-tuple-element.50.after_ref.keep_ref), custom_call_target="tpu_custom_call" | custom-call | flops 4400000000 | tf_op jit(solution)/shard_map/pallas_call | solution.py:553
  65.5 0.0 copy-start.1
  65.5 0.3 collective-permute-done.2.got_ref
  65.8 0.3 shard_map.93
  66.1 2.9 %collective-permute-start.3 = (bf16[64,2176]{1,0:T(8,128)(2,1)S(1)}, bf16[64,2176]{1,0:T(8,128)(2,1)S(1)}, u32[]{:S(2)}, u32[]{:S(2)}) collective-permute-start(bf16[64,2176]{1,0:T(8,128)(2,1)S(1)} %get-tuple-element.55), channel_id=1, source_target_pairs={{0,2},{1,3},{2,4},{3,5},{4,6},{5,7},{6,0},{7,1},{8,10},{9,11},{10,... | collective-permute-start | bytes 835592 | tf_op jit(solution)/shard_map/ppermute | solution.py:798
  69.1 2.7 %collective-permute-start.4 = (bf16[64,2176]{1,0:T(8,128)(2,1)S(1)}, bf16[64,2176]{1,0:T(8,128)(2,1)S(1)}, u32[]{:S(2)}, u32[]{:S(2)}) collective-permute-start(bf16[64,2176]{1,0:T(8,128)(2,1)S(1)} %get-tuple-element.56), channel_id=1, source_target_pairs={{0,4},{1,5},{2,6},{3,7},{4,0},{5,1},{6,2},{7,3},{8,12},{9,13},{10,... | collective-permute-start | bytes 835592 | tf_op jit(solution)/shard_map/ppermute | solution.py:798
  71.8 1.4 %collective-permute-start.5 = (bf16[64,2176]{1,0:T(8,128)(2,1)S(1)}, bf16[64,2176]{1,0:T(8,128)(2,1)S(1)}, u32[]{:S(2)}, u32[]{:S(2)}) collective-permute-start(bf16[64,2176]{1,0:T(8,128)(2,1)S(1)} %get-tuple-element.57), channel_id=1, source_target_pairs={{0,6},{1,7},{2,0},{3,1},{4,2},{5,3},{6,4},{7,5},{8,14},{9,15},{10,... | collective-permute-start | bytes 835592 | tf_op jit(solution)/shard_map/ppermute | solution.py:798
  73.2 16.3 %all_to_all.10.grads_ref = bf16[16,32,256]{2,1,0:T(8,128)(2,1)S(1)} all-to-all(bf16[16,32,256]{2,1,0:T(8,128)(2,1)S(1)} %bitcast.6), channel_id=1, replica_groups=mesh['space'=16,'mp'=8] {'space'}, dimensions={0} | all-to-all | bytes 524288 | tf_op jit(solution)/shard_map/all_to_all | solution.py:791
  89.5 0.0 collective-permute-done.3.b_ref
  89.5 0.0 collective-permute-done.4.c_ref
  89.5 0.0 collective-permute-done.5.d_ref
  89.5 0.0 copy-done.1
  89.5 1.8 %shard_map.94 = (bf16[64,2048]{1,0:T(8,128)(2,1)}, f32[32,192]{1,0:T(8,128)}, f32[32,64]{1,0:T(8,128)}) custom-call(s32[16,1,128]{2,1,0:T(1,128)S(1)} %all-to-all-done.counts_ref, bf16[64,2176]{1,0:T(8,128)(2,1)S(1)} %get-tuple-element.54.a_ref, bf16[64,2176]{1,0:T(8,128)(2,1)S(1)} %collective-permute-done.3.b_ref, ...), custom_call_target="tpu_custom_call" | custom-call | flops 2529999872 | tf_op jit(solution)/shard_map/pallas_call | solution.py:553
Async XLA Ops:
  0.6 0.7 copy-start.2
  2.0 15.6 %all-to-all-start = ((s32[16,1,128]{2,1,0:T(1,128)}), s32[16,1,128]{2,1,0:T(1,128)S(1)}, u32[]{:S(2)}, u32[]{:S(2)}) async-start(s32[16,1,128]{2,1,0:T(1,128)} %shard_map.85), calls=%async_computation | async-start | bytes 16384 | tf_op jit(solution)/shard_map/all_to_all | solution.py:776
  15.0 15.3 %collective-permute-start = (bf16[1024,256]{1,0:T(8,128)(2,1)S(1)}, bf16[1024,256]{1,0:T(8,128)(2,1)S(1)}, u32[]{:S(2)}, u32[]{:S(2)}) collective-permute-start(bf16[1024,256]{1,0:T(8,128)(2,1)S(1)} %get-tuple-element.35.head_hbm), channel_id=1, source_target_pairs={{8,0},{16,8},{24,16},{32,24},{40,32},{48,40},{56,48},{64,56},{72,6... | collective-permute-start | bytes 1572872 | tf_op jit(solution)/shard_map/ppermute | solution.py:783
  44.8 14.6 %collective-permute-start.1 = (bf16[1024,256]{1,0:T(8,128)(2,1)S(1)}, bf16[1024,256]{1,0:T(8,128)(2,1)S(1)}, u32[]{:S(2)}, u32[]{:S(2)}) collective-permute-start(bf16[1024,256]{1,0:T(8,128)(2,1)S(1)} %get-tuple-element.46), channel_id=1, source_target_pairs={{0,8},{8,16},{16,24},{24,32},{32,40},{40,48},{48,56},{56,64},{64,7... | collective-permute-start | bytes 1572872 | tf_op jit(solution)/shard_map/ppermute | solution.py:785
  59.5 4.0 %copy-start = (bf16[2048,512]{1,0:T(8,128)(2,1)S(1)}, bf16[2048,512]{1,0:T(8,128)(2,1)}, u32[]{:S(2)}) copy-start(bf16[2048,512]{1,0:T(8,128)(2,1)} %dy_ref.1) | copy-start | bytes 6291460
  59.5 4.0 %copy-start.3 = (bf16[2048,512]{1,0:T(8,128)(2,1)S(1)}, bf16[2048,512]{1,0:T(8,128)(2,1)}, u32[]{:S(2)}) copy-start(bf16[2048,512]{1,0:T(8,128)(2,1)} %get-tuple-element.53.unit_ref) | copy-start | bytes 6291460
  61.2 4.7 %collective-permute-start.2 = (bf16[272,2048]{1,0:T(8,128)(2,1)S(1)}, bf16[272,2048]{1,0:T(8,128)(2,1)S(1)}, u32[]{:S(2)}, u32[]{:S(2)}) collective-permute-start(bf16[272,2048]{1,0:T(8,128)(2,1)S(1)} %get-tuple-element.51), channel_id=1, source_target_pairs={{0,1},{1,0},{2,3},{3,2},{4,5},{5,4},{6,7},{7,6},{8,9},{9,8},{10,11... | collective-permute-start | bytes 3342344 | tf_op jit(solution)/shard_map/ppermute | solution.py:789
  65.5 24.0 %copy-start.1 = (f32[512]{0:T(512)S(1)}, f32[512]{0:T(512)}, u32[]{:S(2)}) copy-start(f32[512]{0:T(512)} %param.9) | copy-start | bytes 6148
  66.1 23.4 %collective-permute-start.3 = (bf16[64,2176]{1,0:T(8,128)(2,1)S(1)}, bf16[64,2176]{1,0:T(8,128)(2,1)S(1)}, u32[]{:S(2)}, u32[]{:S(2)}) collective-permute-start(bf16[64,2176]{1,0:T(8,128)(2,1)S(1)} %get-tuple-element.55), channel_id=1, source_target_pairs={{0,2},{1,3},{2,4},{3,5},{4,6},{5,7},{6,0},{7,1},{8,10},{9,11},{10,... | collective-permute-start | bytes 835592 | tf_op jit(solution)/shard_map/ppermute | solution.py:798
  69.1 20.4 %collective-permute-start.4 = (bf16[64,2176]{1,0:T(8,128)(2,1)S(1)}, bf16[64,2176]{1,0:T(8,128)(2,1)S(1)}, u32[]{:S(2)}, u32[]{:S(2)}) collective-permute-start(bf16[64,2176]{1,0:T(8,128)(2,1)S(1)} %get-tuple-element.56), channel_id=1, source_target_pairs={{0,4},{1,5},{2,6},{3,7},{4,0},{5,1},{6,2},{7,3},{8,12},{9,13},{10,... | collective-permute-start | bytes 835592 | tf_op jit(solution)/shard_map/ppermute | solution.py:798
  71.8 17.7 %collective-permute-start.5 = (bf16[64,2176]{1,0:T(8,128)(2,1)S(1)}, bf16[64,2176]{1,0:T(8,128)(2,1)S(1)}, u32[]{:S(2)}, u32[]{:S(2)}) collective-permute-start(bf16[64,2176]{1,0:T(8,128)(2,1)S(1)} %get-tuple-element.57), channel_id=1, source_target_pairs={{0,6},{1,7},{2,0},{3,1},{4,2},{5,3},{6,4},{7,5},{8,14},{9,15},{10,... | collective-permute-start | bytes 835592 | tf_op jit(solution)/shard_map/ppermute | solution.py:798

commit v6 on v5

--- a/solution.py
+++ b/solution.py
@@ -162,24 +162,8 @@
         copy.wait()
 
 
-def front_kernel(
-    counts_ref, x_hbm, dy_hbm, gain_hbm, wide_hbm, side_hbm, head_hbm, *rest
-):
-    carried, outs, local_ref = rest[:5], rest[5:10], rest[10]
-    (wide_ref, side_ref, *project_scratch) = rest[11:23]
-    first_ref, first_sem = rest[23:25]
-    half = head_hbm.shape[0]
-    lower = pltpu.make_async_copy(head_hbm.at[:, :PAIR], first_ref.at[pl.ds(0, half)], first_sem.at[0])
-    lower.start()
-    copies = project_rows(
-        False, x_hbm, dy_hbm, gain_hbm, wide_hbm, side_hbm, *carried, *outs,
-        wide_ref, side_ref, *project_scratch,
-    )
-    qkvu_ref = project_scratch[3]
-    first_ref[half:, :] = qkvu_ref[:, :PAIR]
-    lower.wait()
-    attend_kernel(False, 1, counts_ref, first_ref, None, local_ref, *rest[25:])
-    for copy in copies:
+def second_kernel(*refs):
+    for copy in project_rows(False, *refs):
         copy.wait()
 
 
@@ -565,7 +549,7 @@
     )(*args)
 
 
-def project(counts, points, cotangent, gain, w_qkv, w_proj):
+def project(cells, n_space, points, cotangent, gain, w_qkv, w_proj):
     slots, width = points.shape
     cols = width // 8
     half = slots // 2
@@ -609,35 +593,32 @@
     head, wide, side, wg = results[5:]
     carried = list(results[:5])
     carried[2] = pltpu.with_memory_space_constraint(carried[2], pltpu.HBM)
-    outs = outs + [shape((slots, PAIR), BF)]
+    counts = lax.all_to_all(count(cells, n_space, wg), "space", 0, 0)
     again = call(
-        front_kernel,
-        (counts, points, cotangent, gain, wide, side, head, *carried),
+        second_kernel,
+        (points, cotangent, gain, wide, side, *carried),
         (1,),
-        [SMEM] + [ANY] * 11,
-        [ANY] * 5 + [whole((slots, PAIR))],
+        [ANY] * 10,
+        [ANY] * 5,
         outs,
-        [pltpu.VMEM(e.shape, BF) for e in extra[:2]]
-        + scratch
-        + [pltpu.VMEM((slots, PAIR), BF), pltpu.SemaphoreType.DMA((1,))]
-        + attend_scratch(slots, 1),
+        [pltpu.VMEM(e.shape, BF) for e in extra[:2]] + scratch,
         32,
-        11.0,
-        {7 + i: i for i in range(5)},
-    )
-    return (*again, head, wide, wg)
-
-
-def count_kernel(cells_ref, out_ref):
+        3.3,
+        {5 + i: i for i in range(5)},
+    )
+    return (counts, *again, head, wide, wg)
+
+
+def count_kernel(cells_ref, after_ref, out_ref):
     total = jnp.sum(cells_ref[...].astype(F32), axis=1, keepdims=True).astype(jnp.int32)
     out_ref[...] = jnp.broadcast_to(total.reshape(1, 1, 1), out_ref.shape)
 
 
-def count(cells, n_space):
+def count(cells, n_space, after):
     out = shape((n_space, 1, 128), jnp.int32)
     cells = cells.reshape(1, -1)
     return call(
-        count_kernel, (cells,), (1,), [whole(cells.shape)], whole(out.shape), out, [], 1, 0.5
+        count_kernel, (cells, after), (1,), [whole(cells.shape), ANY], whole(out.shape), out, [], 1, 0.5
     )
 
 
@@ -773,15 +754,15 @@
     slots, width = points.shape
     n_space = lax.axis_size("space")
     n_mp = lax.axis_size("mp")
-    counts = lax.all_to_all(count(cell_counts, n_space), "space", 0, 0)
     gain = norm_gain.reshape(1, width)
-    one, two, unit, own, stat, local_a, head, wide, wg = project(
-        counts, points, cotangent, gain, w_qkv.T, w_proj
+    counts, one, two, unit, own, stat, head, wide, wg = project(
+        cell_counts, n_space, points, cotangent, gain, w_qkv.T, w_proj
     )
     back = [(i + 1, i) for i in range(n_space - 1)]
     onward = [(i, i + 1) for i in range(n_space - 1)]
     following = lax.ppermute(head, "space", back)
-    mine, spill = attend(True, counts, (one, two), following, one)
+    local_a = attend(False, counts, (one,), None, one)[0]
+    mine, spill = attend(True, counts, (one, two), following, local_a)
     got = lax.ppermute(spill, "space", onward)
     local_b = attend(False, counts, (two,), None, mine)[0]
     keep, send, total = products(mine, (local_a, local_b), got, (one, two), wide, wg)

time: 92.2 us -> 91.1 us (0.988)
    ppermute x1, starting transfers between devices: 2.28 us -> 0.65 us  [on_device(): other = lax.ppermute(send, 'mp', swap)]
    ppermute x3, starting transfers between devices: 7.1 us -> 8.55 us  [on_device(): received.append(lax.ppermute(parts[d], 'mp', route))]
    ppermute x1, waiting for transfers between devices: 1.08 us -> 0.01 us  [on_device(): following = lax.ppermute(head, 'space', back)]
    pallas_call x10 -> x11, Pallas kernels: 47.4 us -> 48.1 us  [call(): pl.pallas_call(kernel, grid=grid, in_specs=in_specs, out_specs=out_specs,...]
  transfers between devices with their start and end apart: 7 -> 7, of which waited for: 4 -> 3; matrix products, arithmetic and copies ran while one was open for 0% -> 0% of each run, Pallas kernels for 31% -> 27%
where the time goes in v6:
time: 91.1 us; the launch traced here: 90.7 us
  Pallas kernels  48.1 us (53%)
  starting transfers between devices  21.8 us (24%)
  blocking collectives  15.6 us (17%)
  waiting for transfers between devices  4.45 us (5%)
    pallas_call x11, Pallas kernels, call(): pl.pallas_call(kernel, grid=grid, in_specs=in_specs, out_specs=out_specs,...  48.1 us
    all_to_all x1, blocking collectives, on_device(): lax.all_to_all(grads.reshape(n_space, width // n_space, LANES), 'space',...  15.6 us
    ppermute x3, starting transfers between devices, on_device(): received.append(lax.ppermute(parts[d], 'mp', route))  8.55 us
    all_to_all x1, starting transfers between devices, project(): counts = lax.all_to_all(count(cells, n_space, wg), 'space', 0, 0)  8.13 us
    ppermute x1, starting transfers between devices, on_device(): got = lax.ppermute(spill, 'space', onward)  3.15 us
    all_to_all x1, waiting for transfers between devices, project(): counts = lax.all_to_all(count(cells, n_space, wg), 'space', 0, 0)  2.12 us
    ppermute x1, waiting for transfers between devices, on_device(): got = lax.ppermute(spill, 'space', onward)  2.03 us
  transfers between devices with their start and end apart: 7, of which 3 were waited for; matrix products, arithmetic and copies ran while one was open for 0% of the time, Pallas kernels for 27%

profile of v6, /device:TPU:0, one launch (start us, length us, event | category | flops | bytes accessed | tf_op | source)
XLA Modules:
  0.0 90.7 jit_solution(3044672352237986154)
XLA Ops:
  0.6 0.0 copy-start.2
  0.6 4.9 %shard_map.85 = (bf16[2048,128]{1,0:T(8,128)(2,1)S(1)}, bf16[2048,128]{1,0:T(8,128)(2,1)S(1)}, bf16[2048,512]{1,0:T(8,128)(2,1)}, bf16[128,2048]{1,0:T(8,128)(2,...) custom-call(bf16[2048,512]{1,0:T(8,128)(2,1)} %refs_0_.3, ...), custom_call_target="tpu_custom_call" | custom-call | flops 4950000128 | tf_op jit(solution)/shard_map/pallas_call | solution.py:537
  5.5 0.0 copy-done.2
  5.5 0.7 shard_map.86
  6.2 8.1 %all-to-all-start = ((s32[16,1,128]{2,1,0:T(1,128)}), s32[16,1,128]{2,1,0:T(1,128)S(1)}, u32[]{:S(2)}, u32[]{:S(2)}) async-start(s32[16,1,128]{2,1,0:T(1,128)} %shard_map.86), calls=%async_computation | async-start | bytes 16384 | tf_op jit(solution)/shard_map/all_to_all | solution.py:596
  14.4 1.3 %collective-permute-start = (bf16[1024,256]{1,0:T(8,128)(2,1)S(1)}, bf16[1024,256]{1,0:T(8,128)(2,1)S(1)}, u32[]{:S(2)}, u32[]{:S(2)}) collective-permute-start(bf16[1024,256]{1,0:T(8,128)(2,1)S(1)} %get-tuple-element.42), channel_id=1, source_target_pairs={{8,0},{16,8},{24,16},{32,24},{40,32},{48,40},{56,48},{64,56},{72,6... | collective-permute-start | bytes 1572872 | tf_op jit(solution)/shard_map/ppermute | solution.py:763
  15.7 4.0 %shard_map.87 = (bf16[2048,128]{1,0:T(8,128)(2,1)S(1)}, bf16[2048,128]{1,0:T(8,128)(2,1)S(1)}, bf16[2048,512]{1,0:T(8,128)(2,1)}, bf16[128,2048]{1,0:T(8,128)(2,1)S(1)}, f32[8,2048]{1,0:T(8,128)S(1)}) custom-call(bf16[2048,512]{1,0:T(8,128)(2,1)} %refs_0_.3, ...), custom_call_target="tpu_custom_call", output_to_operand_aliasing={{0}: (5, {}), {1}: (6, {}), {2}: (7, {}), {3}: (8, {}), {4}... | custom-call | flops 3630000128 | tf_op jit(solution)/shard_map/pallas_call | solution.py:537
  19.7 2.1 %all-to-all-done.counts_ref = s32[16,1,128]{2,1,0:T(1,128)S(1)} async-done(((s32[16,1,128]{2,1,0:T(1,128)}), s32[16,1,128]{2,1,0:T(1,128)S(1)}, u32[]{:S(2)}, u32[]{:S(2)}) %all-to-all-start) | async-done | bytes 8224 | tf_op jit(solution)/shard_map/all_to_all | solution.py:596
  21.8 8.2 %shard_map.88.rest_3_.a_ref = bf16[2048,128]{1,0:T(8,128)(2,1)S(1)} custom-call(s32[16,1,128]{2,1,0:T(1,128)S(1)} %all-to-all-done.counts_ref, bf16[2048,128]{1,0:T(8,128)(2,1)S(1)} %get-tuple-element.40.rest_0_.rest_1_.one_ref, bf16[2048,128]{1,0:T(8,128)(2,1)S(1)} %get-tuple-element.40.rest_0_.rest_1_.one_ref), custom_call_target="tpu_custom_call" | custom-call | flops 8249999872 | tf_op jit(solution)/shard_map/pallas_call | solution.py:537
  30.0 0.0 collective-permute-done.rest_2_
  30.1 14.6 %shard_map.89 = (bf16[2048,256]{1,0:T(8,128)(2,1)S(1)}, bf16[1024,256]{1,0:T(8,128)(2,1)S(1)}) custom-call(s32[16,1,128]{2,1,0:T(1,128)S(1)} %all-to-all-done.counts_ref, bf16[2048,128]{1,0:T(8,128)(2,1)S(1)} %get-tuple-element.40.rest_0_.rest_1_.one_ref, bf16[2048,128]{1,0:T(8,128)(2,1)S(1)} %get-tuple-element.41.rest_1_.rest_0_.two_ref, ...), custom_call_target="tpu_custom_call" | custom-call | flops 16499999744 | tf_op jit(solution)/shard_map/pallas_call | solution.py:537
  44.6 3.1 %collective-permute-start.1 = (bf16[1024,256]{1,0:T(8,128)(2,1)S(1)}, bf16[1024,256]{1,0:T(8,128)(2,1)S(1)}, u32[]{:S(2)}, u32[]{:S(2)}) collective-permute-start(bf16[1024,256]{1,0:T(8,128)(2,1)S(1)} %get-tuple-element.44), channel_id=1, source_target_pairs={{0,8},{8,16},{16,24},{24,32},{32,40},{40,48},{48,56},{56,64},{64,7... | collective-permute-start | bytes 1572872 | tf_op jit(solution)/shard_map/ppermute | solution.py:766
  47.8 8.2 %shard_map.90.b_ref = bf16[2048,128]{1,0:T(8,128)(2,1)S(1)} custom-call(s32[16,1,128]{2,1,0:T(1,128)S(1)} %all-to-all-done.counts_ref, bf16[2048,128]{1,0:T(8,128)(2,1)S(1)} %get-tuple-element.41.rest_1_.rest_0_.two_ref, bf16[2048,256]{1,0:T(8,128)(2,1)S(1)} %get-tuple-element.43.rest_1_.mine_ref), custom_call_target="tpu_custom_call" | custom-call | flops 8249999872 | tf_op jit(solution)/shard_map/pallas_call | solution.py:537
  56.0 1.6 %shard_map.91 = (bf16[272,2048]{1,0:T(8,128)(2,1)S(1)}, bf16[272,2048]{1,0:T(8,128)(2,1)S(1)}, bf16[2048,256]{1,0:T(8,128)(2,1)S(1)}) custom-call(bf16[2048,256]{1,0:T(8,128)(2,1)S(1)} %get-tuple-element.43.rest_1_.mine_ref, bf16[2048,128]{1,0:T(8,128)(2,1)S(1)} %shard_map.88.rest_3_.a_ref, bf16[2048,128]{1,0:T(8,128)(2,1)S(1)} %shard_map.90.b_ref, ...), custom_call_target="tpu_custom_call" | custom-call | flops 2200000000 | tf_op jit(solution)/shard_map/pallas_call | solution.py:537
  57.7 2.0 %collective-permute-done.1.rest_0_ = bf16[1024,256]{1,0:T(8,128)(2,1)S(1)} collective-permute-done((bf16[1024,256]{1,0:T(8,128)(2,1)S(1)}, bf16[1024,256]{1,0:T(8,128)(2,1)S(1)}, u32[]{:S(2)}, u32[]{:S(2)}) %collective-permute-start.1) | collective-permute-done | bytes 524320 | tf_op jit(solution)/shard_map/ppermute | solution.py:766
  59.7 0.0 copy-start
  59.7 0.0 copy-start.3
  59.7 1.7 %shard_map.92 = (bf16[272,2048]{1,0:T(8,128)(2,1)S(1)}, bf16[272,2048]{1,0:T(8,128)(2,1)S(1)}, bf16[2048,256]{1,0:T(8,128)(2,1)S(1)}) custom-call(bf16[2048,256]{1,0:T(8,128)(2,1)S(1)} %get-tuple-element.43.rest_1_.mine_ref, bf16[2048,128]{1,0:T(8,128)(2,1)S(1)} %shard_map.88.rest_3_.a_ref, ...), custom_call_target="tpu_custom_call", output_to_operand_aliasing={{0}: (8, {}), {1}: (9, {}), {2}: (10, {})} | custom-call | flops 2200000000 | tf_op jit(solution)/shard_map/pallas_call | solution.py:537
  61.4 0.6 collective-permute-start.2
  62.0 0.0 copy-done
  62.0 0.0 copy-done.3
  62.0 2.1 %shard_map.93.after_ref = bf16[512,256]{1,0:T(8,128)(2,1)S(1)} custom-call(bf16[2048,256]{1,0:T(8,128)(2,1)S(1)} %get-tuple-element.50.total_ref, bf16[2048,512]{1,0:T(8,128)(2,1)S(1)} %copy-done.3, bf16[2048,512]{1,0:T(8,128)(2,1)S(1)} %copy-done, bf16[272,2048]{1,0:T(8,128)(2,1)S(1)} %get-tuple-element.48.after_ref.keep_ref), custom_call_target="tpu_custom_call" | custom-call | flops 4400000000 | tf_op jit(solution)/shard_map/pallas_call | solution.py:537
  64.1 0.0 copy-start.1
  64.1 0.3 collective-permute-done.2.got_ref
  64.4 0.3 shard_map.94
  64.7 4.4 %collective-permute-start.3 = (bf16[64,2176]{1,0:T(8,128)(2,1)S(1)}, bf16[64,2176]{1,0:T(8,128)(2,1)S(1)}, u32[]{:S(2)}, u32[]{:S(2)}) collective-permute-start(bf16[64,2176]{1,0:T(8,128)(2,1)S(1)} %get-tuple-element.53), channel_id=1, source_target_pairs={{0,2},{1,3},{2,4},{3,5},{4,6},{5,7},{6,0},{7,1},{8,10},{9,11},{10,... | collective-permute-start | bytes 835592 | tf_op jit(solution)/shard_map/ppermute | solution.py:779
  69.1 2.7 %collective-permute-start.4 = (bf16[64,2176]{1,0:T(8,128)(2,1)S(1)}, bf16[64,2176]{1,0:T(8,128)(2,1)S(1)}, u32[]{:S(2)}, u32[]{:S(2)}) collective-permute-start(bf16[64,2176]{1,0:T(8,128)(2,1)S(1)} %get-tuple-element.54), channel_id=1, source_target_pairs={{0,4},{1,5},{2,6},{3,7},{4,0},{5,1},{6,2},{7,3},{8,12},{9,13},{10,... | collective-permute-start | bytes 835592 | tf_op jit(solution)/shard_map/ppermute | solution.py:779
  71.8 1.4 %collective-permute-start.5 = (bf16[64,2176]{1,0:T(8,128)(2,1)S(1)}, bf16[64,2176]{1,0:T(8,128)(2,1)S(1)}, u32[]{:S(2)}, u32[]{:S(2)}) collective-permute-start(bf16[64,2176]{1,0:T(8,128)(2,1)S(1)} %get-tuple-element.55), channel_id=1, source_target_pairs={{0,6},{1,7},{2,0},{3,1},{4,2},{5,3},{6,4},{7,5},{8,14},{9,15},{10,... | collective-permute-start | bytes 835592 | tf_op jit(solution)/shard_map/ppermute | solution.py:779
  73.3 15.6 %all_to_all.10.grads_ref = bf16[16,32,256]{2,1,0:T(8,128)(2,1)S(1)} all-to-all(bf16[16,32,256]{2,1,0:T(8,128)(2,1)S(1)} %bitcast.6), channel_id=1, replica_groups=mesh['space'=16,'mp'=8] {'space'}, dimensions={0} | all-to-all | bytes 524288 | tf_op jit(solution)/shard_map/all_to_all | solution.py:772
  88.9 0.0 collective-permute-done.3.b_ref
  88.9 0.0 collective-permute-done.4.c_ref
  88.9 0.0 collective-permute-done.5.d_ref
  88.9 0.0 copy-done.1
  88.9 1.8 %shard_map.95 = (bf16[64,2048]{1,0:T(8,128)(2,1)}, f32[32,192]{1,0:T(8,128)}, f32[32,64]{1,0:T(8,128)}) custom-call(s32[16,1,128]{2,1,0:T(1,128)S(1)} %all-to-all-done.counts_ref, bf16[64,2176]{1,0:T(8,128)(2,1)S(1)} %get-tuple-element.52.a_ref, bf16[64,2176]{1,0:T(8,128)(2,1)S(1)} %collective-permute-done.3.b_ref, ...), custom_call_target="tpu_custom_call" | custom-call | flops 2529999872 | tf_op jit(solution)/shard_map/pallas_call | solution.py:537
Async XLA Ops:
  0.6 4.9 %copy-start.2 = (s32[128]{0:T(128)S(1)}, s32[128]{0:T(128)}, u32[]{:S(2)}) copy-start(s32[128]{0:T(128)} %param.8) | copy-start | bytes 1540
  6.2 15.6 %all-to-all-start = ((s32[16,1,128]{2,1,0:T(1,128)}), s32[16,1,128]{2,1,0:T(1,128)S(1)}, u32[]{:S(2)}, u32[]{:S(2)}) async-start(s32[16,1,128]{2,1,0:T(1,128)} %shard_map.86), calls=%async_computation | async-start | bytes 16384 | tf_op jit(solution)/shard_map/all_to_all | solution.py:596
  14.4 15.7 %collective-permute-start = (bf16[1024,256]{1,0:T(8,128)(2,1)S(1)}, bf16[1024,256]{1,0:T(8,128)(2,1)S(1)}, u32[]{:S(2)}, u32[]{:S(2)}) collective-permute-start(bf16[1024,256]{1,0:T(8,128)(2,1)S(1)} %get-tuple-element.42), channel_id=1, source_target_pairs={{8,0},{16,8},{24,16},{32,24},{40,32},{48,40},{56,48},{64,56},{72,6... | collective-permute-start | bytes 1572872 | tf_op jit(solution)/shard_map/ppermute | solution.py:763
  44.6 15.1 %collective-permute-start.1 = (bf16[1024,256]{1,0:T(8,128)(2,1)S(1)}, bf16[1024,256]{1,0:T(8,128)(2,1)S(1)}, u32[]{:S(2)}, u32[]{:S(2)}) collective-permute-start(bf16[1024,256]{1,0:T(8,128)(2,1)S(1)} %get-tuple-element.44), channel_id=1, source_target_pairs={{0,8},{8,16},{16,24},{24,32},{32,40},{40,48},{48,56},{56,64},{64,7... | collective-permute-start | bytes 1572872 | tf_op jit(solution)/shard_map/ppermute | solution.py:766
  59.7 2.3 %copy-start = (bf16[2048,512]{1,0:T(8,128)(2,1)S(1)}, bf16[2048,512]{1,0:T(8,128)(2,1)}, u32[]{:S(2)}) copy-start(bf16[2048,512]{1,0:T(8,128)(2,1)} %dy_ref.1) | copy-start | bytes 6291460
  59.7 2.3 %copy-start.3 = (bf16[2048,512]{1,0:T(8,128)(2,1)S(1)}, bf16[2048,512]{1,0:T(8,128)(2,1)}, u32[]{:S(2)}) copy-start(bf16[2048,512]{1,0:T(8,128)(2,1)} %get-tuple-element.51.unit_ref) | copy-start | bytes 6291460
  61.4 3.0 %collective-permute-start.2 = (bf16[272,2048]{1,0:T(8,128)(2,1)S(1)}, bf16[272,2048]{1,0:T(8,128)(2,1)S(1)}, u32[]{:S(2)}, u32[]{:S(2)}) collective-permute-start(bf16[272,2048]{1,0:T(8,128)(2,1)S(1)} %get-tuple-element.49), channel_id=1, source_target_pairs={{0,1},{1,0},{2,3},{3,2},{4,5},{5,4},{6,7},{7,6},{8,9},{9,8},{10,11... | collective-permute-start | bytes 3342344 | tf_op jit(solution)/shard_map/ppermute | solution.py:770
  64.1 24.8 %copy-start.1 = (f32[512]{0:T(512)S(1)}, f32[512]{0:T(512)}, u32[]{:S(2)}) copy-start(f32[512]{0:T(512)} %param.9) | copy-start | bytes 6148
  64.7 24.1 %collective-permute-start.3 = (bf16[64,2176]{1,0:T(8,128)(2,1)S(1)}, bf16[64,2176]{1,0:T(8,128)(2,1)S(1)}, u32[]{:S(2)}, u32[]{:S(2)}) collective-permute-start(bf16[64,2176]{1,0:T(8,128)(2,1)S(1)} %get-tuple-element.53), channel_id=1, source_target_pairs={{0,2},{1,3},{2,4},{3,5},{4,6},{5,7},{6,0},{7,1},{8,10},{9,11},{10,... | collective-permute-start | bytes 835592 | tf_op jit(solution)/shard_map/ppermute | solution.py:779
  69.1 19.8 %collective-permute-start.4 = (bf16[64,2176]{1,0:T(8,128)(2,1)S(1)}, bf16[64,2176]{1,0:T(8,128)(2,1)S(1)}, u32[]{:S(2)}, u32[]{:S(2)}) collective-permute-start(bf16[64,2176]{1,0:T(8,128)(2,1)S(1)} %get-tuple-element.54), channel_id=1, source_target_pairs={{0,4},{1,5},{2,6},{3,7},{4,0},{5,1},{6,2},{7,3},{8,12},{9,13},{10,... | collective-permute-start | bytes 835592 | tf_op jit(solution)/shard_map/ppermute | solution.py:779
  71.8 17.0 %collective-permute-start.5 = (bf16[64,2176]{1,0:T(8,128)(2,1)S(1)}, bf16[64,2176]{1,0:T(8,128)(2,1)S(1)}, u32[]{:S(2)}, u32[]{:S(2)}) collective-permute-start(bf16[64,2176]{1,0:T(8,128)(2,1)S(1)} %get-tuple-element.55), channel_id=1, source_target_pairs={{0,6},{1,7},{2,0},{3,1},{4,2},{5,3},{6,4},{7,5},{8,14},{9,15},{10,... | collective-permute-start | bytes 835592 | tf_op jit(solution)/shard_map/ppermute | solution.py:779

commit v7 on v5

--- a/solution.py
+++ b/solution.py
@@ -681,7 +681,7 @@
 def products(mine, locals_, got, heads, wide, wg):
     slots = mine.shape[0]
     width = wide.shape[0]
-    rows = 256
+    rows = 512
     half = width // 2 + 16
     outs = [shape((half, slots), BF), shape((half, slots), BF), shape((slots, LANES), BF)]
     steps = PATCH // rows
@@ -710,7 +710,7 @@
 
 def weights(total, unit, dy, after):
     slots, width = unit.shape
-    rows = 512
+    rows = 1024
     down = lambda i: (i, 0)
     return call(
         weight_kernel,

time: 92.2 us -> 91.7 us (level); the launches traced: 91.3 us -> 92 us
  blocking collectives: 16.3 us -> 17.9 us
  Pallas kernels: 47.4 us -> 46.1 us
    all_to_all x1, blocking collectives: 16.3 us -> 17.9 us  [on_device(): lax.all_to_all(grads.reshape(n_space, width // n_space, LANES), 'space',...]
    pallas_call x10, Pallas kernels: 47.4 us -> 46.1 us  [call(): pl.pallas_call(kernel, grid=grid, in_specs=in_specs, out_specs=out_specs,...]
  transfers between devices with their start and end apart: 7 -> 7, of which waited for: 4 -> 4; matrix products, arithmetic and copies ran while one was open for 0% -> 0% of each run, Pallas kernels for 31% -> 30%
where the time goes in v7:
time: 91.7 us; the launch traced here: 92 us
  Pallas kernels  46.1 us (50%)
  starting transfers between devices  21.9 us (24%)
  blocking collectives  17.9 us (20%)
  waiting for transfers between devices  4.65 us (5%)
    pallas_call x10, Pallas kernels, call(): pl.pallas_call(kernel, grid=grid, in_specs=in_specs, out_specs=out_specs,...  46.1 us
    all_to_all x1, blocking collectives, on_device(): lax.all_to_all(grads.reshape(n_space, width // n_space, LANES), 'space',...  17.9 us
    all_to_all x1, starting transfers between devices, on_device(): counts = lax.all_to_all(count(cell_counts, n_space), 'space', 0, 0)  8.13 us
    ppermute x3, starting transfers between devices, on_device(): received.append(lax.ppermute(parts[d], 'mp', route))  7.11 us
    ppermute x1, starting transfers between devices, on_device(): got = lax.ppermute(spill, 'space', onward)  3.58 us
  transfers between devices with their start and end apart: 7, of which 4 were waited for; matrix products, arithmetic and copies ran while one was open for 0% of the time, Pallas kernels for 30%

profile of v7, /device:TPU:0, one launch (start us, length us, event | category | flops | bytes accessed | tf_op | source)
XLA Modules:
  0.0 92.0 jit_solution(8615970160156645730)
XLA Ops:
  0.6 0.0 copy-start.2
  0.6 0.6 copy-done.2
  1.3 0.7 shard_map.85
  2.0 8.1 %all-to-all-start = ((s32[16,1,128]{2,1,0:T(1,128)}), s32[16,1,128]{2,1,0:T(1,128)S(1)}, u32[]{:S(2)}, u32[]{:S(2)}) async-start(s32[16,1,128]{2,1,0:T(1,128)} %shard_map.85), calls=%async_computation | async-start | bytes 16384 | tf_op jit(solution)/shard_map/all_to_all | solution.py:776
  10.1 4.9 %shard_map.86 = (bf16[2048,128]{1,0:T(8,128)(2,1)S(1)}, bf16[2048,128]{1,0:T(8,128)(2,1)S(1)}, bf16[2048,512]{1,0:T(8,128)(2,1)}, bf16[128,2048]{1,0:T(8,128)(2,...) custom-call(bf16[2048,512]{1,0:T(8,128)(2,1)} %x_hbm.1, ...), custom_call_target="tpu_custom_call" | custom-call | flops 4950000128 | tf_op jit(solution)/shard_map/pallas_call | solution.py:553
  15.0 1.3 %collective-permute-start = (bf16[1024,256]{1,0:T(8,128)(2,1)S(1)}, bf16[1024,256]{1,0:T(8,128)(2,1)S(1)}, u32[]{:S(2)}, u32[]{:S(2)}) collective-permute-start(bf16[1024,256]{1,0:T(8,128)(2,1)S(1)} %get-tuple-element.35.head_hbm), channel_id=1, source_target_pairs={{8,0},{16,8},{24,16},{32,24},{40,32},{48,40},{56,48},{64,56},{72,6... | collective-permute-start | bytes 1572872 | tf_op jit(solution)/shard_map/ppermute | solution.py:783
  16.3 1.3 %all-to-all-done.counts_ref = s32[16,1,128]{2,1,0:T(1,128)S(1)} async-done(((s32[16,1,128]{2,1,0:T(1,128)}), s32[16,1,128]{2,1,0:T(1,128)S(1)}, u32[]{:S(2)}, u32[]{:S(2)}) %all-to-all-start) | async-done | bytes 8224 | tf_op jit(solution)/shard_map/all_to_all | solution.py:776
  17.6 11.6 %shard_map.87 = (bf16[2048,128]{1,0:T(8,128)(2,1)S(1)}, bf16[2048,128]{1,0:T(8,128)(2,1)S(1)}, bf16[2048,512]{1,0:T(8,128)(2,1)}, bf16[128,2048]{1,0:T(8,128)(2,...) custom-call(s32[16,1,128]{2,1,0:T(1,128)S(1)} %all-to-all-done.count, ...), custom_call_target="tpu_custom_call", output_to_operand_aliasing={{0}: (7, {}), {1}: (8, {}), {2}: (9, {}), {3}: (10, {}), {4... | custom-call | flops 12099999744 | tf_op jit(solution)/shard_map/pallas_call | solution.py:553
  29.2 1.1 %collective-permute-done.rest_2_ = bf16[1024,256]{1,0:T(8,128)(2,1)S(1)} collective-permute-done((bf16[1024,256]{1,0:T(8,128)(2,1)S(1)}, bf16[1024,256]{1,0:T(8,128)(2,1)S(1)}, u32[]{:S(2)}, u32[]{:S(2)}) %collective-permute-start) | collective-permute-done | bytes 524320 | tf_op jit(solution)/shard_map/ppermute | solution.py:783
  30.3 14.5 %shard_map.88 = (bf16[2048,256]{1,0:T(8,128)(2,1)S(1)}, bf16[1024,256]{1,0:T(8,128)(2,1)S(1)}) custom-call(s32[16,1,128]{2,1,0:T(1,128)S(1)} %all-to-all-done.counts_ref, bf16[2048,128]{1,0:T(8,128)(2,1)S(1)} %get-tuple-element.41.rest_0_.rest_3_.one_ref, bf16[2048,128]{1,0:T(8,128)(2,1)S(1)} %get-tuple-element.42.rest_1_.rest_0_.two_ref, ...), custom_call_target="tpu_custom_call" | custom-call | flops 16499999744 | tf_op jit(solution)/shard_map/pallas_call | solution.py:553
  44.8 3.6 %collective-permute-start.1 = (bf16[1024,256]{1,0:T(8,128)(2,1)S(1)}, bf16[1024,256]{1,0:T(8,128)(2,1)S(1)}, u32[]{:S(2)}, u32[]{:S(2)}) collective-permute-start(bf16[1024,256]{1,0:T(8,128)(2,1)S(1)} %get-tuple-element.46), channel_id=1, source_target_pairs={{0,8},{8,16},{16,24},{24,32},{32,40},{40,48},{48,56},{56,64},{64,7... | collective-permute-start | bytes 1572872 | tf_op jit(solution)/shard_map/ppermute | solution.py:785
  48.4 8.2 %shard_map.89.b_ref = bf16[2048,128]{1,0:T(8,128)(2,1)S(1)} custom-call(s32[16,1,128]{2,1,0:T(1,128)S(1)} %all-to-all-done.counts_ref, bf16[2048,128]{1,0:T(8,128)(2,1)S(1)} %get-tuple-element.42.rest_1_.rest_0_.two_ref, bf16[2048,256]{1,0:T(8,128)(2,1)S(1)} %get-tuple-element.43.rest_1_.mine_ref), custom_call_target="tpu_custom_call" | custom-call | flops 8249999872 | tf_op jit(solution)/shard_map/pallas_call | solution.py:553
  56.7 1.2 %shard_map.90 = (bf16[272,2048]{1,0:T(8,128)(2,1)S(1)}, bf16[272,2048]{1,0:T(8,128)(2,1)S(1)}, bf16[2048,256]{1,0:T(8,128)(2,1)S(1)}) custom-call(bf16[2048,256]{1,0:T(8,128)(2,1)S(1)} %get-tuple-element.43.rest_1_.mine_ref, bf16[2048,128]{1,0:T(8,128)(2,1)S(1)} %get-tuple-element.44.a_ref, bf16[2048,128]{1,0:T(8,128)(2,1)S(1)} %shard_map.89.b_ref, ...), custom_call_target="tpu_custom_call" | custom-call | flops 2200000000 | tf_op jit(solution)/shard_map/pallas_call | solution.py:553
  57.9 1.6 %collective-permute-done.1.rest_0_ = bf16[1024,256]{1,0:T(8,128)(2,1)S(1)} collective-permute-done((bf16[1024,256]{1,0:T(8,128)(2,1)S(1)}, bf16[1024,256]{1,0:T(8,128)(2,1)S(1)}, u32[]{:S(2)}, u32[]{:S(2)}) %collective-permute-start.1) | collective-permute-done | bytes 524320 | tf_op jit(solution)/shard_map/ppermute | solution.py:785
  59.5 0.0 copy-start
  59.5 0.0 copy-start.3
  59.5 1.2 %shard_map.91 = (bf16[272,2048]{1,0:T(8,128)(2,1)S(1)}, bf16[272,2048]{1,0:T(8,128)(2,1)S(1)}, bf16[2048,256]{1,0:T(8,128)(2,1)S(1)}) custom-call(bf16[2048,256]{1,0:T(8,128)(2,1)S(1)} %get-tuple-element.43.rest_1_.mine_ref, bf16[2048,128]{1,0:T(8,128)(2,1)S(1)} %get-tuple-element.44.a_ref, ...), custom_call_target="tpu_custom_call", output_to_operand_aliasing={{0}: (8, {}), {1}: (9, {}), {2}: (10, {})} | custom-call | flops 2200000000 | tf_op jit(solution)/shard_map/pallas_call | solution.py:553
  60.7 1.8 %collective-permute-start.2 = (bf16[272,2048]{1,0:T(8,128)(2,1)S(1)}, bf16[272,2048]{1,0:T(8,128)(2,1)S(1)}, u32[]{:S(2)}, u32[]{:S(2)}) collective-permute-start(bf16[272,2048]{1,0:T(8,128)(2,1)S(1)} %get-tuple-element.51), channel_id=1, source_target_pairs={{0,1},{1,0},{2,3},{3,2},{4,5},{5,4},{6,7},{7,6},{8,9},{9,8},{10,11... | collective-permute-start | bytes 3342344 | tf_op jit(solution)/shard_map/ppermute | solution.py:789
  62.5 0.0 copy-done
  62.5 0.0 copy-done.3
  62.5 1.7 %shard_map.92.after_ref = bf16[512,256]{1,0:T(8,128)(2,1)S(1)} custom-call(bf16[2048,256]{1,0:T(8,128)(2,1)S(1)} %get-tuple-element.52.total_ref, bf16[2048,512]{1,0:T(8,128)(2,1)S(1)} %copy-done.3, bf16[2048,512]{1,0:T(8,128)(2,1)S(1)} %copy-done, bf16[272,2048]{1,0:T(8,128)(2,1)S(1)} %get-tuple-element.50.after_ref.keep_ref), custom_call_target="tpu_custom_call" | custom-call | flops 4400000000 | tf_op jit(solution)/shard_map/pallas_call | solution.py:553
  64.2 0.0 copy-start.1
  64.2 0.7 collective-permute-done.2.got_ref
  64.9 0.3 shard_map.93
  65.2 3.0 %collective-permute-start.3 = (bf16[64,2176]{1,0:T(8,128)(2,1)S(1)}, bf16[64,2176]{1,0:T(8,128)(2,1)S(1)}, u32[]{:S(2)}, u32[]{:S(2)}) collective-permute-start(bf16[64,2176]{1,0:T(8,128)(2,1)S(1)} %get-tuple-element.55), channel_id=1, source_target_pairs={{0,2},{1,3},{2,4},{3,5},{4,6},{5,7},{6,0},{7,1},{8,10},{9,11},{10,... | collective-permute-start | bytes 835592 | tf_op jit(solution)/shard_map/ppermute | solution.py:798
  68.1 2.7 %collective-permute-start.4 = (bf16[64,2176]{1,0:T(8,128)(2,1)S(1)}, bf16[64,2176]{1,0:T(8,128)(2,1)S(1)}, u32[]{:S(2)}, u32[]{:S(2)}) collective-permute-start(bf16[64,2176]{1,0:T(8,128)(2,1)S(1)} %get-tuple-element.56), channel_id=1, source_target_pairs={{0,4},{1,5},{2,6},{3,7},{4,0},{5,1},{6,2},{7,3},{8,12},{9,13},{10,... | collective-permute-start | bytes 835592 | tf_op jit(solution)/shard_map/ppermute | solution.py:798
  70.9 1.4 %collective-permute-start.5 = (bf16[64,2176]{1,0:T(8,128)(2,1)S(1)}, bf16[64,2176]{1,0:T(8,128)(2,1)S(1)}, u32[]{:S(2)}, u32[]{:S(2)}) collective-permute-start(bf16[64,2176]{1,0:T(8,128)(2,1)S(1)} %get-tuple-element.57), channel_id=1, source_target_pairs={{0,6},{1,7},{2,0},{3,1},{4,2},{5,3},{6,4},{7,5},{8,14},{9,15},{10,... | collective-permute-start | bytes 835592 | tf_op jit(solution)/shard_map/ppermute | solution.py:798
  72.3 17.9 %all_to_all.10.grads_ref = bf16[16,32,256]{2,1,0:T(8,128)(2,1)S(1)} all-to-all(bf16[16,32,256]{2,1,0:T(8,128)(2,1)S(1)} %bitcast.6), channel_id=1, replica_groups=mesh['space'=16,'mp'=8] {'space'}, dimensions={0} | all-to-all | bytes 524288 | tf_op jit(solution)/shard_map/all_to_all | solution.py:791
  90.2 0.0 collective-permute-done.3.b_ref
  90.2 0.0 collective-permute-done.4.c_ref
  90.2 0.0 collective-permute-done.5.d_ref
  90.2 0.0 copy-done.1
  90.2 1.8 %shard_map.94 = (bf16[64,2048]{1,0:T(8,128)(2,1)}, f32[32,192]{1,0:T(8,128)}, f32[32,64]{1,0:T(8,128)}) custom-call(s32[16,1,128]{2,1,0:T(1,128)S(1)} %all-to-all-done.counts_ref, bf16[64,2176]{1,0:T(8,128)(2,1)S(1)} %get-tuple-element.54.a_ref, bf16[64,2176]{1,0:T(8,128)(2,1)S(1)} %collective-permute-done.3.b_ref, ...), custom_call_target="tpu_custom_call" | custom-call | flops 2529999872 | tf_op jit(solution)/shard_map/pallas_call | solution.py:553
Async XLA Ops:
  0.6 0.7 copy-start.2
  2.0 15.6 %all-to-all-start = ((s32[16,1,128]{2,1,0:T(1,128)}), s32[16,1,128]{2,1,0:T(1,128)S(1)}, u32[]{:S(2)}, u32[]{:S(2)}) async-start(s32[16,1,128]{2,1,0:T(1,128)} %shard_map.85), calls=%async_computation | async-start | bytes 16384 | tf_op jit(solution)/shard_map/all_to_all | solution.py:776
  15.0 15.3 %collective-permute-start = (bf16[1024,256]{1,0:T(8,128)(2,1)S(1)}, bf16[1024,256]{1,0:T(8,128)(2,1)S(1)}, u32[]{:S(2)}, u32[]{:S(2)}) collective-permute-start(bf16[1024,256]{1,0:T(8,128)(2,1)S(1)} %get-tuple-element.35.head_hbm), channel_id=1, source_target_pairs={{8,0},{16,8},{24,16},{32,24},{40,32},{48,40},{56,48},{64,56},{72,6... | collective-permute-start | bytes 1572872 | tf_op jit(solution)/shard_map/ppermute | solution.py:783
  44.8 14.6 %collective-permute-start.1 = (bf16[1024,256]{1,0:T(8,128)(2,1)S(1)}, bf16[1024,256]{1,0:T(8,128)(2,1)S(1)}, u32[]{:S(2)}, u32[]{:S(2)}) collective-permute-start(bf16[1024,256]{1,0:T(8,128)(2,1)S(1)} %get-tuple-element.46), channel_id=1, source_target_pairs={{0,8},{8,16},{16,24},{24,32},{32,40},{40,48},{48,56},{56,64},{64,7... | collective-permute-start | bytes 1572872 | tf_op jit(solution)/shard_map/ppermute | solution.py:785
  59.5 3.0 %copy-start = (bf16[2048,512]{1,0:T(8,128)(2,1)S(1)}, bf16[2048,512]{1,0:T(8,128)(2,1)}, u32[]{:S(2)}) copy-start(bf16[2048,512]{1,0:T(8,128)(2,1)} %dy_ref.1) | copy-start | bytes 6291460
  59.5 3.0 %copy-start.3 = (bf16[2048,512]{1,0:T(8,128)(2,1)S(1)}, bf16[2048,512]{1,0:T(8,128)(2,1)}, u32[]{:S(2)}) copy-start(bf16[2048,512]{1,0:T(8,128)(2,1)} %get-tuple-element.53.unit_ref) | copy-start | bytes 6291460
  60.7 4.2 %collective-permute-start.2 = (bf16[272,2048]{1,0:T(8,128)(2,1)S(1)}, bf16[272,2048]{1,0:T(8,128)(2,1)S(1)}, u32[]{:S(2)}, u32[]{:S(2)}) collective-permute-start(bf16[272,2048]{1,0:T(8,128)(2,1)S(1)} %get-tuple-element.51), channel_id=1, source_target_pairs={{0,1},{1,0},{2,3},{3,2},{4,5},{5,4},{6,7},{7,6},{8,9},{9,8},{10,11... | collective-permute-start | bytes 3342344 | tf_op jit(solution)/shard_map/ppermute | solution.py:789
  64.2 26.0 %copy-start.1 = (f32[512]{0:T(512)S(1)}, f32[512]{0:T(512)}, u32[]{:S(2)}) copy-start(f32[512]{0:T(512)} %param.9) | copy-start | bytes 6148
  65.2 25.0 %collective-permute-start.3 = (bf16[64,2176]{1,0:T(8,128)(2,1)S(1)}, bf16[64,2176]{1,0:T(8,128)(2,1)S(1)}, u32[]{:S(2)}, u32[]{:S(2)}) collective-permute-start(bf16[64,2176]{1,0:T(8,128)(2,1)S(1)} %get-tuple-element.55), channel_id=1, source_target_pairs={{0,2},{1,3},{2,4},{3,5},{4,6},{5,7},{6,0},{7,1},{8,10},{9,11},{10,... | collective-permute-start | bytes 835592 | tf_op jit(solution)/shard_map/ppermute | solution.py:798
  68.1 22.1 %collective-permute-start.4 = (bf16[64,2176]{1,0:T(8,128)(2,1)S(1)}, bf16[64,2176]{1,0:T(8,128)(2,1)S(1)}, u32[]{:S(2)}, u32[]{:S(2)}) collective-permute-start(bf16[64,2176]{1,0:T(8,128)(2,1)S(1)} %get-tuple-element.56), channel_id=1, source_target_pairs={{0,4},{1,5},{2,6},{3,7},{4,0},{5,1},{6,2},{7,3},{8,12},{9,13},{10,... | collective-permute-start | bytes 835592 | tf_op jit(solution)/shard_map/ppermute | solution.py:798
  70.9 19.3 %collective-permute-start.5 = (bf16[64,2176]{1,0:T(8,128)(2,1)S(1)}, bf16[64,2176]{1,0:T(8,128)(2,1)S(1)}, u32[]{:S(2)}, u32[]{:S(2)}) collective-permute-start(bf16[64,2176]{1,0:T(8,128)(2,1)S(1)} %get-tuple-element.57), channel_id=1, source_target_pairs={{0,6},{1,7},{2,0},{3,1},{4,2},{5,3},{6,4},{7,5},{8,14},{9,15},{10,... | collective-permute-start | bytes 835592 | tf_op jit(solution)/shard_map/ppermute | solution.py:798
